TPU v7x, 256 devices: a whole 4x4x8 slice. The times are simulated.
256 devices in a mesh: depth: 8 (over z_lo, core), row: 4 (over y), col: 8 (over x, z_hi).
Axes of the slice: x: 4, y: 4, z: 8 (z_hi: 2, z_lo: 4; z = z_hi * 4 + z_lo), core: 2. Of those that a mesh axis runs over, the one named last changes fastest.
Arguments:
- x_code: bfloat16 [512, 9216], P(('depth', 'col'), 'row'), may hold values from -4 to 4
- x_scale: float32 [512, 72], P(('depth', 'col'), 'row'), may hold values from 0.3 to 3
- g_code: bfloat16 [512, 9216], P(('depth', 'col'), 'row'), may hold values from -4 to 4
- g_scale: float32 [512, 72], P(('depth', 'col'), 'row'), may hold values from 0.3 to 3
- up_weight: bfloat16 [36864, 9216], P(('depth', 'col'), 'row'), may hold values from -0.0625 to 0.0625
- down_weight: bfloat16 [36864, 9216], P(('depth', 'col'), 'row'), may hold values from -0.03125 to 0.03125
Outputs:
- grad_input: bfloat16 [512, 9216], P(('depth', 'col'), 'row')
- grad_up: bfloat16 [36864, 9216], P(('depth', 'col'), 'row')
- grad_down: bfloat16 [36864, 9216], P(('depth', 'col'), 'row')
All inputs are finite; a program needn't handle non-finite values.
Results may differ from a plain program's by a relative error of at most 0.017.
Values may be sent and summed in bfloat16 or wider, within the bound.
No kernel may reach another device: no remote copies, remote signals or barrier semaphores. Data moves between devices by JAX's collectives and lax.ppermute only.
A program may use at most 64 MiB of HBM per device.

v0:
```python
import math

import jax
import jax.numpy as jnp
from jax import lax
from jax.sharding import PartitionSpec as P


def hadamard():
    indices = jnp.arange(128, dtype=jnp.int32)
    common_bits = jnp.bitwise_and(indices[:, None], indices[None, :])
    parity = jnp.zeros((128, 128), jnp.int32)
    for shift_count in range(7):
        parity = parity + jnp.bitwise_and(jnp.right_shift(common_bits, shift_count), 1)
    sign_table = 1 - 2 * jnp.bitwise_and(parity, 1)
    return sign_table.astype(jnp.float32) / math.sqrt(128.0)


def dequant(codes, scales):
    row_count = codes.shape[0]
    col_count = codes.shape[1]
    tiles = codes.astype(jnp.float32).reshape(row_count, col_count // 128, 128) * scales[:, :, None]
    turned = jnp.einsum("rki,ij->rkj", tiles, hadamard(), precision=lax.Precision.HIGHEST)
    return turned.reshape(row_count, col_count).astype(jnp.bfloat16)


def activate(preact, grad_act):
    positive = jnp.maximum(preact, jnp.float32(0.0))
    squared = (positive * positive).astype(jnp.bfloat16)
    grad_pre = (2.0 * grad_act * positive).astype(jnp.bfloat16)
    return (squared, grad_pre)


def shards(x_code, x_scale, g_code, g_scale, up_weight, down_weight):
    local_inputs = dequant(x_code, x_scale)
    inputs = lax.all_gather(local_inputs, ("depth", "col"), axis=0, tiled=True)
    local_grads = dequant(g_code, g_scale)
    grads = lax.all_gather(local_grads, ("depth", "col"), axis=0, tiled=True)
    pre_part = jnp.dot(inputs, up_weight.T, preferred_element_type=jnp.float32)
    act_part = jnp.dot(grads, down_weight.T, preferred_element_type=jnp.float32)
    preact, grad_act = lax.psum((pre_part, act_part), "row")
    squared, grad_pre = activate(preact, grad_act)
    grad_down = jnp.dot(squared.T, grads, preferred_element_type=jnp.float32).astype(jnp.bfloat16)
    grad_up = jnp.dot(grad_pre.T, inputs, preferred_element_type=jnp.float32).astype(jnp.bfloat16)
    summed = lax.psum_scatter(
        jnp.dot(grad_pre, up_weight, preferred_element_type=jnp.float32),
        ("depth", "col"),
        scatter_dimension=0,
        tiled=True,
    )
    return (summed.astype(jnp.bfloat16), grad_up, grad_down)


def solution(mesh):
    return jax.shard_map(
        shards,
        mesh=mesh,
        in_specs=(
            P(("depth", "col"), "row"),
            P(("depth", "col"), "row"),
            P(("depth", "col"), "row"),
            P(("depth", "col"), "row"),
            P(("depth", "col"), "row"),
            P(("depth", "col"), "row"),
        ),
        out_specs=(
            P(("depth", "col"), "row"),
            P(("depth", "col"), "row"),
            P(("depth", "col"), "row"),
        ),
        check_vma=False,
    )
```

profile of v0, /device:TPU:1, one launch (start us, length us, event | category | flops | bytes accessed | tf_op | source)
XLA Modules:
  0.0 881.5 jit_solution(2519622635687974712)
XLA Ops:
  7.2 0.0 copy-start
  7.2 0.0 all-gather.3.cloned.1.call-start
  7.2 0.9 bitcast_convert_fusion.1
  8.2 1.0 fusion
  9.1 0.6 copy.22
  9.7 0.0 all-gather.3.cloned.1.call-update
  9.8 0.0 all-gather.5.cloned.1.call-start
  9.8 0.8 bitcast_convert_fusion
  10.6 1.0 fusion.1
  11.6 0.6 copy.21
  12.2 0.0 all-gather.5.cloned.1.call-update
  12.2 0.0 all-reduce.3.cloned.1.call-start
  12.3 185.2 %all-gather.3.cloned.1.call-done = bf16[512,2304]{1,0:T(8,128)(2,1)} async-done(((bf16[8,2304]{1,0:T(8,128)(2,1)}), bf16[512,2304]{1,0:T(8,128)(2,1)}) %all-gather.3.cloned.1.call-update) | async-done | bytes 2359312 | tf_op jit(solution)/shard_map/all_gather | solution.py:38
  197.5 5.0 fusion.24
  202.5 184.9 %all-gather.5.cloned.1.call-done = bf16[512,2304]{1,0:T(8,128)(2,1)} async-done(((bf16[8,2304]{1,0:T(8,128)(2,1)}), bf16[512,2304]{1,0:T(8,128)(2,1)}) %all-gather.5.cloned.1.call-update) | async-done | bytes 2359312 | tf_op jit(solution)/shard_map/all_gather | solution.py:36
  387.4 0.0 copy-done
  387.4 4.2 fusion.25
  391.7 0.0 all-reduce.3.cloned.1.call-update
  391.7 0.0 reduce-scatter.2.cloned.1.call-start
  391.8 72.6 %all-reduce.3.cloned.1.call-done = (f32[512,576]{0,1:T(8,128)}, f32[512,576]{0,1:T(8,128)}) async-done(((f32[512,576]{0,1:T(8,128)}, f32[512,576]{0,1:T(8,128)}), (f32[512,576]{0,1:T(8,128)}, f32[512,576]{0,1:T(8,128)})) %all-reduce.3.cloned.1.call-update) | async-done | bytes 2359312 | tf_op jit(solution)/shard_map/psum | solution.py:41
  464.4 1.9 multiply_convert_fusion.1
  466.3 4.2 fusion.26
  470.5 0.0 reduce-scatter.2.cloned.1.call-update
  470.5 0.0 copy-start.1
  470.5 0.0 copy-start.2
  470.5 4.9 convolution_convert_fusion.1
  475.4 0.0 copy-done.1
  475.4 0.0 copy-done.2
  475.4 3.1 convolution_convert_fusion
  478.5 395.0 %reduce-scatter.2.cloned.1.call-done = f32[8,2304]{1,0:T(8,128)} async-done(((f32[512,2304]{1,0:T(8,128)}), f32[8,2304]{1,0:T(8,128)}) %reduce-scatter.2.cloned.1.call-update) | async-done | bytes 73744 | tf_op jit(solution)/shard_map/reduce_scatter | solution.py:45
  873.5 1.5 convert_element_type.41
Async XLA Ops:
  7.2 380.3 %copy-start = (bf16[576,2304]{1,0:T(8,128)(2,1)S(1)}, bf16[576,2304]{1,0:T(8,128)(2,1)}, u32[]{:S(2)}) copy-start(bf16[576,2304]{1,0:T(8,128)(2,1)} %param.10) | copy-start | bytes 7962628
  7.2 190.3 %all-gather.3.cloned.1.call-start = ((), (), s32[]{:S(2)}) async-start(), calls=%async_computation.1 | async-start | bytes 2396160 | tf_op jit(solution)/shard_map/all_gather | solution.py:38
  9.8 377.7 %all-gather.5.cloned.1.call-start = ((), (), s32[]{:S(2)}) async-start(), calls=%async_computation.2 | async-start | bytes 2396160 | tf_op jit(solution)/shard_map/all_gather | solution.py:36
  12.2 452.2 %all-reduce.3.cloned.1.call-start = ((), (), s32[]{:S(2)}) async-start(), calls=%async_computation.4 | async-start | bytes 4718592 | tf_op jit(solution)/shard_map/psum | solution.py:41
  391.7 481.8 %reduce-scatter.2.cloned.1.call-start = ((), (), s32[]{:S(2)}) async-start(), calls=%async_computation.3 | async-start | bytes 4792320 | tf_op jit(solution)/shard_map/reduce_scatter | solution.py:45
  470.5 4.9 copy-start.1
  470.5 4.9 copy-start.2
Sparse Core Ops, SparseCore 0:
  10.4 187.0 all-gather.2
  199.9 187.4 all-gather.4
  391.8 72.5 all-reduce.2
  470.6 402.8 reduce-scatter.1
where the time goes:
time: 883 us; the launch traced here: 882 us
  waiting for transfers between devices  838 us (95%)
  matrix products  23.3 us (3%)
  between operations  13.8 us (2%)
    reduce_scatter x1, waiting for transfers between devices, shards(): lax.psum_scatter(jnp.dot(grad_pre, up_weight, preferred_element_type=jnp....  395 us
    all_gather x1, waiting for transfers between devices, shards(): grads = lax.all_gather(local_grads, ('depth', 'col'), axis=0, tiled=True)  185 us
    all_gather x1, waiting for transfers between devices, shards(): inputs = lax.all_gather(local_inputs, ('depth', 'col'), axis=0, tiled=True)  185 us
    psum x1, waiting for transfers between devices, shards(): preact, grad_act = lax.psum((pre_part, act_part), 'row')  72.6 us
  transfers between devices with their start and end apart: 4, of which 4 were waited for; matrix products, arithmetic and copies ran while one was open for 2% of the time, Pallas kernels for 0%

commit v1 on v0

v1 whole, which is shorter than its diff:
```python
import math

import jax
import jax.numpy as jnp
from jax import lax
from jax.experimental import pallas as pl
from jax.experimental.pallas import tpu as pltpu
from jax.sharding import Mesh, PartitionSpec as P

BF = jnp.bfloat16
F32 = jnp.float32
TILE = 128
OFFSETS = (0, -1, -2, -3, -4, 1, 2, 3)
VMEM = 48 * 1024 * 1024


def z_index(z):
    z %= 8
    return (z % 4) * 2 + z // 4


def z_shift(array, k):
    return lax.ppermute(array, ("zl", "zh"), [(z_index(z), z_index(z + k)) for z in range(8)])


def y_shift(array, k):
    return lax.ppermute(array, "y", [(y, (y + k) % 4) for y in range(4)])


def x_from(array, k):
    return lax.ppermute(array, ("y", "x"), [(y * 4 + (x + y + k) % 4, y * 4 + x) for y in range(4) for x in range(4)])


def x_back(array, k):
    return lax.ppermute(array, ("y", "x"), [(y * 4 + x, y * 4 + (x + y + k) % 4) for y in range(4) for x in range(4)])


def other_core(array):
    return lax.ppermute(array, "core", [(0, 1), (1, 0)])


def signs():
    rows = lax.broadcasted_iota(jnp.int32, (TILE, TILE), 0)
    cols = lax.broadcasted_iota(jnp.int32, (TILE, TILE), 1)
    bits = jnp.bitwise_and(rows, cols)
    bits = jnp.bitwise_xor(bits, jnp.right_shift(bits, 4))
    bits = jnp.bitwise_xor(bits, jnp.right_shift(bits, 2))
    bits = jnp.bitwise_xor(bits, jnp.right_shift(bits, 1))
    return (1 - 2 * jnp.bitwise_and(bits, 1)).astype(F32).astype(BF)


def dequant_kernel(xc, xs, gc, gs, inputs, grads):
    tiles = xc.shape[1] // TILE
    codes = [ref[:, k * TILE : (k + 1) * TILE].astype(F32) for ref in (xc, gc) for k in range(tiles)]
    turned = jnp.dot(jnp.concatenate(codes, 0).astype(BF), signs(), preferred_element_type=F32)
    turned = turned * (1.0 / math.sqrt(TILE))
    for at, (scale, out) in enumerate(((xs, inputs), (gs, grads))):
        for k in range(tiles):
            row = (at * tiles + k) * 8
            out[:, k * TILE : (k + 1) * TILE] = (turned[row : row + 8] * scale[:, k : k + 1]).astype(BF)


def dequant(xc, xs, gc, gs):
    shape = jax.ShapeDtypeStruct(xc.shape, BF)
    return pl.pallas_call(dequant_kernel, out_shape=(shape, shape), name="dequant")(xc, xs, gc, gs)


def any_spec():
    return pl.BlockSpec(memory_space=pl.ANY)


def vmem_spec():
    return pl.BlockSpec(memory_space=pltpu.VMEM)


def to_slots(rows):
    return jnp.concatenate([rows[32 * d + 8 * s : 32 * d + 8 * s + 8] for s in range(4) for d in range(8)], 0)


def from_slots(rows):
    return jnp.concatenate([rows[64 * s + 8 * d : 64 * s + 8 * d + 8] for d in range(8) for s in range(4)], 0)


def pre_kernel(*refs):
    i_parts, g_parts, weights = refs[:8], refs[8:12], refs[12:16]
    own, s1, s2, s3, both = refs[16:21]
    i_all, g_all, wu, wd, sems, out_sem = refs[21:]
    copies = []

    def start(src, dst):
        copy = pltpu.make_async_copy(src, dst, sems.at[len(copies)])
        copy.start()
        copies.append(copy)

    hid = weights[0].shape[0]
    start(weights[0], wu.at[pl.ds(0, hid)])
    start(weights[1], wu.at[pl.ds(hid, hid)])
    for n, ref in enumerate(i_parts):
        start(ref, i_all.at[pl.ds(32 * n, 32)])
    first = len(copies)
    start(weights[2], wd.at[pl.ds(0, hid)])
    start(weights[3], wd.at[pl.ds(hid, hid)])
    for n, ref in enumerate(g_parts):
        start(ref, g_all.at[pl.ds(64 * n, 64)])
    outs = (s1, s2, s3)
    step = 384
    for at, (mat, w, lo, hi) in enumerate(((i_all, wu, 0, first), (g_all, wd, first, len(copies)))):
        for copy in copies[lo:hi]:
            copy.wait()
        back = pltpu.make_async_copy(mat, both.at[at], out_sem.at[at])
        back.start()
        for n in range(0, 2 * hid, step):
            part = lax.dot_general(mat[...], w[n : n + step, :], (((1,), (1,)), ((), ())), preferred_element_type=F32)
            if at == 0:
                part = to_slots(part)
            own[at, :, n : n + step] = part[:64]
            for k in range(3):
                outs[k][at, :, n : n + step] = part[64 * (k + 1) : 64 * (k + 2)].astype(BF)
        back.wait()


def pre(i_parts, g_parts, weights):
    hid, wide = weights[0].shape
    sent = jax.ShapeDtypeStruct((2, 64, 2 * hid), BF)
    return pl.pallas_call(
        pre_kernel,
        out_shape=(jax.ShapeDtypeStruct((2, 64, 2 * hid), F32), sent, sent, sent, jax.ShapeDtypeStruct((2, 256, wide), BF)),
        in_specs=[any_spec()] * 16,
        out_specs=[vmem_spec()] * 4 + [any_spec()],
        scratch_shapes=[
            pltpu.VMEM((256, wide), BF),
            pltpu.VMEM((256, wide), BF),
            pltpu.VMEM((2 * hid, wide), BF),
            pltpu.VMEM((2 * hid, wide), BF),
            pltpu.SemaphoreType.DMA((16,)),
            pltpu.SemaphoreType.DMA((2,)),
        ],
        compiler_params=pltpu.CompilerParams(vmem_limit_bytes=VMEM),
        name="pre",
    )(*i_parts, *g_parts, *weights)


def act_kernel(own, r1, r2, r3, out):
    total = [own[at] + r1[at].astype(F32) + r2[at].astype(F32) + r3[at].astype(F32) for at in range(2)]
    positive = jnp.maximum(total[0], 0.0)
    out[0] = (positive * positive).astype(BF)
    out[1] = (2.0 * total[1] * positive).astype(BF)


def act(own, parts):
    return pl.pallas_call(
        act_kernel,
        out_shape=jax.ShapeDtypeStruct(own.shape, BF),
        compiler_params=pltpu.CompilerParams(vmem_limit_bytes=VMEM),
        name="act",
    )(own, *parts)


def back_kernel(p0, p1, p2, p3, w_own, w_oth, o0, o1, o2, o3, keep, send, wu, sems):
    hid = w_own.shape[0]
    c0 = pltpu.make_async_copy(w_own, wu.at[pl.ds(0, hid)], sems.at[0])
    c1 = pltpu.make_async_copy(w_oth, wu.at[pl.ds(hid, hid)], sems.at[1])
    c0.start()
    c1.start()
    parts = (p0, p1, p2, p3)
    for at in range(2):
        full = jnp.concatenate([p[at].astype(F32) for p in parts], 0)
        if at == 1:
            full = from_slots(full)
        full = full.astype(BF)
        keep[at] = full[:, :hid]
        send[at] = full[:, hid:]
    lhs = jnp.concatenate([p[1] for p in parts], 0)
    c0.wait()
    c1.wait()
    step = 768
    for n in range(0, wu.shape[1], step):
        out = jnp.dot(lhs, wu[:, n : n + step], preferred_element_type=F32).astype(BF)
        for k, ref in enumerate((o0, o1, o2, o3)):
            ref[:, n : n + step] = out[64 * k : 64 * k + 64]


def back(parts, w_own, w_oth):
    hid, wide = w_own.shape
    piece = jax.ShapeDtypeStruct((64, wide), BF)
    swap = jax.ShapeDtypeStruct((2, 256, hid), BF)
    return pl.pallas_call(
        back_kernel,
        out_shape=(piece,) * 4 + (swap, swap),
        in_specs=[vmem_spec()] * 4 + [any_spec()] * 2,
        out_specs=[vmem_spec()] * 6,
        scratch_shapes=[pltpu.VMEM((2 * hid, wide), BF), pltpu.SemaphoreType.DMA((2,))],
        compiler_params=pltpu.CompilerParams(vmem_limit_bytes=VMEM),
        name="back",
    )(*parts, w_own, w_oth)


def add_kernel(*refs):
    out = refs[-1]
    total = refs[0][...].astype(F32)
    for ref in refs[1:-1]:
        total = total + ref[...].astype(F32)
    out[...] = total.astype(BF)


def add(*parts):
    return pl.pallas_call(
        add_kernel,
        out_shape=jax.ShapeDtypeStruct(parts[0].shape, BF),
        compiler_params=pltpu.CompilerParams(vmem_limit_bytes=VMEM),
        name="add",
    )(*parts)


def split_kernel(p0, p1, p2, p3, *outs):
    total = p0[...].astype(F32) + p1[...].astype(F32) + p2[...].astype(F32) + p3[...].astype(F32)
    for d, out in enumerate(outs):
        out[...] = total[8 * d : 8 * d + 8].astype(BF)


def add_split(parts):
    return pl.pallas_call(
        split_kernel,
        out_shape=(jax.ShapeDtypeStruct((8, parts[0].shape[1]), BF),) * 8,
        compiler_params=pltpu.CompilerParams(vmem_limit_bytes=VMEM),
        name="add_split",
    )(*parts)


def weights_kernel(keep, came, both, both_came, up, down, sq, gp, mats, sems):
    copies = []
    for at in range(2):
        for half, src in enumerate((both, both_came)):
            copy = pltpu.make_async_copy(src.at[at], mats.at[at, pl.ds(256 * half, 256)], sems.at[at, half])
            copy.start()
            copies.append(copy)
    for at, (ref, out, mat) in enumerate(((sq, down, 1), (gp, up, 0))):
        ref[...] = jnp.concatenate([keep[at], came[at]], 0).T
    for at, (ref, out, mat) in enumerate(((gp, up, 0), (sq, down, 1))):
        copies[2 * mat].wait()
        copies[2 * mat + 1].wait()
        step = 768
        for n in range(0, out.shape[1], step):
            out[:, n : n + step] = jnp.dot(ref[...], mats[mat, :, n : n + step], preferred_element_type=F32).astype(BF)


def weight_grads(keep, came, both, both_came):
    hid, wide = keep.shape[2], both.shape[2]
    shape = jax.ShapeDtypeStruct((hid, wide), BF)
    return pl.pallas_call(
        weights_kernel,
        out_shape=(shape, shape),
        in_specs=[vmem_spec()] * 2 + [any_spec()] * 2,
        out_specs=[vmem_spec()] * 2,
        scratch_shapes=[
            pltpu.VMEM((hid, 512), BF),
            pltpu.VMEM((hid, 512), BF),
            pltpu.VMEM((2, 512, wide), BF),
            pltpu.SemaphoreType.DMA((2, 2)),
        ],
        compiler_params=pltpu.CompilerParams(vmem_limit_bytes=VMEM),
        name="weight_grads",
    )(keep, came, both, both_came)


def gather_z(block):
    right, left = [block], [block]
    for _ in range(3):
        right.append(z_shift(right[-1], 1))
        left.append(z_shift(left[-1], -1))
    right.append(z_shift(right[-1], 1))
    return right + left[1:]


def shards(x_code, x_scale, g_code, g_scale, up_weight, down_weight):
    up_other = other_core(up_weight)
    down_other = other_core(down_weight)
    inputs, grads = dequant(x_code, x_scale, g_code, g_scale)
    i_parts = gather_z(jnp.concatenate([x_from(inputs, k) for k in range(4)], 0))
    column = jnp.concatenate(gather_z(grads), 0)
    g_parts = [x_from(column, k) for k in range(4)]
    own, s1, s2, s3, both = pre(i_parts, g_parts, (up_weight, up_other, down_weight, down_other))
    both_came = other_core(both)
    mine = act(own, [y_shift(s, k) for s, k in ((s1, 1), (s2, 2), (s3, 3))])
    parts = [mine] + [y_shift(mine, -k) for k in (1, 2, 3)]
    *pieces, keep, send = back(parts, up_weight, up_other)
    came = other_core(send)
    blocks = add_split([x_back(piece, k) for k, piece in enumerate(pieces)])
    grad_input = add(*[z_shift(block, dz) if dz else block for block, dz in zip(blocks, OFFSETS)])
    grad_up, grad_down = weight_grads(keep, came, both, both_came)
    return (grad_input, grad_up, grad_down)


def solution(mesh):
    fine = Mesh(mesh.devices.reshape(4, 2, 4, 4, 2), ("zl", "core", "y", "x", "zh"))
    spec = P(("zl", "core", "x", "zh"), "y")
    return jax.shard_map(shards, mesh=fine, in_specs=(spec,) * 6, out_specs=(spec,) * 3, check_vma=False)
```

time: 883 us -> 188 us (0.21)
  the two profiles are of different devices: /device:TPU:1 before, /device:TPU:24 now
where the time goes in v1:
time: 188 us
  waiting for transfers between devices  84.7 us (45%)
  starting transfers between devices  70.4 us (37%)
  Pallas kernels  21.2 us (11%)
  local copies, waits for them, and re-layouts  10.3 us (5%)
    ppermute x21, waiting for transfers between devices, z_shift(): lax.ppermute(array, ('zl', 'zh'), [(z_index(z), z_index(z + k)) for z in...  39.5 us
    ppermute x6, waiting for transfers between devices, y_shift(): return lax.ppermute(array, 'y', [(y, (y + k) % 4) for y in range(4)])  26.9 us
    ppermute x21, starting transfers between devices, z_shift(): lax.ppermute(array, ('zl', 'zh'), [(z_index(z), z_index(z + k)) for z in...  24.1 us
    ppermute x8, starting transfers between devices, x_from(): lax.ppermute(array, ('y', 'x'), [(y * 4 + (x + y + k) % 4, y * 4 + x) for...  20.9 us
    ppermute x4, starting transfers between devices, x_back(): lax.ppermute(array, ('y', 'x'), [(y * 4 + x, y * 4 + (x + y + k) % 4) for...  13.2 us
    ppermute x4, waiting for transfers between devices, x_back(): lax.ppermute(array, ('y', 'x'), [(y * 4 + x, y * 4 + (x + y + k) % 4) for...  12 us
    ppermute x6, starting transfers between devices, y_shift(): return lax.ppermute(array, 'y', [(y, (y + k) % 4) for y in range(4)])  11.7 us
    unnamed x24, local copies, waits for them, and re-layouts  7.87 us
  transfers between devices with their start and end apart: 43, of which 22 were waited for; matrix products, arithmetic and copies ran while one was open for 2% of the time, Pallas kernels for 3%

profile of v1, /device:TPU:24, one launch (start us, length us, event | category | flops | bytes accessed | tf_op | source)
XLA Modules:
  0.0 187.7 jit_solution(17361688949984842675)
XLA Ops:
  2.2 5.9 %collective-permute-start.15 = (bf16[8,2304]{1,0:T(8,128)(2,1)}, bf16[8,2304]{1,0:T(8,128)(2,1)S(1)}, u32[]{:S(2)}, u32[]{:S(2)}) collective-permute-start(bf16[8,2304]{1,0:T(8,128)(2,1)} %get-tuple-element.27), channel_id=1, source_target_pairs={{0,193},{64,0},{128,64},{192,128},{1,192},{65,1},{129,65},{193,129... | collective-permute-start | bytes 110600 | tf_op jit(solution)/shard_map/ppermute | solution.py:23
  8.1 4.9 %collective-permute-start.3 = (bf16[8,2304]{1,0:T(8,128)(2,1)}, bf16[8,2304]{1,0:T(8,128)(2,1)S(1)}, u32[]{:S(2)}, u32[]{:S(2)}) collective-permute-start(bf16[8,2304]{1,0:T(8,128)(2,1)} %get-tuple-element.26), channel_id=1, source_target_pairs={{6,0},{0,2},{2,4},{4,6},{8,8},{10,10},{12,12},{14,14},{18,16},{20,... | collective-permute-start | bytes 110600 | tf_op jit(solution)/shard_map/ppermute | solution.py:31
  13.0 3.0 %collective-permute-start.2 = (bf16[8,2304]{1,0:T(8,128)(2,1)}, bf16[8,2304]{1,0:T(8,128)(2,1)S(1)}, u32[]{:S(2)}, u32[]{:S(2)}) collective-permute-start(bf16[8,2304]{1,0:T(8,128)(2,1)} %get-tuple-element.26), channel_id=1, source_target_pairs={{4,0},{6,2},{0,4},{2,6},{14,8},{8,10},{10,12},{12,14},{16,16},{18,... | collective-permute-start | bytes 110600 | tf_op jit(solution)/shard_map/ppermute | solution.py:31
  16.1 2.8 %collective-permute-start = (bf16[8,2304]{1,0:T(8,128)(2,1)}, bf16[8,2304]{1,0:T(8,128)(2,1)S(1)}, u32[]{:S(2)}, u32[]{:S(2)}) collective-permute-start(bf16[8,2304]{1,0:T(8,128)(2,1)} %get-tuple-element.26), channel_id=1, source_target_pairs={{0,0},{2,2},{4,4},{6,6},{10,8},{12,10},{14,12},{8,14},{20,16},{22,... | collective-permute-start | bytes 110600 | tf_op jit(solution)/shard_map/ppermute | solution.py:31
  19.7 3.7 %collective-permute-done = bf16[8,2304]{1,0:T(8,128)(2,1)S(1)} collective-permute-done((bf16[8,2304]{1,0:T(8,128)(2,1)}, bf16[8,2304]{1,0:T(8,128)(2,1)S(1)}, u32[]{:S(2)}, u32[]{:S(2)}) %collective-permute-start) | collective-permute-done | bytes 36896 | tf_op jit(solution)/shard_map/ppermute | solution.py:31
  25.3 3.3 %collective-permute-start.8 = (bf16[32,2304]{1,0:T(8,128)(2,1)S(1)}, bf16[32,2304]{1,0:T(8,128)(2,1)S(1)}, u32[]{:S(2)}, u32[]{:S(2)}) collective-permute-start(bf16[32,2304]{1,0:T(8,128)(2,1)S(1)} %constant_dynamic-update-slice_fusion.refs_0_), channel_id=1, source_target_pairs={{0,193},{64,0},{128,64},{192,128},{1,192},{65,1},{129,65},{193,129... | collective-permute-start | bytes 442376 | tf_op jit(solution)/shard_map/ppermute | solution.py:23
  30.7 3.2 %collective-permute-done.12 = bf16[8,2304]{1,0:T(8,128)(2,1)S(1)} collective-permute-done((bf16[8,2304]{1,0:T(8,128)(2,1)S(1)}, bf16[8,2304]{1,0:T(8,128)(2,1)S(1)}, u32[]{:S(2)}, u32[]{:S(2)}) %collective-permute-start.12) | collective-permute-done | bytes 36896 | tf_op jit(solution)/shard_map/ppermute | solution.py:23
  34.6 4.4 %collective-permute-done.13 = bf16[8,2304]{1,0:T(8,128)(2,1)S(1)} collective-permute-done((bf16[8,2304]{1,0:T(8,128)(2,1)S(1)}, bf16[8,2304]{1,0:T(8,128)(2,1)S(1)}, u32[]{:S(2)}, u32[]{:S(2)}) %collective-permute-start.13) | collective-permute-done | bytes 36896 | tf_op jit(solution)/shard_map/ppermute | solution.py:23
  39.2 5.1 %collective-permute-done.14 = bf16[8,2304]{1,0:T(8,128)(2,1)S(1)} collective-permute-done((bf16[8,2304]{1,0:T(8,128)(2,1)S(1)}, bf16[8,2304]{1,0:T(8,128)(2,1)S(1)}, u32[]{:S(2)}, u32[]{:S(2)}) %collective-permute-start.14) | collective-permute-done | bytes 36896 | tf_op jit(solution)/shard_map/ppermute | solution.py:23
  44.5 3.7 %collective-permute-done.17 = bf16[8,2304]{1,0:T(8,128)(2,1)S(1)} collective-permute-done((bf16[8,2304]{1,0:T(8,128)(2,1)S(1)}, bf16[8,2304]{1,0:T(8,128)(2,1)S(1)}, u32[]{:S(2)}, u32[]{:S(2)}) %collective-permute-start.17) | collective-permute-done | bytes 36896 | tf_op jit(solution)/shard_map/ppermute | solution.py:23
  48.2 2.2 %collective-permute-start.21 = (bf16[64,2304]{1,0:T(8,128)(2,1)S(1)}, bf16[64,2304]{1,0:T(8,128)(2,1)S(1)}, u32[]{:S(2)}, u32[]{:S(2)}) collective-permute-start(bf16[64,2304]{1,0:T(8,128)(2,1)S(1)} %constant_dynamic-update-slice_fusion.4), channel_id=1, source_target_pairs={{6,0},{0,2},{2,4},{4,6},{8,8},{10,10},{12,12},{14,14},{18,16},{20,... | collective-permute-start | bytes 884744 | tf_op jit(solution)/shard_map/ppermute | solution.py:31
  50.5 3.9 %collective-permute-start.20 = (bf16[64,2304]{1,0:T(8,128)(2,1)S(1)}, bf16[64,2304]{1,0:T(8,128)(2,1)S(1)}, u32[]{:S(2)}, u32[]{:S(2)}) collective-permute-start(bf16[64,2304]{1,0:T(8,128)(2,1)S(1)} %constant_dynamic-update-slice_fusion.4), channel_id=1, source_target_pairs={{4,0},{6,2},{0,4},{2,6},{14,8},{8,10},{10,12},{12,14},{16,16},{18,... | collective-permute-start | bytes 884744 | tf_op jit(solution)/shard_map/ppermute | solution.py:31
  54.5 2.4 %collective-permute-done.5.refs_2_ = bf16[32,2304]{1,0:T(8,128)(2,1)S(1)} collective-permute-done((bf16[32,2304]{1,0:T(8,128)(2,1)S(1)}, bf16[32,2304]{1,0:T(8,128)(2,1)S(1)}, u32[]{:S(2)}, u32[]{:S(2)}) %collective-permute-start.5) | collective-permute-done | bytes 147488 | tf_op jit(solution)/shard_map/ppermute | solution.py:23
  61.6 2.9 %collective-permute-start.10 = (bf16[32,2304]{1,0:T(8,128)(2,1)S(1)}, bf16[32,2304]{1,0:T(8,128)(2,1)S(1)}, u32[]{:S(2)}, u32[]{:S(2)}) collective-permute-start(bf16[32,2304]{1,0:T(8,128)(2,1)S(1)} %collective-permute-done.9.refs_6_), channel_id=1, source_target_pairs={{0,193},{64,0},{128,64},{192,128},{1,192},{65,1},{129,65},{193,129... | collective-permute-start | bytes 442376 | tf_op jit(solution)/shard_map/ppermute | solution.py:23
  64.5 3.7 %collective-permute-done.6.refs_3_ = bf16[32,2304]{1,0:T(8,128)(2,1)S(1)} collective-permute-done((bf16[32,2304]{1,0:T(8,128)(2,1)S(1)}, bf16[32,2304]{1,0:T(8,128)(2,1)S(1)}, u32[]{:S(2)}, u32[]{:S(2)}) %collective-permute-start.6) | collective-permute-done | bytes 147488 | tf_op jit(solution)/shard_map/ppermute | solution.py:23
  69.1 5.5 %collective-permute-done.7.refs_4_ = bf16[32,2304]{1,0:T(8,128)(2,1)S(1)} collective-permute-done((bf16[32,2304]{1,0:T(8,128)(2,1)S(1)}, bf16[32,2304]{1,0:T(8,128)(2,1)S(1)}, u32[]{:S(2)}, u32[]{:S(2)}) %collective-permute-start.7) | collective-permute-done | bytes 147488 | tf_op jit(solution)/shard_map/ppermute | solution.py:23
  77.6 7.2 %pre.1 = (f32[2,64,1152]{2,1,0:T(8,128)S(1)}, bf16[2,64,1152]{2,1,0:T(8,128)(2,1)S(1)}, bf16[2,64,1152]{2,1,0:T(8,128)(2,1)S(1)}, bf16[2,64,1152]{2,1,0:T(8,128)(2,1)S(1)}, bf16[2,256,2304]{2,1,0:T(8,128)(2,1)S(1)}) custom-call(bf16[32,2304]{1,0:T(8,128)(2,1)S(1)} %constant_dynamic-update-slice_fusion.refs_0_, ...), custom_call_target="tpu_custom_call" | custom-call | tf_op jit(solution)/shard_map/pre/pallas_call | solution.py:125
  86.5 6.2 %collective-permute-start.25 = (bf16[2,64,1152]{2,1,0:T(8,128)(2,1)S(1)}, bf16[2,64,1152]{2,1,0:T(8,128)(2,1)S(1)}, u32[]{:S(2)}, u32[]{:S(2)}) collective-permute-start(bf16[2,64,1152]{2,1,0:T(8,128)(2,1)S(1)} %get-tuple-element.30), channel_id=1, source_target_pairs={{0,16},{8,24},{16,0},{24,8},{1,17},{9,25},{17,1},{25,9},{2,18},{10... | collective-permute-start | bytes 884744 | tf_op jit(solution)/shard_map/ppermute | solution.py:27
  92.7 5.8 %collective-permute-done.24.r1 = bf16[2,64,1152]{2,1,0:T(8,128)(2,1)S(1)} collective-permute-done((bf16[2,64,1152]{2,1,0:T(8,128)(2,1)S(1)}, bf16[2,64,1152]{2,1,0:T(8,128)(2,1)S(1)}, u32[]{:S(2)}, u32[]{:S(2)}) %collective-permute-start.24) | collective-permute-done | bytes 294944 | tf_op jit(solution)/shard_map/ppermute | solution.py:27
  100.5 5.8 %collective-permute-done.26.r3 = bf16[2,64,1152]{2,1,0:T(8,128)(2,1)S(1)} collective-permute-done((bf16[2,64,1152]{2,1,0:T(8,128)(2,1)S(1)}, bf16[2,64,1152]{2,1,0:T(8,128)(2,1)S(1)}, u32[]{:S(2)}, u32[]{:S(2)}) %collective-permute-start.26) | collective-permute-done | bytes 294944 | tf_op jit(solution)/shard_map/ppermute | solution.py:27
  107.5 3.0 %collective-permute-start.28 = (bf16[2,64,1152]{2,1,0:T(8,128)(2,1)S(1)}, bf16[2,64,1152]{2,1,0:T(8,128)(2,1)S(1)}, u32[]{:S(2)}, u32[]{:S(2)}) collective-permute-start(bf16[2,64,1152]{2,1,0:T(8,128)(2,1)S(1)} %act.1.p0), channel_id=1, source_target_pairs={{0,16},{8,24},{16,0},{24,8},{1,17},{9,25},{17,1},{25,9},{2,18},{10... | collective-permute-start | bytes 884744 | tf_op jit(solution)/shard_map/ppermute | solution.py:27
  110.4 6.0 %collective-permute-done.29.p3 = bf16[2,64,1152]{2,1,0:T(8,128)(2,1)S(1)} collective-permute-done((bf16[2,64,1152]{2,1,0:T(8,128)(2,1)S(1)}, bf16[2,64,1152]{2,1,0:T(8,128)(2,1)S(1)}, u32[]{:S(2)}, u32[]{:S(2)}) %collective-permute-start.29) | collective-permute-done | bytes 294944 | tf_op jit(solution)/shard_map/ppermute | solution.py:27
  116.5 2.5 %collective-permute-done.28.p2 = bf16[2,64,1152]{2,1,0:T(8,128)(2,1)S(1)} collective-permute-done((bf16[2,64,1152]{2,1,0:T(8,128)(2,1)S(1)}, bf16[2,64,1152]{2,1,0:T(8,128)(2,1)S(1)}, u32[]{:S(2)}, u32[]{:S(2)}) %collective-permute-start.28) | collective-permute-done | bytes 294944 | tf_op jit(solution)/shard_map/ppermute | solution.py:27
  118.9 4.8 %collective-permute-done.27.p1 = bf16[2,64,1152]{2,1,0:T(8,128)(2,1)S(1)} collective-permute-done((bf16[2,64,1152]{2,1,0:T(8,128)(2,1)S(1)}, bf16[2,64,1152]{2,1,0:T(8,128)(2,1)S(1)}, u32[]{:S(2)}, u32[]{:S(2)}) %collective-permute-start.27) | collective-permute-done | bytes 294944 | tf_op jit(solution)/shard_map/ppermute | solution.py:27
  123.8 4.9 %back.1 = (bf16[64,2304]{1,0:T(8,128)(2,1)}, bf16[64,2304]{1,0:T(8,128)(2,1)S(1)}, bf16[64,2304]{1,0:T(8,128)(2,1)S(1)}, bf16[64,2304]{1,0:T(8,128)(2,1)S(1)}, b...) custom-call(bf16[2,64,1152]{2,1,0:T(8,128)(2,1)S(1)} %act.1.p0, ...), custom_call_target="tpu_custom_call" | custom-call | tf_op jit(solution)/shard_map/back/pallas_call | solution.py:187
  131.7 4.6 %collective-permute-start.30 = (bf16[64,2304]{1,0:T(8,128)(2,1)}, bf16[64,2304]{1,0:T(8,128)(2,1)S(1)}, u32[]{:S(2)}, u32[]{:S(2)}) collective-permute-start(bf16[64,2304]{1,0:T(8,128)(2,1)} %get-tuple-element.32), channel_id=1, source_target_pairs={{0,0},{2,2},{4,4},{6,6},{8,10},{10,12},{12,14},{14,8},{16,20},{18,... | collective-permute-start | bytes 884744 | tf_op jit(solution)/shard_map/ppermute | solution.py:35
  143.0 5.1 %collective-permute-start.33 = (bf16[64,2304]{1,0:T(8,128)(2,1)}, bf16[64,2304]{1,0:T(8,128)(2,1)S(1)}, u32[]{:S(2)}, u32[]{:S(2)}) collective-permute-start(bf16[64,2304]{1,0:T(8,128)(2,1)} %copy-done.2), channel_id=1, source_target_pairs={{0,6},{2,0},{4,2},{6,4},{8,8},{10,10},{12,12},{14,14},{16,18},{18,... | collective-permute-start | bytes 884744 | tf_op jit(solution)/shard_map/ppermute | solution.py:35
  148.1 9.8 %collective-permute-done.32.p2 = bf16[64,2304]{1,0:T(8,128)(2,1)S(1)} collective-permute-done((bf16[64,2304]{1,0:T(8,128)(2,1)}, bf16[64,2304]{1,0:T(8,128)(2,1)S(1)}, u32[]{:S(2)}, u32[]{:S(2)}) %collective-permute-start.32) | collective-permute-done | bytes 294944 | tf_op jit(solution)/shard_map/ppermute | solution.py:35
  160.2 2.4 %collective-permute-done.34.refs_1_ = bf16[8,2304]{1,0:T(8,128)(2,1)S(1)} collective-permute-done((bf16[8,2304]{1,0:T(8,128)(2,1)S(1)}, bf16[8,2304]{1,0:T(8,128)(2,1)S(1)}, u32[]{:S(2)}, u32[]{:S(2)}) %collective-permute-start.34) | collective-permute-done | bytes 36896 | tf_op jit(solution)/shard_map/ppermute | solution.py:23
  166.5 2.5 %collective-permute-start.39 = (bf16[8,2304]{1,0:T(8,128)(2,1)S(1)}, bf16[8,2304]{1,0:T(8,128)(2,1)S(1)}, u32[]{:S(2)}, u32[]{:S(2)}) collective-permute-start(bf16[8,2304]{1,0:T(8,128)(2,1)S(1)} %get-tuple-element.42), channel_id=1, source_target_pairs={{0,128},{64,192},{128,1},{192,65},{1,129},{65,193},{129,0},{193,64... | collective-permute-start | bytes 110600 | tf_op jit(solution)/shard_map/ppermute | solution.py:23
  172.9 5.1 %collective-permute-done.40.refs_7_ = bf16[8,2304]{1,0:T(8,128)(2,1)S(1)} collective-permute-done((bf16[8,2304]{1,0:T(8,128)(2,1)S(1)}, bf16[8,2304]{1,0:T(8,128)(2,1)S(1)}, u32[]{:S(2)}, u32[]{:S(2)}) %collective-permute-start.40) | collective-permute-done | bytes 36896 | tf_op jit(solution)/shard_map/ppermute | solution.py:23
  181.1 6.4 %weight_grads.1 = (bf16[576,2304]{1,0:T(8,128)(2,1)}, bf16[576,2304]{1,0:T(8,128)(2,1)}) custom-call(bf16[2,256,576]{2,1,0:T(8,128)(2,1)S(1)} %copy-done.1, bf16[2,256,576]{2,1,0:T(8,128)(2,1)S(1)} %copy.10.came, bf16[2,256,2304]{2,1,0:T(8,128)(2,1)S(1)} %get-tuple-element.46.both, bf16[2,256,2304]{2,1,0:T(8,128)(2,1)} %collective-permute-done.42.both_came), custom_call_target="tpu_custom_call" | custom-call | tf_op jit(solution)/shard_map/weight_grads/pallas_call | solution.py:250
  (89 shorter events, 43.6 us)
Async XLA Ops:
  2.2 26.4 %collective-permute-start.15 = (bf16[8,2304]{1,0:T(8,128)(2,1)}, bf16[8,2304]{1,0:T(8,128)(2,1)S(1)}, u32[]{:S(2)}, u32[]{:S(2)}) collective-permute-start(bf16[8,2304]{1,0:T(8,128)(2,1)} %get-tuple-element.27), channel_id=1, source_target_pairs={{0,193},{64,0},{128,64},{192,128},{1,192},{65,1},{129,65},{193,129... | collective-permute-start | bytes 110600 | tf_op jit(solution)/shard_map/ppermute | solution.py:23
  8.1 20.6 %collective-permute-start.11 = (bf16[8,2304]{1,0:T(8,128)(2,1)}, bf16[8,2304]{1,0:T(8,128)(2,1)S(1)}, u32[]{:S(2)}, u32[]{:S(2)}) collective-permute-start(bf16[8,2304]{1,0:T(8,128)(2,1)} %get-tuple-element.27), channel_id=1, source_target_pairs={{0,64},{64,128},{128,192},{192,1},{1,65},{65,129},{129,193},{193,0... | collective-permute-start | bytes 110600 | tf_op jit(solution)/shard_map/ppermute | solution.py:23
  8.1 17.2 %collective-permute-start.3 = (bf16[8,2304]{1,0:T(8,128)(2,1)}, bf16[8,2304]{1,0:T(8,128)(2,1)S(1)}, u32[]{:S(2)}, u32[]{:S(2)}) collective-permute-start(bf16[8,2304]{1,0:T(8,128)(2,1)} %get-tuple-element.26), channel_id=1, source_target_pairs={{6,0},{0,2},{2,4},{4,6},{8,8},{10,10},{12,12},{14,14},{18,16},{20,... | collective-permute-start | bytes 110600 | tf_op jit(solution)/shard_map/ppermute | solution.py:31
  13.0 11.8 %collective-permute-start.2 = (bf16[8,2304]{1,0:T(8,128)(2,1)}, bf16[8,2304]{1,0:T(8,128)(2,1)S(1)}, u32[]{:S(2)}, u32[]{:S(2)}) collective-permute-start(bf16[8,2304]{1,0:T(8,128)(2,1)} %get-tuple-element.26), channel_id=1, source_target_pairs={{4,0},{6,2},{0,4},{2,6},{14,8},{8,10},{10,12},{12,14},{16,16},{18,... | collective-permute-start | bytes 110600 | tf_op jit(solution)/shard_map/ppermute | solution.py:31
  16.1 7.3 %collective-permute-start = (bf16[8,2304]{1,0:T(8,128)(2,1)}, bf16[8,2304]{1,0:T(8,128)(2,1)S(1)}, u32[]{:S(2)}, u32[]{:S(2)}) collective-permute-start(bf16[8,2304]{1,0:T(8,128)(2,1)} %get-tuple-element.26), channel_id=1, source_target_pairs={{0,0},{2,2},{4,4},{6,6},{10,8},{12,10},{14,12},{8,14},{20,16},{22,... | collective-permute-start | bytes 110600 | tf_op jit(solution)/shard_map/ppermute | solution.py:31
  24.8 49.8 %collective-permute-start.23 = (bf16[576,2304]{1,0:T(8,128)(2,1)}, bf16[576,2304]{1,0:T(8,128)(2,1)S(1)}, u32[]{:S(2)}, u32[]{:S(2)}) collective-permute-start(bf16[576,2304]{1,0:T(8,128)(2,1)} %refs_14_.1), channel_id=1, source_target_pairs={{0,32},{32,0},{1,33},{33,1},{2,34},{34,2},{3,35},{35,3},{4,36},{36... | collective-permute-start | bytes 7962632 | tf_op jit(solution)/shard_map/ppermute | solution.py:39
  24.8 49.8 %collective-permute-start.22 = (bf16[576,2304]{1,0:T(8,128)(2,1)}, bf16[576,2304]{1,0:T(8,128)(2,1)S(1)}, u32[]{:S(2)}, u32[]{:S(2)}) collective-permute-start(bf16[576,2304]{1,0:T(8,128)(2,1)} %w_own.1), channel_id=1, source_target_pairs={{0,32},{32,0},{1,33},{33,1},{2,34},{34,2},{3,35},{35,3},{4,36},{36... | collective-permute-start | bytes 7962632 | tf_op jit(solution)/shard_map/ppermute | solution.py:39
  25.3 19.0 %collective-permute-start.8 = (bf16[32,2304]{1,0:T(8,128)(2,1)S(1)}, bf16[32,2304]{1,0:T(8,128)(2,1)S(1)}, u32[]{:S(2)}, u32[]{:S(2)}) collective-permute-start(bf16[32,2304]{1,0:T(8,128)(2,1)S(1)} %constant_dynamic-update-slice_fusion.refs_0_), channel_id=1, source_target_pairs={{0,193},{64,0},{128,64},{192,128},{1,192},{65,1},{129,65},{193,129... | collective-permute-start | bytes 442376 | tf_op jit(solution)/shard_map/ppermute | solution.py:23
  28.6 10.4 %collective-permute-start.16 = (bf16[8,2304]{1,0:T(8,128)(2,1)S(1)}, bf16[8,2304]{1,0:T(8,128)(2,1)S(1)}, u32[]{:S(2)}, u32[]{:S(2)}) collective-permute-start(bf16[8,2304]{1,0:T(8,128)(2,1)S(1)} %collective-permute-done.15), channel_id=1, source_target_pairs={{0,193},{64,0},{128,64},{192,128},{1,192},{65,1},{129,65},{193,129... | collective-permute-start | bytes 110600 | tf_op jit(solution)/shard_map/ppermute | solution.py:23
  39.1 11.3 %collective-permute-start.4 = (bf16[32,2304]{1,0:T(8,128)(2,1)S(1)}, bf16[32,2304]{1,0:T(8,128)(2,1)S(1)}, u32[]{:S(2)}, u32[]{:S(2)}) collective-permute-start(bf16[32,2304]{1,0:T(8,128)(2,1)S(1)} %constant_dynamic-update-slice_fusion.refs_0_), channel_id=1, source_target_pairs={{0,64},{64,128},{128,192},{192,1},{1,65},{65,129},{129,193},{193,0... | collective-permute-start | bytes 442376 | tf_op jit(solution)/shard_map/ppermute | solution.py:23
  48.2 11.0 %collective-permute-start.21 = (bf16[64,2304]{1,0:T(8,128)(2,1)S(1)}, bf16[64,2304]{1,0:T(8,128)(2,1)S(1)}, u32[]{:S(2)}, u32[]{:S(2)}) collective-permute-start(bf16[64,2304]{1,0:T(8,128)(2,1)S(1)} %constant_dynamic-update-slice_fusion.4), channel_id=1, source_target_pairs={{6,0},{0,2},{2,4},{4,6},{8,8},{10,10},{12,12},{14,14},{18,16},{20,... | collective-permute-start | bytes 884744 | tf_op jit(solution)/shard_map/ppermute | solution.py:31
  50.4 6.4 %collective-permute-start.5 = (bf16[32,2304]{1,0:T(8,128)(2,1)S(1)}, bf16[32,2304]{1,0:T(8,128)(2,1)S(1)}, u32[]{:S(2)}, u32[]{:S(2)}) collective-permute-start(bf16[32,2304]{1,0:T(8,128)(2,1)S(1)} %collective-permute-done.4.refs_1_), channel_id=1, source_target_pairs={{0,64},{64,128},{128,192},{192,1},{1,65},{65,129},{129,193},{193,0... | collective-permute-start | bytes 442376 | tf_op jit(solution)/shard_map/ppermute | solution.py:23
  50.5 10.6 %collective-permute-start.20 = (bf16[64,2304]{1,0:T(8,128)(2,1)S(1)}, bf16[64,2304]{1,0:T(8,128)(2,1)S(1)}, u32[]{:S(2)}, u32[]{:S(2)}) collective-permute-start(bf16[64,2304]{1,0:T(8,128)(2,1)S(1)} %constant_dynamic-update-slice_fusion.4), channel_id=1, source_target_pairs={{4,0},{6,2},{0,4},{2,6},{14,8},{8,10},{10,12},{12,14},{16,16},{18,... | collective-permute-start | bytes 884744 | tf_op jit(solution)/shard_map/ppermute | solution.py:31
  59.2 9.8 %collective-permute-start.18 = (bf16[64,2304]{1,0:T(8,128)(2,1)S(1)}, bf16[64,2304]{1,0:T(8,128)(2,1)S(1)}, u32[]{:S(2)}, u32[]{:S(2)}) collective-permute-start(bf16[64,2304]{1,0:T(8,128)(2,1)S(1)} %constant_dynamic-update-slice_fusion.4), channel_id=1, source_target_pairs={{0,0},{2,2},{4,4},{6,6},{10,8},{12,10},{14,12},{8,14},{20,16},{22,... | collective-permute-start | bytes 884744 | tf_op jit(solution)/shard_map/ppermute | solution.py:31
  61.2 7.1 %collective-permute-start.6 = (bf16[32,2304]{1,0:T(8,128)(2,1)S(1)}, bf16[32,2304]{1,0:T(8,128)(2,1)S(1)}, u32[]{:S(2)}, u32[]{:S(2)}) collective-permute-start(bf16[32,2304]{1,0:T(8,128)(2,1)S(1)} %collective-permute-done.5.refs_2_), channel_id=1, source_target_pairs={{0,64},{64,128},{128,192},{192,1},{1,65},{65,129},{129,193},{193,0... | collective-permute-start | bytes 442376 | tf_op jit(solution)/shard_map/ppermute | solution.py:23
  61.6 7.5 %collective-permute-start.10 = (bf16[32,2304]{1,0:T(8,128)(2,1)S(1)}, bf16[32,2304]{1,0:T(8,128)(2,1)S(1)}, u32[]{:S(2)}, u32[]{:S(2)}) collective-permute-start(bf16[32,2304]{1,0:T(8,128)(2,1)S(1)} %collective-permute-done.9.refs_6_), channel_id=1, source_target_pairs={{0,193},{64,0},{128,64},{192,128},{1,192},{65,1},{129,65},{193,129... | collective-permute-start | bytes 442376 | tf_op jit(solution)/shard_map/ppermute | solution.py:23
  84.8 95.2 %collective-permute-start.42 = (bf16[2,256,2304]{2,1,0:T(8,128)(2,1)S(1)}, bf16[2,256,2304]{2,1,0:T(8,128)(2,1)}, u32[]{:S(2)}, u32[]{:S(2)}) collective-permute-start(bf16[2,256,2304]{2,1,0:T(8,128)(2,1)S(1)} %get-tuple-element.46.both), channel_id=1, source_target_pairs={{0,32},{32,0},{1,33},{33,1},{2,34},{34,2},{3,35},{35,3},{4,36},{36... | collective-permute-start | bytes 7077896 | tf_op jit(solution)/shard_map/ppermute | solution.py:39
  84.9 13.5 %collective-permute-start.24 = (bf16[2,64,1152]{2,1,0:T(8,128)(2,1)S(1)}, bf16[2,64,1152]{2,1,0:T(8,128)(2,1)S(1)}, u32[]{:S(2)}, u32[]{:S(2)}) collective-permute-start(bf16[2,64,1152]{2,1,0:T(8,128)(2,1)S(1)} %get-tuple-element.29), channel_id=1, source_target_pairs={{0,8},{8,16},{16,24},{24,0},{1,9},{9,17},{17,25},{25,1},{2,10},{10... | collective-permute-start | bytes 884744 | tf_op jit(solution)/shard_map/ppermute | solution.py:27
  86.5 14.0 %collective-permute-start.25 = (bf16[2,64,1152]{2,1,0:T(8,128)(2,1)S(1)}, bf16[2,64,1152]{2,1,0:T(8,128)(2,1)S(1)}, u32[]{:S(2)}, u32[]{:S(2)}) collective-permute-start(bf16[2,64,1152]{2,1,0:T(8,128)(2,1)S(1)} %get-tuple-element.30), channel_id=1, source_target_pairs={{0,16},{8,24},{16,0},{24,8},{1,17},{9,25},{17,1},{25,9},{2,18},{10... | collective-permute-start | bytes 884744 | tf_op jit(solution)/shard_map/ppermute | solution.py:27
  92.7 13.6 %collective-permute-start.26 = (bf16[2,64,1152]{2,1,0:T(8,128)(2,1)S(1)}, bf16[2,64,1152]{2,1,0:T(8,128)(2,1)S(1)}, u32[]{:S(2)}, u32[]{:S(2)}) collective-permute-start(bf16[2,64,1152]{2,1,0:T(8,128)(2,1)S(1)} %get-tuple-element.31), channel_id=1, source_target_pairs={{0,24},{8,0},{16,8},{24,16},{1,25},{9,1},{17,9},{25,17},{2,26},{10... | collective-permute-start | bytes 884744 | tf_op jit(solution)/shard_map/ppermute | solution.py:27
  106.5 9.9 %collective-permute-start.29 = (bf16[2,64,1152]{2,1,0:T(8,128)(2,1)S(1)}, bf16[2,64,1152]{2,1,0:T(8,128)(2,1)S(1)}, u32[]{:S(2)}, u32[]{:S(2)}) collective-permute-start(bf16[2,64,1152]{2,1,0:T(8,128)(2,1)S(1)} %act.1.p0), channel_id=1, source_target_pairs={{0,8},{8,16},{16,24},{24,0},{1,9},{9,17},{17,25},{25,1},{2,10},{10... | collective-permute-start | bytes 884744 | tf_op jit(solution)/shard_map/ppermute | solution.py:27
  107.5 11.5 %collective-permute-start.28 = (bf16[2,64,1152]{2,1,0:T(8,128)(2,1)S(1)}, bf16[2,64,1152]{2,1,0:T(8,128)(2,1)S(1)}, u32[]{:S(2)}, u32[]{:S(2)}) collective-permute-start(bf16[2,64,1152]{2,1,0:T(8,128)(2,1)S(1)} %act.1.p0), channel_id=1, source_target_pairs={{0,16},{8,24},{16,0},{24,8},{1,17},{9,25},{17,1},{25,9},{2,18},{10... | collective-permute-start | bytes 884744 | tf_op jit(solution)/shard_map/ppermute | solution.py:27
  110.4 13.3 %collective-permute-start.27 = (bf16[2,64,1152]{2,1,0:T(8,128)(2,1)S(1)}, bf16[2,64,1152]{2,1,0:T(8,128)(2,1)S(1)}, u32[]{:S(2)}, u32[]{:S(2)}) collective-permute-start(bf16[2,64,1152]{2,1,0:T(8,128)(2,1)S(1)} %act.1.p0), channel_id=1, source_target_pairs={{0,24},{8,0},{16,8},{24,16},{1,25},{9,1},{17,9},{25,17},{2,26},{10... | collective-permute-start | bytes 884744 | tf_op jit(solution)/shard_map/ppermute | solution.py:27
  131.7 11.4 %collective-permute-start.30 = (bf16[64,2304]{1,0:T(8,128)(2,1)}, bf16[64,2304]{1,0:T(8,128)(2,1)S(1)}, u32[]{:S(2)}, u32[]{:S(2)}) collective-permute-start(bf16[64,2304]{1,0:T(8,128)(2,1)} %get-tuple-element.32), channel_id=1, source_target_pairs={{0,0},{2,2},{4,4},{6,6},{8,10},{10,12},{12,14},{14,8},{16,20},{18,... | collective-permute-start | bytes 884744 | tf_op jit(solution)/shard_map/ppermute | solution.py:35
  137.3 41.3 %collective-permute-start.41 = (bf16[2,256,576]{1,2,0:T(8,128)(2,1)}, bf16[2,256,576]{1,2,0:T(8,128)(2,1)}, u32[]{:S(2)}, u32[]{:S(2)}) collective-permute-start(bf16[2,256,576]{1,2,0:T(8,128)(2,1)} %copy.9), channel_id=1, source_target_pairs={{0,32},{32,0},{1,33},{33,1},{2,34},{34,2},{3,35},{35,3},{4,36},{36... | collective-permute-start | bytes 1769480 | tf_op jit(solution)/shard_map/ppermute | solution.py:39
  137.3 10.8 %collective-permute-start.31 = (bf16[64,2304]{1,0:T(8,128)(2,1)}, bf16[64,2304]{1,0:T(8,128)(2,1)S(1)}, u32[]{:S(2)}, u32[]{:S(2)}) collective-permute-start(bf16[64,2304]{1,0:T(8,128)(2,1)} %copy-done.4), channel_id=1, source_target_pairs={{0,2},{2,4},{4,6},{6,0},{8,12},{10,14},{12,8},{14,10},{16,22},{18,... | collective-permute-start | bytes 884744 | tf_op jit(solution)/shard_map/ppermute | solution.py:35
  138.9 19.0 %collective-permute-start.32 = (bf16[64,2304]{1,0:T(8,128)(2,1)}, bf16[64,2304]{1,0:T(8,128)(2,1)S(1)}, u32[]{:S(2)}, u32[]{:S(2)}) collective-permute-start(bf16[64,2304]{1,0:T(8,128)(2,1)} %copy-done.3), channel_id=1, source_target_pairs={{0,4},{2,6},{4,0},{6,2},{8,14},{10,8},{12,10},{14,12},{16,16},{18,... | collective-permute-start | bytes 884744 | tf_op jit(solution)/shard_map/ppermute | solution.py:35
  143.0 14.9 %collective-permute-start.33 = (bf16[64,2304]{1,0:T(8,128)(2,1)}, bf16[64,2304]{1,0:T(8,128)(2,1)S(1)}, u32[]{:S(2)}, u32[]{:S(2)}) collective-permute-start(bf16[64,2304]{1,0:T(8,128)(2,1)} %copy-done.2), channel_id=1, source_target_pairs={{0,6},{2,0},{4,2},{6,4},{8,8},{10,10},{12,12},{14,14},{16,18},{18,... | collective-permute-start | bytes 884744 | tf_op jit(solution)/shard_map/ppermute | solution.py:35
  158.2 6.5 %collective-permute-start.35 = (bf16[8,2304]{1,0:T(8,128)(2,1)S(1)}, bf16[8,2304]{1,0:T(8,128)(2,1)S(1)}, u32[]{:S(2)}, u32[]{:S(2)}) collective-permute-start(bf16[8,2304]{1,0:T(8,128)(2,1)S(1)} %get-tuple-element.38), channel_id=1, source_target_pairs={{0,129},{64,193},{128,0},{192,64},{1,128},{65,192},{129,1},{193,65... | collective-permute-start | bytes 110600 | tf_op jit(solution)/shard_map/ppermute | solution.py:23
  158.5 8.0 %collective-permute-start.36 = (bf16[8,2304]{1,0:T(8,128)(2,1)S(1)}, bf16[8,2304]{1,0:T(8,128)(2,1)S(1)}, u32[]{:S(2)}, u32[]{:S(2)}) collective-permute-start(bf16[8,2304]{1,0:T(8,128)(2,1)S(1)} %get-tuple-element.39), channel_id=1, source_target_pairs={{0,65},{64,129},{128,193},{192,0},{1,64},{65,128},{129,192},{193,1... | collective-permute-start | bytes 110600 | tf_op jit(solution)/shard_map/ppermute | solution.py:23
  162.6 8.4 %collective-permute-start.37 = (bf16[8,2304]{1,0:T(8,128)(2,1)S(1)}, bf16[8,2304]{1,0:T(8,128)(2,1)S(1)}, u32[]{:S(2)}, u32[]{:S(2)}) collective-permute-start(bf16[8,2304]{1,0:T(8,128)(2,1)S(1)} %get-tuple-element.40), channel_id=1, source_target_pairs={{0,1},{64,65},{128,129},{192,193},{1,0},{65,64},{129,128},{193,192... | collective-permute-start | bytes 110600 | tf_op jit(solution)/shard_map/ppermute | solution.py:23
  171.0 7.0 %collective-permute-start.40 = (bf16[8,2304]{1,0:T(8,128)(2,1)S(1)}, bf16[8,2304]{1,0:T(8,128)(2,1)S(1)}, u32[]{:S(2)}, u32[]{:S(2)}) collective-permute-start(bf16[8,2304]{1,0:T(8,128)(2,1)S(1)} %get-tuple-element.43), channel_id=1, source_target_pairs={{0,192},{64,1},{128,65},{192,129},{1,193},{65,0},{129,64},{193,128... | collective-permute-start | bytes 110600 | tf_op jit(solution)/shard_map/ppermute | solution.py:23
  (18 other events, 62.4 us)

commit v2 on v0

v2 whole, which is shorter than its diff:
```python
import functools
import math

import jax
import jax.numpy as jnp
from jax import lax
from jax.experimental import pallas as pl
from jax.experimental.pallas import tpu as pltpu
from jax.sharding import Mesh, PartitionSpec as P

BF = jnp.bfloat16
F32 = jnp.float32
TILE = 128
MIB = 1024 * 1024
NEAR_FIRST = (0, 1, 3, 2)


def on_cores(array, moves):
    def index(z, core):
        z %= 8
        return (z % 4) * 4 + core * 2 + z // 4

    pairs = [(index(z, a), index(z + k, b)) for z in range(8) for a, b, k in moves]
    return lax.ppermute(array, ("zl", "core", "zh"), pairs)


def z_shift(array, k, k1):
    return on_cores(array, ((0, 0, k), (1, 1, k1)))


def xor_shift(array, axis, k):
    return lax.ppermute(array, axis, [(i, i ^ k) for i in range(4)])


def exchange(arrays, axis):
    return [xor_shift(array, axis, k) if k else array for array, k in zip(arrays, NEAR_FIRST)]


def other_core(array):
    return lax.ppermute(array, "core", [(0, 1), (1, 0)])


def in_hbm(*arrays):
    return [pltpu.with_memory_space_constraint(array, pltpu.HBM) for array in arrays]


def in_vmem(array):
    return pltpu.with_memory_space_constraint(array, pltpu.VMEM)


def any_spec():
    return pl.BlockSpec(memory_space=pl.ANY)


def vmem_spec():
    return pl.BlockSpec(memory_space=pltpu.VMEM)


def call(kernel, name, out, operands, ins=None, outs=None, scratch=(), limit=8):
    ins = ins or [False] * len(operands)
    outs = outs or [False] * len(out)
    return pl.pallas_call(
        kernel,
        out_shape=tuple(out),
        in_specs=[any_spec() if a else vmem_spec() for a in ins],
        out_specs=tuple(pl.BlockSpec(memory_space=a) if a else vmem_spec() for a in outs),
        scratch_shapes=list(scratch),
        compiler_params=pltpu.CompilerParams(vmem_limit_bytes=limit * MIB),
        cost_estimate=pl.CostEstimate(flops=1, bytes_accessed=1, transcendentals=0),
        name=name,
    )(*operands)


def struct(*shape, dtype=BF):
    return jax.ShapeDtypeStruct(shape, dtype)


def signs():
    rows = lax.broadcasted_iota(jnp.int32, (TILE, TILE), 0)
    cols = lax.broadcasted_iota(jnp.int32, (TILE, TILE), 1)
    bits = jnp.bitwise_and(rows, cols)
    bits = jnp.bitwise_xor(bits, jnp.right_shift(bits, 4))
    bits = jnp.bitwise_xor(bits, jnp.right_shift(bits, 2))
    bits = jnp.bitwise_xor(bits, jnp.right_shift(bits, 1))
    return (1 - 2 * jnp.bitwise_and(bits, 1)).astype(F32).astype(BF)


def dequant_kernel(xc_in, xs_in, gc_in, gs_in, out, xc, xs, gc, gs, sems):
    copies = [
        pltpu.make_async_copy(src, dst, sems.at[n])
        for n, (src, dst) in enumerate(((xc_in, xc), (gc_in, gc), (xs_in, xs), (gs_in, gs)))
    ]
    for copy in copies:
        copy.start()
    turn = signs()
    for copy in copies:
        copy.wait()
    tiles = xc.shape[1] // TILE
    codes = [ref[:, k * TILE : (k + 1) * TILE].astype(F32) for k in range(tiles) for ref in (xc, gc)]
    turned = jnp.dot(jnp.concatenate(codes, 0).astype(BF), turn, preferred_element_type=F32)
    turned = turned * (1.0 / math.sqrt(TILE))
    for k in range(tiles):
        scale = jnp.concatenate([xs[:, k : k + 1], gs[:, k : k + 1]], 0)
        out[:, k * TILE : (k + 1) * TILE] = (turned[16 * k : 16 * k + 16] * scale).astype(BF)


def regroup_kernel(own, oth, _, inputs, grads):
    own, oth = own[...].astype(F32), oth[...].astype(F32)
    inputs[...] = jnp.concatenate([own[:8], oth[:8]], 0).astype(BF)
    grads[...] = jnp.concatenate([own[8:], oth[8:]], 0).astype(BF)


def first_kernel(x0, x1, x2, x3, g0, g1, _, row, near):
    for n, ref in enumerate((x0, x1, x2, x3)):
        row[n] = ref[...]
    near[0] = g0[...]
    near[1] = g1[...]


def second_kernel(row, row1, near, near1, pair, column):
    pair[0] = row[...]
    pair[1] = row1[...]
    column[:2] = near[...]
    column[2:] = near1[...]


def join_kernel(up_own, up_oth, down_own, down_oth, _, up, down, sems):
    hid = up_own.shape[0]
    copies = []
    for n, (src, dst, at) in enumerate(((up_own, up, 0), (up_oth, up, hid), (down_own, down, 0), (down_oth, down, hid))):
        copies.append(pltpu.make_async_copy(src, dst.at[pl.ds(at, hid)], sems.at[n]))
        copies[-1].start()
    for copy in copies:
        copy.wait()


def pre_kernel(*refs, at, before):
    parts, weights, before, refs = refs[: 2 + 2 * at], refs[2 + 2 * at], refs[3 + 2 * at : 3 + 2 * at + before], refs[3 + 2 * at + before :]
    outs, rows_out, (rows, slots, sems, out_sem) = refs[:4], refs[4], refs[5:]
    y = lax.axis_index("y")
    copies = []
    for n in range(4):
        if at:
            copies.append(pltpu.make_async_copy(parts[n], rows.at[n], sems.at[n]))
        else:
            copies.append(pltpu.make_async_copy(parts[n // 2].at[n % 2], rows.at[:, n], sems.at[n]))
        copies[-1].start()
    for done, out in zip(before, outs):
        out[1 - at] = done[1 - at]
    for copy in copies:
        copy.wait()
    back = pltpu.make_async_copy(rows, rows_out, out_sem)
    back.start()
    hidden, wide = weights.shape
    step = slots.shape[2]
    for n in range(0, hidden, step):
        part = lax.dot_general(
            rows[...].reshape(256, wide), weights[n : n + step, :], (((1,), (1,)), ((), ())), preferred_element_type=F32
        )
        slots[...] = part.reshape(4, 64, step)
        for k, out in zip(NEAR_FIRST, outs):
            out[at, :, n : n + step] = slots[jnp.bitwise_xor(y, k)].astype(out.dtype)
    back.wait()


def pre(parts, weights, at, before):
    hidden, wide = weights.shape
    sent = struct(2, 64, hidden)
    *partial, rows = call(
        functools.partial(pre_kernel, at=at, before=len(before)), "pre",
        [struct(2, 64, hidden, dtype=F32), sent, sent, sent, struct(4, 4, 16, wide)], (*parts, in_vmem(weights), *before),
        ins=[True] * len(parts) + [False] * (1 + len(before)), outs=[False] * 4 + [pl.ANY],
        scratch=[pltpu.VMEM((4, 4, 16, wide), BF), pltpu.VMEM((4, 64, 384), F32), pltpu.SemaphoreType.DMA((4,)), pltpu.SemaphoreType.DMA],
        limit=12,
    )
    return partial, rows


def act_kernel(own, r1, r2, r3, _, __, hidden):
    total = [own[at] + r1[at].astype(F32) + r2[at].astype(F32) + r3[at].astype(F32) for at in range(2)]
    positive = jnp.maximum(total[0], 0.0)
    hidden[0] = (positive * positive).astype(BF)
    hidden[1] = (2.0 * total[1] * positive).astype(BF)


def back_kernel(p0, p1, p2, p3, weights, o0, o1, o2, o3, slots):
    hidden, wide = weights.shape
    y = lax.axis_index("y")
    for k, part in zip(NEAR_FIRST, (p0, p1, p2, p3)):
        slots[jnp.bitwise_xor(y, k)] = part[1]
    step = 768
    for n in range(0, wide, step):
        out = jnp.dot(slots[...].reshape(256, hidden), weights[:, n : n + step], preferred_element_type=F32).astype(BF)
        for k, ref in enumerate((o0, o1, o2, o3)):
            ref[:, n : n + step] = out[64 * k : 64 * k + 64]


def turn_kernel(p0, p1, p2, p3, _, keep, send, slots):
    hid = keep.shape[1]
    y = lax.axis_index("y")
    for k, part in zip(NEAR_FIRST, (p0, p1, p2, p3)):
        slots[jnp.bitwise_xor(y, k)] = part[...]
    for at in range(2):
        turned = slots[:, at].reshape(256, 2 * hid).T
        keep[at] = turned[:hid]
        send[at] = turned[hid:]


def weights_kernel(keep, came, i_own, i_oth, g_own, g_oth, up, down, up_block, down_block, sems):
    hid, wide = up_block.shape
    step = 768
    copies = []
    for at, (own, oth, block, out) in enumerate(((g_own, g_oth, down_block, down), (i_own, i_oth, up_block, up))):
        for i, n in enumerate(range(0, wide, step)):
            cols = pl.ds(n, step)
            total = jnp.dot(keep[at], own[:, :, :, cols].reshape(256, step), preferred_element_type=F32)
            total += jnp.dot(came[at], oth[:, :, :, cols].reshape(256, step), preferred_element_type=F32)
            block[:, cols] = total.astype(BF)
            copies.append(pltpu.make_async_copy(block.at[:, cols], out.at[:, cols], sems.at[at, i]))
            copies[-1].start()
    for copy in copies:
        copy.wait()


def add_kernel(*refs, parts):
    total = refs[0][...].astype(F32)
    for ref in refs[1:parts]:
        total = total + ref[...].astype(F32)
    at = 0
    for out in refs[parts + 1 :]:
        out[...] = total[at : at + out.shape[0]].astype(BF)
        at += out.shape[0]


def add(parts, pieces, after):
    rows, wide = parts[0].shape
    return call(
        functools.partial(add_kernel, parts=len(parts)), "add", [struct(rows // pieces, wide)] * pieces, (*parts, after),
        ins=[False] * len(parts) + [True],
    )


def shards(x_code, x_scale, g_code, g_scale, up_weight, down_weight):
    hid, wide = up_weight.shape
    (mine,) = call(
        dequant_kernel, "dequant", [struct(16, wide)], in_hbm(x_code, x_scale, g_code, g_scale), ins=[True] * 4,
        scratch=[pltpu.VMEM(a.shape, a.dtype) for a in (x_code, x_scale, g_code, g_scale)] + [pltpu.SemaphoreType.DMA((4,))],
    )
    oth = on_cores(mine, ((1, 0, 0), (0, 1, -1)))
    own = on_cores(mine, ((0, 0, 0), (1, 1, -1)))
    up_other = other_core(up_weight)
    down_other = other_core(down_weight)
    inputs, grads = call(regroup_kernel, "regroup", [struct(16, wide)] * 2, (own, oth, up_other), ins=[False] * 2 + [True])
    row, near = call(
        first_kernel, "first", [struct(4, 16, wide), struct(2, 16, wide)],
        (*exchange([inputs] * 4, "x"), grads, z_shift(grads, 1, -1), down_other), ins=[False] * 6 + [True],
    )
    pair, column = call(
        second_kernel, "second", [struct(2, 4, 16, wide), struct(4, 16, wide)], (row, z_shift(row, 1, -1), near, z_shift(near, 2, -2))
    )
    far = z_shift(pair, 2, -2)
    g_parts = exchange([column] * 4, "x")
    up_both, down_both = call(
        join_kernel, "join", [struct(2 * hid, wide)] * 2, (*in_hbm(up_weight, up_other, down_weight, down_other), column),
        ins=[True] * 5, outs=[pl.ANY] * 2, scratch=[pltpu.SemaphoreType.DMA((4,))], limit=1,
    )
    partial, i_rows = pre((pair, far), up_both, 0, ())
    partial, g_rows = pre(g_parts, down_both, 1, partial)
    i_other = other_core(i_rows)
    g_other = other_core(g_rows)
    (hidden,) = call(
        act_kernel, "act", [struct(2, 64, 2 * hid)], (*exchange(partial, "y"), *in_hbm(i_other, g_other)),
        ins=[False] * 4 + [True] * 2,
    )
    hidden = exchange([hidden] * 4, "y")
    pieces = call(
        back_kernel, "back", [struct(64, wide)] * 4, (*hidden, in_vmem(up_both)), scratch=[pltpu.VMEM((4, 64, 2 * hid), BF)], limit=12
    )
    keep, send = call(
        turn_kernel, "turn", [struct(2, hid, 256)] * 2, (*hidden, pieces[0]), ins=[False] * 4 + [True],
        scratch=[pltpu.VMEM((4, 2, 64, 2 * hid), BF)],
    )
    grad_up, grad_down = call(
        weights_kernel, "weight_grads", [struct(hid, wide)] * 2, (keep, other_core(send), i_rows, i_other, g_rows, g_other),
        outs=[pltpu.HBM] * 2, scratch=[pltpu.VMEM((hid, wide), BF), pltpu.VMEM((hid, wide), BF), pltpu.SemaphoreType.DMA((2, 3))],
        limit=24,
    )
    blocks = add(exchange(pieces, "x"), 4, pieces[0])
    home = [z_shift(block, -t, 1 + t) for t, block in enumerate(blocks)]
    half, other_half = add(home, 2, *in_hbm(grad_up))
    (grad_input,) = add([half, other_core(other_half)], 1, half)
    return (grad_input, grad_up, grad_down)


def solution(mesh):
    fine = Mesh(mesh.devices.reshape(4, 2, 4, 4, 2), ("zl", "core", "y", "x", "zh"))
    spec = P(("zl", "core", "x", "zh"), "y")
    return jax.shard_map(shards, mesh=fine, in_specs=(spec,) * 6, out_specs=(spec,) * 3, check_vma=False)
```

time: 883 us -> 129 us (0.15)
  waiting for transfers between devices: 838 us -> 60.7 us
  starting transfers between devices: 0.16 us -> 48.4 us
  matrix products: 23.3 us -> 0 us
  Pallas kernels: 0 us -> 17.4 us
  between operations: 13.8 us -> 0.86 us
    reduce_scatter x1 -> x0, waiting for transfers between devices: 395 us -> none  [shards(): lax.psum_scatter(jnp.dot(grad_pre, up_weight, preferred_element_type=jnp....]
    all_gather x2 -> x0, waiting for transfers between devices: 370 us -> none  [the longest x1 185 us: shards(): grads = lax.all_gather(local_grads, ('depth', 'col'), axis=0, tiled=True)]
    psum x1 -> x0, waiting for transfers between devices: 72.6 us -> none  [shards(): preact, grad_act = lax.psum((pre_part, act_part), 'row')]
    ppermute x0 -> x31, waiting for transfers between devices: none -> 60.7 us  [the longest x15 42.1 us: xor_shift(): return lax.ppermute(array, axis, [(i, i ^ k) for i in range(4)])]
    ppermute x0 -> x31, starting transfers between devices: none -> 48.4 us  [the longest x10 21.4 us: on_cores(): return lax.ppermute(array, ('zl', 'core', 'zh'), pairs)]
    dot_general x7 -> x0, matrix products: 23.3 us -> none  [the longest x1 5.03 us: shards(): act_part = jnp.dot(grads, down_weight.T, preferred_element_type=jnp.float32)]
    pallas_call x0 -> x14, Pallas kernels: none -> 17.4 us  [call(): pl.pallas_call(kernel, out_shape=tuple(out), in_specs=[any_spec() if a el...]
  transfers between devices with their start and end apart: 4 -> 31, of which waited for: 4 -> 18; matrix products, arithmetic and copies ran while one was open for 2% -> 0% of each run, Pallas kernels for 0% -> 9%
where the time goes in v2:
time: 129 us
  waiting for transfers between devices  60.7 us (47%)
  starting transfers between devices  48.4 us (38%)
  Pallas kernels  17.4 us (13%)
  local copies, waits for them, and re-layouts  1.41 us (1%)
    ppermute x15, waiting for transfers between devices, xor_shift(): return lax.ppermute(array, axis, [(i, i ^ k) for i in range(4)])  42.1 us
    ppermute x10, starting transfers between devices, on_cores(): return lax.ppermute(array, ('zl', 'core', 'zh'), pairs)  21.4 us
    ppermute x15, starting transfers between devices, xor_shift(): return lax.ppermute(array, axis, [(i, i ^ k) for i in range(4)])  17.8 us
    pallas_call x14, Pallas kernels, call(): pl.pallas_call(kernel, out_shape=tuple(out), in_specs=[any_spec() if a el...  17.4 us
    ppermute x10, waiting for transfers between devices, on_cores(): return lax.ppermute(array, ('zl', 'core', 'zh'), pairs)  17.4 us
    ppermute x6, starting transfers between devices, other_core(): return lax.ppermute(array, 'core', [(0, 1), (1, 0)])  9.19 us
  transfers between devices with their start and end apart: 31, of which 18 were waited for; matrix products, arithmetic and copies ran while one was open for 0% of the time, Pallas kernels for 9%

profile of v2, /device:TPU:1, one launch (start us, length us, event | category | flops | bytes accessed | tf_op | source)
XLA Modules:
  0.0 128.8 jit_solution(9834732995278143067)
XLA Ops:
  0.6 3.3 %collective-permute-start.2 = (bf16[576,2304]{1,0:T(8,128)(2,1)}, bf16[576,2304]{1,0:T(8,128)(2,1)S(1)}, u32[]{:S(2)}, u32[]{:S(2)}) collective-permute-start(bf16[576,2304]{1,0:T(8,128)(2,1)} %up_own.1), channel_id=1, source_target_pairs={{0,32},{32,0},{1,33},{33,1},{2,34},{34,2},{3,35},{35,3},{4,36},{36... | collective-permute-start | bytes 7962632 | tf_op jit(solution)/shard_map/ppermute | solution.py:40
  5.1 5.7 %collective-permute-start = (bf16[16,2304]{1,0:T(8,128)(2,1)S(1)}, bf16[16,2304]{1,0:T(8,128)(2,1)S(1)}, u32[]{:S(2)}, u32[]{:S(2)}) collective-permute-start(bf16[16,2304]{1,0:T(8,128)(2,1)S(1)} %dequant.1), channel_id=1, source_target_pairs={{0,0},{32,225},{64,64},{96,32},{128,128},{160,96},{192,192},{224,1... | collective-permute-start | bytes 221192 | tf_op jit(solution)/shard_map/ppermute | solution.py:24
  12.2 2.4 %collective-permute-done.1.oth = bf16[16,2304]{1,0:T(8,128)(2,1)S(1)} collective-permute-done((bf16[16,2304]{1,0:T(8,128)(2,1)S(1)}, bf16[16,2304]{1,0:T(8,128)(2,1)S(1)}, u32[]{:S(2)}, u32[]{:S(2)}) %collective-permute-start.1) | collective-permute-done | bytes 73760 | tf_op jit(solution)/shard_map/ppermute | solution.py:24
  15.9 1.8 %collective-permute-start.4 = (bf16[16,2304]{1,0:T(8,128)(2,1)S(1)}, bf16[16,2304]{1,0:T(8,128)(2,1)S(1)}, u32[]{:S(2)}, u32[]{:S(2)}) collective-permute-start(bf16[16,2304]{1,0:T(8,128)(2,1)S(1)} %get-tuple-element.35.x0), channel_id=1, source_target_pairs={{0,6},{2,4},{4,2},{6,0},{1,7},{3,5},{5,3},{7,1},{8,14},{10,12},{12... | collective-permute-start | bytes 221192 | tf_op jit(solution)/shard_map/ppermute | solution.py:32
  18.4 1.9 %collective-permute-start.6 = (bf16[16,2304]{1,0:T(8,128)(2,1)S(1)}, bf16[16,2304]{1,0:T(8,128)(2,1)S(1)}, u32[]{:S(2)}, u32[]{:S(2)}) collective-permute-start(bf16[16,2304]{1,0:T(8,128)(2,1)S(1)} %get-tuple-element.36.g0), channel_id=1, source_target_pairs={{0,64},{32,225},{64,128},{96,32},{128,192},{160,96},{192,1},{224,1... | collective-permute-start | bytes 221192 | tf_op jit(solution)/shard_map/ppermute | solution.py:24
  21.4 1.9 %collective-permute-done.5.x3 = bf16[16,2304]{1,0:T(8,128)(2,1)S(1)} collective-permute-done((bf16[16,2304]{1,0:T(8,128)(2,1)S(1)}, bf16[16,2304]{1,0:T(8,128)(2,1)S(1)}, u32[]{:S(2)}, u32[]{:S(2)}) %collective-permute-start.5) | collective-permute-done | bytes 73760 | tf_op jit(solution)/shard_map/ppermute | solution.py:32
  25.0 6.4 %collective-permute-done.9.near1 = bf16[2,16,2304]{2,1,0:T(8,128)(2,1)S(1)} collective-permute-done((bf16[2,16,2304]{2,1,0:T(8,128)(2,1)S(1)}, bf16[2,16,2304]{2,1,0:T(8,128)(2,1)S(1)}, u32[]{:S(2)}, u32[]{:S(2)}) %collective-permute-start.9) | collective-permute-done | bytes 147488 | tf_op jit(solution)/shard_map/ppermute | solution.py:24
  31.5 4.4 %collective-permute-start.13 = (bf16[2,4,16,2304]{3,2,1,0:T(8,128)(2,1)S(1)}, bf16[2,4,16,2304]{3,2,1,0:T(8,128)(2,1)S(1)}, u32[]{:S(2)}, u32[]{:S(2)}) collective-permute-start(bf16[2,4,16,2304]{3,2,1,0:T(8,128)(2,1)S(1)} %get-tuple-element.41.refs_0_), channel_id=1, source_target_pairs={{0,128},{32,161},{64,192},{96,225},{128,1},{160,32},{192,65},{224,... | collective-permute-start | bytes 1769480 | tf_op jit(solution)/shard_map/ppermute | solution.py:24
  36.6 1.8 %collective-permute-start.11 = (bf16[4,16,2304]{2,1,0:T(8,128)(2,1)S(1)}, bf16[4,16,2304]{2,1,0:T(8,128)(2,1)S(1)}, u32[]{:S(2)}, u32[]{:S(2)}) collective-permute-start(bf16[4,16,2304]{2,1,0:T(8,128)(2,1)S(1)} %get-tuple-element.39._.refs_0_), channel_id=1, source_target_pairs={{0,6},{2,4},{4,2},{6,0},{1,7},{3,5},{5,3},{7,1},{8,14},{10,12},{12... | collective-permute-start | bytes 884744 | tf_op jit(solution)/shard_map/ppermute | solution.py:32
  39.1 4.1 %join.1 = (bf16[1152,2304]{1,0:T(8,128)(2,1)S(1)}, bf16[1152,2304]{1,0:T(8,128)(2,1)S(1)}) custom-call(bf16[576,2304]{1,0:T(8,128)(2,1)} %up_own.1, bf16[576,2304]{1,0:T(8,128)(2,1)} %copy-done, bf16[576,2304]{1,0:T(8,128)(2,1)} %down_own.1, bf16[576,2304]{1,0:T(8,128)(2,1)} %copy-done.1, bf16[4,16,2304]{2,1,0:T(8,128)(2,1)S(1)} %get-tuple-element.39._.refs_0_), custom_call_target="tpu_custom_call" | custom-call | flops 1 | bytes 1 | tf_op jit(solution)/shard_map/join/pallas_call | solution.py:62
  43.2 4.6 %collective-permute-done.13.refs_1_ = bf16[2,4,16,2304]{3,2,1,0:T(8,128)(2,1)S(1)} collective-permute-done((bf16[2,4,16,2304]{3,2,1,0:T(8,128)(2,1)S(1)}, bf16[2,4,16,2304]{3,2,1,0:T(8,128)(2,1)S(1)}, u32[]{:S(2)}, u32[]{:S(2)}) %collective-permute-start.13) | collective-permute-done | bytes 589856 | tf_op jit(solution)/shard_map/ppermute | solution.py:24
  47.8 2.5 %pre.2 = (f32[2,64,1152]{2,1,0:T(8,128)S(1)}, bf16[2,64,1152]{2,1,0:T(8,128)(2,1)S(1)}, bf16[2,64,1152]{2,1,0:T(8,128)(2,1)S(1)}, bf16[2,64,1152]{2,1,0:T(8,128)(2,1)S(1)}, bf16[4,4,16,2304]{3,2,1,0:T(8,128)(2,1)S(1)}) custom-call(bf16[2,4,16,2304]{3,2,1,0:T(8,128)(2,1)S(1)} %get-tuple-element.41.refs_0_, ...), custom_call_target="tpu_custom_call" | custom-call | flops 1 | bytes 1 | tf_op jit(solution)/shard_map/pre/pallas_call | solution.py:62
  51.8 2.7 %pre.3 = (f32[2,64,1152]{2,1,0:T(8,128)S(1)}, bf16[2,64,1152]{2,1,0:T(8,128)(2,1)S(1)}, bf16[2,64,1152]{2,1,0:T(8,128)(2,1)S(1)}, bf16[2,64,1152]{2,1,0:T(8,128)(2,1)S(1)}, bf16[4,4,16,2304]{3,2,1,0:T(8,128)(2,1)S(1)}) custom-call(bf16[4,16,2304]{2,1,0:T(8,128)(2,1)S(1)} %get-tuple-element.39._.refs_0_, ...), custom_call_target="tpu_custom_call" | custom-call | flops 1 | bytes 1 | tf_op jit(solution)/shard_map/pre/pallas_call | solution.py:62
  54.5 3.0 %collective-permute-start.18 = (bf16[4,4,16,2304]{3,2,1,0:T(8,128)(2,1)S(1)}, bf16[4,4,16,2304]{3,2,1,0:T(8,128)(2,1)S(1)}, u32[]{:S(2)}, u32[]{:S(2)}) collective-permute-start(bf16[4,4,16,2304]{3,2,1,0:T(8,128)(2,1)S(1)} %get-tuple-element.52.g_own), channel_id=1, source_target_pairs={{0,32},{32,0},{1,33},{33,1},{2,34},{34,2},{3,35},{35,3},{4,36},{36... | collective-permute-start | bytes 3538952 | tf_op jit(solution)/shard_map/ppermute | solution.py:40
  58.8 1.9 %collective-permute-start.15 = (bf16[2,64,1152]{2,1,0:T(8,128)(2,1)S(1)}, bf16[2,64,1152]{2,1,0:T(8,128)(2,1)S(1)}, u32[]{:S(2)}, u32[]{:S(2)}) collective-permute-start(bf16[2,64,1152]{2,1,0:T(8,128)(2,1)S(1)} %get-tuple-element.49), channel_id=1, source_target_pairs={{0,24},{8,16},{16,8},{24,0},{1,25},{9,17},{17,9},{25,1},{2,26},{10... | collective-permute-start | bytes 884744 | tf_op jit(solution)/shard_map/ppermute | solution.py:32
  61.6 4.1 %collective-permute-done.14.r1 = bf16[2,64,1152]{2,1,0:T(8,128)(2,1)S(1)} collective-permute-done((bf16[2,64,1152]{2,1,0:T(8,128)(2,1)S(1)}, bf16[2,64,1152]{2,1,0:T(8,128)(2,1)S(1)}, u32[]{:S(2)}, u32[]{:S(2)}) %collective-permute-start.14) | collective-permute-done | bytes 294944 | tf_op jit(solution)/shard_map/ppermute | solution.py:32
  65.7 6.9 %collective-permute-done.15.r2 = bf16[2,64,1152]{2,1,0:T(8,128)(2,1)S(1)} collective-permute-done((bf16[2,64,1152]{2,1,0:T(8,128)(2,1)S(1)}, bf16[2,64,1152]{2,1,0:T(8,128)(2,1)S(1)}, u32[]{:S(2)}, u32[]{:S(2)}) %collective-permute-start.15) | collective-permute-done | bytes 294944 | tf_op jit(solution)/shard_map/ppermute | solution.py:32
  72.6 2.0 %collective-permute-done.16.r3 = bf16[2,64,1152]{2,1,0:T(8,128)(2,1)S(1)} collective-permute-done((bf16[2,64,1152]{2,1,0:T(8,128)(2,1)S(1)}, bf16[2,64,1152]{2,1,0:T(8,128)(2,1)S(1)}, u32[]{:S(2)}, u32[]{:S(2)}) %collective-permute-start.16) | collective-permute-done | bytes 294944 | tf_op jit(solution)/shard_map/ppermute | solution.py:32
  79.5 4.0 %collective-permute-done.19.p1 = bf16[2,64,1152]{2,1,0:T(8,128)(2,1)S(1)} collective-permute-done((bf16[2,64,1152]{2,1,0:T(8,128)(2,1)S(1)}, bf16[2,64,1152]{2,1,0:T(8,128)(2,1)S(1)}, u32[]{:S(2)}, u32[]{:S(2)}) %collective-permute-start.19) | collective-permute-done | bytes 294944 | tf_op jit(solution)/shard_map/ppermute | solution.py:32
  83.5 1.7 %collective-permute-done.20.p2 = bf16[2,64,1152]{2,1,0:T(8,128)(2,1)S(1)} collective-permute-done((bf16[2,64,1152]{2,1,0:T(8,128)(2,1)S(1)}, bf16[2,64,1152]{2,1,0:T(8,128)(2,1)S(1)}, u32[]{:S(2)}, u32[]{:S(2)}) %collective-permute-start.20) | collective-permute-done | bytes 294944 | tf_op jit(solution)/shard_map/ppermute | solution.py:32
  85.2 5.6 %collective-permute-done.21.p3 = bf16[2,64,1152]{2,1,0:T(8,128)(2,1)S(1)} collective-permute-done((bf16[2,64,1152]{2,1,0:T(8,128)(2,1)S(1)}, bf16[2,64,1152]{2,1,0:T(8,128)(2,1)S(1)}, u32[]{:S(2)}, u32[]{:S(2)}) %collective-permute-start.21) | collective-permute-done | bytes 294944 | tf_op jit(solution)/shard_map/ppermute | solution.py:32
  90.8 1.7 %back.1 = (bf16[64,2304]{1,0:T(8,128)(2,1)S(1)}, bf16[64,2304]{1,0:T(8,128)(2,1)S(1)}, bf16[64,2304]{1,0:T(8,128)(2,1)S(1)}, bf16[64,2304]{1,0:T(8,128)(2,1)S(1)}) custom-call(bf16[2,64,1152]{2,1,0:T(8,128)(2,1)S(1)} %act.1.p0, bf16[2,64,1152]{2,1,0:T(8,128)(2,1)S(1)} %collective-permute-done.19.p1, bf16[2,64,1152]{2,1,0:T(8,128)(2,1)S(1)} %collective-permute-done.20.p2, ...), custom_call_target="tpu_custom_call" | custom-call | flops 1 | bytes 1 | tf_op jit(solution)/shard_map/back/pallas_call | solution.py:62
  93.0 2.6 %collective-permute-start.29 = (bf16[2,576,256]{2,1,0:T(8,128)(2,1)S(1)}, bf16[2,576,256]{2,1,0:T(8,128)(2,1)S(1)}, u32[]{:S(2)}, u32[]{:S(2)}) collective-permute-start(bf16[2,576,256]{2,1,0:T(8,128)(2,1)S(1)} %get-tuple-element.62), channel_id=1, source_target_pairs={{0,32},{32,0},{1,33},{33,1},{2,34},{34,2},{3,35},{35,3},{4,36},{36... | collective-permute-start | bytes 1769480 | tf_op jit(solution)/shard_map/ppermute | solution.py:40
  96.5 1.8 %collective-permute-start.23 = (bf16[64,2304]{1,0:T(8,128)(2,1)S(1)}, bf16[64,2304]{1,0:T(8,128)(2,1)S(1)}, u32[]{:S(2)}, u32[]{:S(2)}) collective-permute-start(bf16[64,2304]{1,0:T(8,128)(2,1)S(1)} %get-tuple-element.55), channel_id=1, source_target_pairs={{0,6},{2,4},{4,2},{6,0},{1,7},{3,5},{5,3},{7,1},{8,14},{10,12},{12... | collective-permute-start | bytes 884744 | tf_op jit(solution)/shard_map/ppermute | solution.py:32
  99.0 5.2 %collective-permute-done.22.refs_1_ = bf16[64,2304]{1,0:T(8,128)(2,1)S(1)} collective-permute-done((bf16[64,2304]{1,0:T(8,128)(2,1)S(1)}, bf16[64,2304]{1,0:T(8,128)(2,1)S(1)}, u32[]{:S(2)}, u32[]{:S(2)}) %collective-permute-start.22) | collective-permute-done | bytes 294944 | tf_op jit(solution)/shard_map/ppermute | solution.py:32
  104.2 6.4 %collective-permute-done.23.refs_2_ = bf16[64,2304]{1,0:T(8,128)(2,1)S(1)} collective-permute-done((bf16[64,2304]{1,0:T(8,128)(2,1)S(1)}, bf16[64,2304]{1,0:T(8,128)(2,1)S(1)}, u32[]{:S(2)}, u32[]{:S(2)}) %collective-permute-start.23) | collective-permute-done | bytes 294944 | tf_op jit(solution)/shard_map/ppermute | solution.py:32
  110.6 1.9 %collective-permute-done.24.refs_3_ = bf16[64,2304]{1,0:T(8,128)(2,1)S(1)} collective-permute-done((bf16[64,2304]{1,0:T(8,128)(2,1)S(1)}, bf16[64,2304]{1,0:T(8,128)(2,1)S(1)}, u32[]{:S(2)}, u32[]{:S(2)}) %collective-permute-start.24) | collective-permute-done | bytes 294944 | tf_op jit(solution)/shard_map/ppermute | solution.py:32
  112.6 1.9 %collective-permute-start.25 = (bf16[16,2304]{1,0:T(8,128)(2,1)S(1)}, bf16[16,2304]{1,0:T(8,128)(2,1)S(1)}, u32[]{:S(2)}, u32[]{:S(2)}) collective-permute-start(bf16[16,2304]{1,0:T(8,128)(2,1)S(1)} %get-tuple-element.57), channel_id=1, source_target_pairs={{0,0},{32,96},{64,64},{96,160},{128,128},{160,224},{192,192},{224,... | collective-permute-start | bytes 221192 | tf_op jit(solution)/shard_map/ppermute | solution.py:24
  114.6 3.3 %collective-permute-start.27 = (bf16[16,2304]{1,0:T(8,128)(2,1)S(1)}, bf16[16,2304]{1,0:T(8,128)(2,1)S(1)}, u32[]{:S(2)}, u32[]{:S(2)}) collective-permute-start(bf16[16,2304]{1,0:T(8,128)(2,1)S(1)} %get-tuple-element.59), channel_id=1, source_target_pairs={{0,129},{32,224},{64,193},{96,33},{128,0},{160,97},{192,64},{224,1... | collective-permute-start | bytes 221192 | tf_op jit(solution)/shard_map/ppermute | solution.py:24
  117.9 2.5 %collective-permute-start.28 = (bf16[16,2304]{1,0:T(8,128)(2,1)S(1)}, bf16[16,2304]{1,0:T(8,128)(2,1)S(1)}, u32[]{:S(2)}, u32[]{:S(2)}) collective-permute-start(bf16[16,2304]{1,0:T(8,128)(2,1)S(1)} %get-tuple-element.60), channel_id=1, source_target_pairs={{0,65},{32,33},{64,129},{96,97},{128,193},{160,161},{192,0},{224,2... | collective-permute-start | bytes 221192 | tf_op jit(solution)/shard_map/ppermute | solution.py:24
  120.3 3.9 %weight_grads.1 = (bf16[576,2304]{1,0:T(8,128)(2,1)}, bf16[576,2304]{1,0:T(8,128)(2,1)}) custom-call(bf16[2,576,256]{2,1,0:T(8,128)(2,1)S(1)} %get-tuple-element.61.keep, bf16[2,576,256]{2,1,0:T(8,128)(2,1)S(1)} %collective-permute-done.29.came, bf16[4,4,16,2304]{3,2,1,0:T(8,128)(2,1)S(1)} %get-tuple-element.51.i_own, ...), custom_call_target="tpu_custom_call" | custom-call | flops 1 | bytes 1 | tf_op jit(solution)/shard_map/weight_grads/pallas_call | solution.py:62
  124.3 2.6 %collective-permute-done.28.refs_3_ = bf16[16,2304]{1,0:T(8,128)(2,1)S(1)} collective-permute-done((bf16[16,2304]{1,0:T(8,128)(2,1)S(1)}, bf16[16,2304]{1,0:T(8,128)(2,1)S(1)}, u32[]{:S(2)}, u32[]{:S(2)}) %collective-permute-start.28) | collective-permute-done | bytes 73760 | tf_op jit(solution)/shard_map/ppermute | solution.py:24
  (56 shorter events, 21.4 us)
Async XLA Ops:
  0.6 14.0 %collective-permute-start.2 = (bf16[576,2304]{1,0:T(8,128)(2,1)}, bf16[576,2304]{1,0:T(8,128)(2,1)S(1)}, u32[]{:S(2)}, u32[]{:S(2)}) collective-permute-start(bf16[576,2304]{1,0:T(8,128)(2,1)} %up_own.1), channel_id=1, source_target_pairs={{0,32},{32,0},{1,33},{33,1},{2,34},{34,2},{3,35},{35,3},{4,36},{36... | collective-permute-start | bytes 7962632 | tf_op jit(solution)/shard_map/ppermute | solution.py:40
  4.0 16.4 %collective-permute-start.7 = (bf16[576,2304]{1,0:T(8,128)(2,1)}, bf16[576,2304]{1,0:T(8,128)(2,1)S(1)}, u32[]{:S(2)}, u32[]{:S(2)}) collective-permute-start(bf16[576,2304]{1,0:T(8,128)(2,1)} %down_own.1), channel_id=1, source_target_pairs={{0,32},{32,0},{1,33},{33,1},{2,34},{34,2},{3,35},{35,3},{4,36},{36... | collective-permute-start | bytes 7962632 | tf_op jit(solution)/shard_map/ppermute | solution.py:40
  5.1 7.1 %collective-permute-start = (bf16[16,2304]{1,0:T(8,128)(2,1)S(1)}, bf16[16,2304]{1,0:T(8,128)(2,1)S(1)}, u32[]{:S(2)}, u32[]{:S(2)}) collective-permute-start(bf16[16,2304]{1,0:T(8,128)(2,1)S(1)} %dequant.1), channel_id=1, source_target_pairs={{0,0},{32,225},{64,64},{96,32},{128,128},{160,96},{192,192},{224,1... | collective-permute-start | bytes 221192 | tf_op jit(solution)/shard_map/ppermute | solution.py:24
  10.8 3.8 %collective-permute-start.1 = (bf16[16,2304]{1,0:T(8,128)(2,1)S(1)}, bf16[16,2304]{1,0:T(8,128)(2,1)S(1)}, u32[]{:S(2)}, u32[]{:S(2)}) collective-permute-start(bf16[16,2304]{1,0:T(8,128)(2,1)S(1)} %dequant.1), channel_id=1, source_target_pairs={{32,0},{0,225},{96,64},{64,32},{160,128},{128,96},{224,192},{192,1... | collective-permute-start | bytes 221192 | tf_op jit(solution)/shard_map/ppermute | solution.py:24
  14.6 5.7 %collective-permute-start.3 = (bf16[16,2304]{1,0:T(8,128)(2,1)S(1)}, bf16[16,2304]{1,0:T(8,128)(2,1)S(1)}, u32[]{:S(2)}, u32[]{:S(2)}) collective-permute-start(bf16[16,2304]{1,0:T(8,128)(2,1)S(1)} %get-tuple-element.35.x0), channel_id=1, source_target_pairs={{0,2},{2,0},{4,6},{6,4},{1,3},{3,1},{5,7},{7,5},{8,10},{10,8},{12,... | collective-permute-start | bytes 221192 | tf_op jit(solution)/shard_map/ppermute | solution.py:32
  15.9 5.4 %collective-permute-start.4 = (bf16[16,2304]{1,0:T(8,128)(2,1)S(1)}, bf16[16,2304]{1,0:T(8,128)(2,1)S(1)}, u32[]{:S(2)}, u32[]{:S(2)}) collective-permute-start(bf16[16,2304]{1,0:T(8,128)(2,1)S(1)} %get-tuple-element.35.x0), channel_id=1, source_target_pairs={{0,6},{2,4},{4,2},{6,0},{1,7},{3,5},{5,3},{7,1},{8,14},{10,12},{12... | collective-permute-start | bytes 221192 | tf_op jit(solution)/shard_map/ppermute | solution.py:32
  17.7 5.5 %collective-permute-start.5 = (bf16[16,2304]{1,0:T(8,128)(2,1)S(1)}, bf16[16,2304]{1,0:T(8,128)(2,1)S(1)}, u32[]{:S(2)}, u32[]{:S(2)}) collective-permute-start(bf16[16,2304]{1,0:T(8,128)(2,1)S(1)} %get-tuple-element.35.x0), channel_id=1, source_target_pairs={{0,4},{2,6},{4,0},{6,2},{1,5},{3,7},{5,1},{7,3},{8,12},{10,14},{12... | collective-permute-start | bytes 221192 | tf_op jit(solution)/shard_map/ppermute | solution.py:32
  18.4 4.9 %collective-permute-start.6 = (bf16[16,2304]{1,0:T(8,128)(2,1)S(1)}, bf16[16,2304]{1,0:T(8,128)(2,1)S(1)}, u32[]{:S(2)}, u32[]{:S(2)}) collective-permute-start(bf16[16,2304]{1,0:T(8,128)(2,1)S(1)} %get-tuple-element.36.g0), channel_id=1, source_target_pairs={{0,64},{32,225},{64,128},{96,32},{128,192},{160,96},{192,1},{224,1... | collective-permute-start | bytes 221192 | tf_op jit(solution)/shard_map/ppermute | solution.py:24
  23.3 8.1 %collective-permute-start.8 = (bf16[4,16,2304]{2,1,0:T(8,128)(2,1)S(1)}, bf16[4,16,2304]{2,1,0:T(8,128)(2,1)S(1)}, u32[]{:S(2)}, u32[]{:S(2)}) collective-permute-start(bf16[4,16,2304]{2,1,0:T(8,128)(2,1)S(1)} %get-tuple-element.37.row), channel_id=1, source_target_pairs={{0,64},{32,225},{64,128},{96,32},{128,192},{160,96},{192,1},{224,1... | collective-permute-start | bytes 884744 | tf_op jit(solution)/shard_map/ppermute | solution.py:24
  24.8 6.5 %collective-permute-start.9 = (bf16[2,16,2304]{2,1,0:T(8,128)(2,1)S(1)}, bf16[2,16,2304]{2,1,0:T(8,128)(2,1)S(1)}, u32[]{:S(2)}, u32[]{:S(2)}) collective-permute-start(bf16[2,16,2304]{2,1,0:T(8,128)(2,1)S(1)} %get-tuple-element.38.near), channel_id=1, source_target_pairs={{0,128},{32,161},{64,192},{96,225},{128,1},{160,32},{192,65},{224,... | collective-permute-start | bytes 442376 | tf_op jit(solution)/shard_map/ppermute | solution.py:24
  31.5 16.4 %collective-permute-start.13 = (bf16[2,4,16,2304]{3,2,1,0:T(8,128)(2,1)S(1)}, bf16[2,4,16,2304]{3,2,1,0:T(8,128)(2,1)S(1)}, u32[]{:S(2)}, u32[]{:S(2)}) collective-permute-start(bf16[2,4,16,2304]{3,2,1,0:T(8,128)(2,1)S(1)} %get-tuple-element.41.refs_0_), channel_id=1, source_target_pairs={{0,128},{32,161},{64,192},{96,225},{128,1},{160,32},{192,65},{224,... | collective-permute-start | bytes 1769480 | tf_op jit(solution)/shard_map/ppermute | solution.py:24
  35.8 14.5 %collective-permute-start.10 = (bf16[4,16,2304]{2,1,0:T(8,128)(2,1)S(1)}, bf16[4,16,2304]{2,1,0:T(8,128)(2,1)S(1)}, u32[]{:S(2)}, u32[]{:S(2)}) collective-permute-start(bf16[4,16,2304]{2,1,0:T(8,128)(2,1)S(1)} %get-tuple-element.39._.refs_0_), channel_id=1, source_target_pairs={{0,2},{2,0},{4,6},{6,4},{1,3},{3,1},{5,7},{7,5},{8,10},{10,8},{12,... | collective-permute-start | bytes 884744 | tf_op jit(solution)/shard_map/ppermute | solution.py:32
  36.6 15.2 %collective-permute-start.11 = (bf16[4,16,2304]{2,1,0:T(8,128)(2,1)S(1)}, bf16[4,16,2304]{2,1,0:T(8,128)(2,1)S(1)}, u32[]{:S(2)}, u32[]{:S(2)}) collective-permute-start(bf16[4,16,2304]{2,1,0:T(8,128)(2,1)S(1)} %get-tuple-element.39._.refs_0_), channel_id=1, source_target_pairs={{0,6},{2,4},{4,2},{6,0},{1,7},{3,5},{5,3},{7,1},{8,14},{10,12},{12... | collective-permute-start | bytes 884744 | tf_op jit(solution)/shard_map/ppermute | solution.py:32
  38.5 13.3 %collective-permute-start.12 = (bf16[4,16,2304]{2,1,0:T(8,128)(2,1)S(1)}, bf16[4,16,2304]{2,1,0:T(8,128)(2,1)S(1)}, u32[]{:S(2)}, u32[]{:S(2)}) collective-permute-start(bf16[4,16,2304]{2,1,0:T(8,128)(2,1)S(1)} %get-tuple-element.39._.refs_0_), channel_id=1, source_target_pairs={{0,4},{2,6},{4,0},{6,2},{1,5},{3,7},{5,1},{7,3},{8,12},{10,14},{12... | collective-permute-start | bytes 884744 | tf_op jit(solution)/shard_map/ppermute | solution.py:32
  54.5 20.1 %collective-permute-start.18 = (bf16[4,4,16,2304]{3,2,1,0:T(8,128)(2,1)S(1)}, bf16[4,4,16,2304]{3,2,1,0:T(8,128)(2,1)S(1)}, u32[]{:S(2)}, u32[]{:S(2)}) collective-permute-start(bf16[4,4,16,2304]{3,2,1,0:T(8,128)(2,1)S(1)} %get-tuple-element.52.g_own), channel_id=1, source_target_pairs={{0,32},{32,0},{1,33},{33,1},{2,34},{34,2},{3,35},{35,3},{4,36},{36... | collective-permute-start | bytes 3538952 | tf_op jit(solution)/shard_map/ppermute | solution.py:40
  57.4 17.2 %collective-permute-start.17 = (bf16[4,4,16,2304]{3,2,1,0:T(8,128)(2,1)S(1)}, bf16[4,4,16,2304]{3,2,1,0:T(8,128)(2,1)S(1)}, u32[]{:S(2)}, u32[]{:S(2)}) collective-permute-start(bf16[4,4,16,2304]{3,2,1,0:T(8,128)(2,1)S(1)} %get-tuple-element.51.i_own), channel_id=1, source_target_pairs={{0,32},{32,0},{1,33},{33,1},{2,34},{34,2},{3,35},{35,3},{4,36},{36... | collective-permute-start | bytes 3538952 | tf_op jit(solution)/shard_map/ppermute | solution.py:40
  57.5 8.2 %collective-permute-start.14 = (bf16[2,64,1152]{2,1,0:T(8,128)(2,1)S(1)}, bf16[2,64,1152]{2,1,0:T(8,128)(2,1)S(1)}, u32[]{:S(2)}, u32[]{:S(2)}) collective-permute-start(bf16[2,64,1152]{2,1,0:T(8,128)(2,1)S(1)} %get-tuple-element.48), channel_id=1, source_target_pairs={{0,8},{8,0},{16,24},{24,16},{1,9},{9,1},{17,25},{25,17},{2,10},{10... | collective-permute-start | bytes 884744 | tf_op jit(solution)/shard_map/ppermute | solution.py:32
  58.8 13.8 %collective-permute-start.15 = (bf16[2,64,1152]{2,1,0:T(8,128)(2,1)S(1)}, bf16[2,64,1152]{2,1,0:T(8,128)(2,1)S(1)}, u32[]{:S(2)}, u32[]{:S(2)}) collective-permute-start(bf16[2,64,1152]{2,1,0:T(8,128)(2,1)S(1)} %get-tuple-element.49), channel_id=1, source_target_pairs={{0,24},{8,16},{16,8},{24,0},{1,25},{9,17},{17,9},{25,1},{2,26},{10... | collective-permute-start | bytes 884744 | tf_op jit(solution)/shard_map/ppermute | solution.py:32
  60.8 13.8 %collective-permute-start.16 = (bf16[2,64,1152]{2,1,0:T(8,128)(2,1)S(1)}, bf16[2,64,1152]{2,1,0:T(8,128)(2,1)S(1)}, u32[]{:S(2)}, u32[]{:S(2)}) collective-permute-start(bf16[2,64,1152]{2,1,0:T(8,128)(2,1)S(1)} %get-tuple-element.50), channel_id=1, source_target_pairs={{0,16},{8,24},{16,0},{24,8},{1,17},{9,25},{17,1},{25,9},{2,18},{10... | collective-permute-start | bytes 884744 | tf_op jit(solution)/shard_map/ppermute | solution.py:32
  76.2 7.3 %collective-permute-start.19 = (bf16[2,64,1152]{2,1,0:T(8,128)(2,1)S(1)}, bf16[2,64,1152]{2,1,0:T(8,128)(2,1)S(1)}, u32[]{:S(2)}, u32[]{:S(2)}) collective-permute-start(bf16[2,64,1152]{2,1,0:T(8,128)(2,1)S(1)} %act.1.p0), channel_id=1, source_target_pairs={{0,8},{8,0},{16,24},{24,16},{1,9},{9,1},{17,25},{25,17},{2,10},{10... | collective-permute-start | bytes 884744 | tf_op jit(solution)/shard_map/ppermute | solution.py:32
  76.3 8.9 %collective-permute-start.20 = (bf16[2,64,1152]{2,1,0:T(8,128)(2,1)S(1)}, bf16[2,64,1152]{2,1,0:T(8,128)(2,1)S(1)}, u32[]{:S(2)}, u32[]{:S(2)}) collective-permute-start(bf16[2,64,1152]{2,1,0:T(8,128)(2,1)S(1)} %act.1.p0), channel_id=1, source_target_pairs={{0,24},{8,16},{16,8},{24,0},{1,25},{9,17},{17,9},{25,1},{2,26},{10... | collective-permute-start | bytes 884744 | tf_op jit(solution)/shard_map/ppermute | solution.py:32
  77.9 12.9 %collective-permute-start.21 = (bf16[2,64,1152]{2,1,0:T(8,128)(2,1)S(1)}, bf16[2,64,1152]{2,1,0:T(8,128)(2,1)S(1)}, u32[]{:S(2)}, u32[]{:S(2)}) collective-permute-start(bf16[2,64,1152]{2,1,0:T(8,128)(2,1)S(1)} %act.1.p0), channel_id=1, source_target_pairs={{0,16},{8,24},{16,0},{24,8},{1,17},{9,25},{17,1},{25,9},{2,18},{10... | collective-permute-start | bytes 884744 | tf_op jit(solution)/shard_map/ppermute | solution.py:32
  92.5 27.8 %copy-start.3 = (bf16[4,4,16,2304]{3,2,1,0:T(8,128)(2,1)S(1)}, bf16[4,4,16,2304]{3,2,1,0:T(8,128)(2,1)}, u32[]{:S(2)}) copy-start(bf16[4,4,16,2304]{3,2,1,0:T(8,128)(2,1)} %copy-done.2) | copy-start | bytes 3538948
  93.0 27.3 %collective-permute-start.29 = (bf16[2,576,256]{2,1,0:T(8,128)(2,1)S(1)}, bf16[2,576,256]{2,1,0:T(8,128)(2,1)S(1)}, u32[]{:S(2)}, u32[]{:S(2)}) collective-permute-start(bf16[2,576,256]{2,1,0:T(8,128)(2,1)S(1)} %get-tuple-element.62), channel_id=1, source_target_pairs={{0,32},{32,0},{1,33},{33,1},{2,34},{34,2},{3,35},{35,3},{4,36},{36... | collective-permute-start | bytes 1769480 | tf_op jit(solution)/shard_map/ppermute | solution.py:40
  95.6 8.6 %collective-permute-start.22 = (bf16[64,2304]{1,0:T(8,128)(2,1)S(1)}, bf16[64,2304]{1,0:T(8,128)(2,1)S(1)}, u32[]{:S(2)}, u32[]{:S(2)}) collective-permute-start(bf16[64,2304]{1,0:T(8,128)(2,1)S(1)} %get-tuple-element.54), channel_id=1, source_target_pairs={{0,2},{2,0},{4,6},{6,4},{1,3},{3,1},{5,7},{7,5},{8,10},{10,8},{12,... | collective-permute-start | bytes 884744 | tf_op jit(solution)/shard_map/ppermute | solution.py:32
  96.5 14.0 %collective-permute-start.23 = (bf16[64,2304]{1,0:T(8,128)(2,1)S(1)}, bf16[64,2304]{1,0:T(8,128)(2,1)S(1)}, u32[]{:S(2)}, u32[]{:S(2)}) collective-permute-start(bf16[64,2304]{1,0:T(8,128)(2,1)S(1)} %get-tuple-element.55), channel_id=1, source_target_pairs={{0,6},{2,4},{4,2},{6,0},{1,7},{3,5},{5,3},{7,1},{8,14},{10,12},{12... | collective-permute-start | bytes 884744 | tf_op jit(solution)/shard_map/ppermute | solution.py:32
  98.4 14.1 %collective-permute-start.24 = (bf16[64,2304]{1,0:T(8,128)(2,1)S(1)}, bf16[64,2304]{1,0:T(8,128)(2,1)S(1)}, u32[]{:S(2)}, u32[]{:S(2)}) collective-permute-start(bf16[64,2304]{1,0:T(8,128)(2,1)S(1)} %get-tuple-element.56), channel_id=1, source_target_pairs={{0,4},{2,6},{4,0},{6,2},{1,5},{3,7},{5,1},{7,3},{8,12},{10,14},{12... | collective-permute-start | bytes 884744 | tf_op jit(solution)/shard_map/ppermute | solution.py:32
  112.6 11.7 %collective-permute-start.25 = (bf16[16,2304]{1,0:T(8,128)(2,1)S(1)}, bf16[16,2304]{1,0:T(8,128)(2,1)S(1)}, u32[]{:S(2)}, u32[]{:S(2)}) collective-permute-start(bf16[16,2304]{1,0:T(8,128)(2,1)S(1)} %get-tuple-element.57), channel_id=1, source_target_pairs={{0,0},{32,96},{64,64},{96,160},{128,128},{160,224},{192,192},{224,... | collective-permute-start | bytes 221192 | tf_op jit(solution)/shard_map/ppermute | solution.py:24
  114.5 9.7 %collective-permute-start.26 = (bf16[16,2304]{1,0:T(8,128)(2,1)S(1)}, bf16[16,2304]{1,0:T(8,128)(2,1)S(1)}, u32[]{:S(2)}, u32[]{:S(2)}) collective-permute-start(bf16[16,2304]{1,0:T(8,128)(2,1)S(1)} %get-tuple-element.58), channel_id=1, source_target_pairs={{0,193},{32,160},{64,0},{96,224},{128,64},{160,33},{192,128},{224,... | collective-permute-start | bytes 221192 | tf_op jit(solution)/shard_map/ppermute | solution.py:24
  114.6 9.7 %collective-permute-start.27 = (bf16[16,2304]{1,0:T(8,128)(2,1)S(1)}, bf16[16,2304]{1,0:T(8,128)(2,1)S(1)}, u32[]{:S(2)}, u32[]{:S(2)}) collective-permute-start(bf16[16,2304]{1,0:T(8,128)(2,1)S(1)} %get-tuple-element.59), channel_id=1, source_target_pairs={{0,129},{32,224},{64,193},{96,33},{128,0},{160,97},{192,64},{224,1... | collective-permute-start | bytes 221192 | tf_op jit(solution)/shard_map/ppermute | solution.py:24
  117.9 9.0 %collective-permute-start.28 = (bf16[16,2304]{1,0:T(8,128)(2,1)S(1)}, bf16[16,2304]{1,0:T(8,128)(2,1)S(1)}, u32[]{:S(2)}, u32[]{:S(2)}) collective-permute-start(bf16[16,2304]{1,0:T(8,128)(2,1)S(1)} %get-tuple-element.60), channel_id=1, source_target_pairs={{0,65},{32,33},{64,129},{96,97},{128,193},{160,161},{192,0},{224,2... | collective-permute-start | bytes 221192 | tf_op jit(solution)/shard_map/ppermute | solution.py:24
  126.9 1.3 %collective-permute-start.30 = (bf16[8,2304]{1,0:T(8,128)(2,1)S(1)}, bf16[8,2304]{1,0:T(8,128)(2,1)S(1)}, u32[]{:S(2)}, u32[]{:S(2)}) collective-permute-start(bf16[8,2304]{1,0:T(8,128)(2,1)S(1)} %get-tuple-element.65), channel_id=1, source_target_pairs={{0,32},{32,0},{1,33},{33,1},{2,34},{34,2},{3,35},{35,3},{4,36},{36... | collective-permute-start | bytes 110600 | tf_op jit(solution)/shard_map/ppermute | solution.py:40
  (5 other events, 57.7 us)

commit v3 on v2

--- a/solution.py
+++ b/solution.py
@@ -117,11 +117,10 @@
     near[1] = g1[...]
 
 
-def second_kernel(row, row1, near, near1, pair, column):
+def second_kernel(row, row1, near1, _, __, pair, distant):
     pair[0] = row[...]
     pair[1] = row1[...]
-    column[:2] = near[...]
-    column[2:] = near1[...]
+    distant[...] = near1[...]
 
 
 def join_kernel(up_own, up_oth, down_own, down_oth, _, up, down, sems):
@@ -134,17 +133,19 @@
         copy.wait()
 
 
-def pre_kernel(*refs, at, before):
-    parts, weights, before, refs = refs[: 2 + 2 * at], refs[2 + 2 * at], refs[3 + 2 * at : 3 + 2 * at + before], refs[3 + 2 * at + before :]
+def pre_kernel(*refs, parts, at, before):
+    parts, weights, before, refs = refs[:parts], refs[parts], refs[parts + 1 : parts + 1 + before], refs[parts + 1 + before :]
     outs, rows_out, (rows, slots, sems, out_sem) = refs[:4], refs[4], refs[5:]
     y = lax.axis_index("y")
     copies = []
-    for n in range(4):
-        if at:
-            copies.append(pltpu.make_async_copy(parts[n], rows.at[n], sems.at[n]))
-        else:
+    if at:
+        for n, ref in enumerate(parts):
+            copies.append(pltpu.make_async_copy(ref, rows.at[n % 4, pl.ds(2 * (n // 4), 2)], sems.at[n]))
+    else:
+        for n in range(4):
             copies.append(pltpu.make_async_copy(parts[n // 2].at[n % 2], rows.at[:, n], sems.at[n]))
-        copies[-1].start()
+    for copy in copies:
+        copy.start()
     for done, out in zip(before, outs):
         out[1 - at] = done[1 - at]
     for copy in copies:
@@ -167,27 +168,27 @@
     hidden, wide = weights.shape
     sent = struct(2, 64, hidden)
     *partial, rows = call(
-        functools.partial(pre_kernel, at=at, before=len(before)), "pre",
+        functools.partial(pre_kernel, parts=len(parts), at=at, before=len(before)), "pre",
         [struct(2, 64, hidden, dtype=F32), sent, sent, sent, struct(4, 4, 16, wide)], (*parts, in_vmem(weights), *before),
         ins=[True] * len(parts) + [False] * (1 + len(before)), outs=[False] * 4 + [pl.ANY],
-        scratch=[pltpu.VMEM((4, 4, 16, wide), BF), pltpu.VMEM((4, 64, 384), F32), pltpu.SemaphoreType.DMA((4,)), pltpu.SemaphoreType.DMA],
+        scratch=[pltpu.VMEM((4, 4, 16, wide), BF), pltpu.VMEM((4, 64, 384), F32), pltpu.SemaphoreType.DMA((8,)), pltpu.SemaphoreType.DMA],
         limit=12,
     )
     return partial, rows
 
 
-def act_kernel(own, r1, r2, r3, _, __, hidden):
+def act_kernel(own, r1, r2, r3, _, __, squared, grad_pre):
     total = [own[at] + r1[at].astype(F32) + r2[at].astype(F32) + r3[at].astype(F32) for at in range(2)]
     positive = jnp.maximum(total[0], 0.0)
-    hidden[0] = (positive * positive).astype(BF)
-    hidden[1] = (2.0 * total[1] * positive).astype(BF)
+    squared[...] = (positive * positive).astype(BF)
+    grad_pre[...] = (2.0 * total[1] * positive).astype(BF)
 
 
 def back_kernel(p0, p1, p2, p3, weights, o0, o1, o2, o3, slots):
     hidden, wide = weights.shape
     y = lax.axis_index("y")
     for k, part in zip(NEAR_FIRST, (p0, p1, p2, p3)):
-        slots[jnp.bitwise_xor(y, k)] = part[1]
+        slots[jnp.bitwise_xor(y, k)] = part[...]
     step = 768
     for n in range(0, wide, step):
         out = jnp.dot(slots[...].reshape(256, hidden), weights[:, n : n + step], preferred_element_type=F32).astype(BF)
@@ -195,13 +196,14 @@
             ref[:, n : n + step] = out[64 * k : 64 * k + 64]
 
 
-def turn_kernel(p0, p1, p2, p3, _, keep, send, slots):
+def turn_kernel(*refs):
+    parts, keep, send, slots = refs[:8], refs[9], refs[10], refs[11]
     hid = keep.shape[1]
     y = lax.axis_index("y")
-    for k, part in zip(NEAR_FIRST, (p0, p1, p2, p3)):
-        slots[jnp.bitwise_xor(y, k)] = part[...]
     for at in range(2):
-        turned = slots[:, at].reshape(256, 2 * hid).T
+        for k, part in zip(NEAR_FIRST, parts[4 * at : 4 * at + 4]):
+            slots[at, jnp.bitwise_xor(y, k)] = part[...]
+        turned = slots[at].reshape(256, 2 * hid).T
         keep[at] = turned[:hid]
         send[at] = turned[hid:]
 
@@ -255,38 +257,42 @@
         first_kernel, "first", [struct(4, 16, wide), struct(2, 16, wide)],
         (*exchange([inputs] * 4, "x"), grads, z_shift(grads, 1, -1), down_other), ins=[False] * 6 + [True],
     )
-    pair, column = call(
-        second_kernel, "second", [struct(2, 4, 16, wide), struct(4, 16, wide)], (row, z_shift(row, 1, -1), near, z_shift(near, 2, -2))
+    g_near = exchange([near] * 4, "x")
+    pair, distant = call(
+        second_kernel, "second", [struct(2, 4, 16, wide), struct(2, 16, wide)],
+        (row, z_shift(row, 1, -1), z_shift(near, 2, -2), g_near[1], g_near[2]), ins=[False] * 3 + [True] * 2,
     )
     far = z_shift(pair, 2, -2)
-    g_parts = exchange([column] * 4, "x")
+    g_distant = exchange([distant] * 4, "x")
     up_both, down_both = call(
-        join_kernel, "join", [struct(2 * hid, wide)] * 2, (*in_hbm(up_weight, up_other, down_weight, down_other), column),
+        join_kernel, "join", [struct(2 * hid, wide)] * 2, (*in_hbm(up_weight, up_other, down_weight, down_other), row),
         ins=[True] * 5, outs=[pl.ANY] * 2, scratch=[pltpu.SemaphoreType.DMA((4,))], limit=1,
     )
-    partial, i_rows = pre((pair, far), up_both, 0, ())
-    partial, g_rows = pre(g_parts, down_both, 1, partial)
+    partial, g_rows = pre((*g_near, *g_distant), down_both, 1, ())
+    partial, i_rows = pre((pair, far), up_both, 0, partial)
     i_other = other_core(i_rows)
     g_other = other_core(g_rows)
-    (hidden,) = call(
-        act_kernel, "act", [struct(2, 64, 2 * hid)], (*exchange(partial, "y"), *in_hbm(i_other, g_other)),
+    squared, grad_pre = call(
+        act_kernel, "act", [struct(64, 2 * hid)] * 2, (*exchange(partial, "y"), i_other, g_other),
         ins=[False] * 4 + [True] * 2,
     )
-    hidden = exchange([hidden] * 4, "y")
+    grad_pre = exchange([grad_pre] * 4, "y")
+    squared = exchange([squared] * 4, "y")
     pieces = call(
-        back_kernel, "back", [struct(64, wide)] * 4, (*hidden, in_vmem(up_both)), scratch=[pltpu.VMEM((4, 64, 2 * hid), BF)], limit=12
-    )
+        back_kernel, "back", [struct(64, wide)] * 4, (*grad_pre, in_vmem(up_both)), scratch=[pltpu.VMEM((4, 64, 2 * hid), BF)], limit=12
+    )
+    pieces = exchange(pieces, "x")
+    blocks = add(pieces, 4, pieces[0])
+    home = [z_shift(block, -t, 1 + t) for t, block in enumerate(blocks)]
     keep, send = call(
-        turn_kernel, "turn", [struct(2, hid, 256)] * 2, (*hidden, pieces[0]), ins=[False] * 4 + [True],
-        scratch=[pltpu.VMEM((4, 2, 64, 2 * hid), BF)],
+        turn_kernel, "turn", [struct(2, hid, 256)] * 2, (*squared, *grad_pre, home[0]), ins=[False] * 8 + [True],
+        scratch=[pltpu.VMEM((2, 4, 64, 2 * hid), BF)],
     )
     grad_up, grad_down = call(
         weights_kernel, "weight_grads", [struct(hid, wide)] * 2, (keep, other_core(send), i_rows, i_other, g_rows, g_other),
         outs=[pltpu.HBM] * 2, scratch=[pltpu.VMEM((hid, wide), BF), pltpu.VMEM((hid, wide), BF), pltpu.SemaphoreType.DMA((2, 3))],
         limit=24,
     )
-    blocks = add(exchange(pieces, "x"), 4, pieces[0])
-    home = [z_shift(block, -t, 1 + t) for t, block in enumerate(blocks)]
     half, other_half = add(home, 2, *in_hbm(grad_up))
     (grad_input,) = add([half, other_core(other_half)], 1, half)
     return (grad_input, grad_up, grad_down)

time: 129 us -> 119 us (0.922)
  waiting for transfers between devices: 60.7 us -> 51.4 us
  Pallas kernels: 17.4 us -> 18.8 us
  local copies, waits for them, and re-layouts: 1.41 us -> 0.01 us
    ppermute x15 -> x21, starting transfers between devices: 17.8 us -> 23.6 us  [xor_shift(): return lax.ppermute(array, axis, [(i, i ^ k) for i in range(4)])]
    ppermute x10, waiting for transfers between devices: 17.4 us -> 11.8 us  [on_cores(): return lax.ppermute(array, ('zl', 'core', 'zh'), pairs)]
    ppermute x15 -> x21, waiting for transfers between devices: 42.1 us -> 38.5 us  [xor_shift(): return lax.ppermute(array, axis, [(i, i ^ k) for i in range(4)])]
    ppermute x10, starting transfers between devices: 21.4 us -> 17.8 us  [on_cores(): return lax.ppermute(array, ('zl', 'core', 'zh'), pairs)]
    ppermute x6, starting transfers between devices: 9.19 us -> 6.39 us  [other_core(): return lax.ppermute(array, 'core', [(0, 1), (1, 0)])]
    unnamed x12 -> x4, local copies, waits for them, and re-layouts: 1.41 us -> 0.01 us
    pallas_call x14, Pallas kernels: 17.4 us -> 18.8 us  [call(): pl.pallas_call(kernel, out_shape=tuple(out), in_specs=[any_spec() if a el...]
  transfers between devices with their start and end apart: 31 -> 37, of which waited for: 18 -> 22; matrix products, arithmetic and copies ran while one was open for 0% -> 0% of each run, Pallas kernels for 9% -> 13%
where the time goes in v3:
time: 119 us
  waiting for transfers between devices  51.4 us (43%)
  starting transfers between devices  47.8 us (40%)
  Pallas kernels  18.8 us (16%)
    ppermute x21, waiting for transfers between devices, xor_shift(): return lax.ppermute(array, axis, [(i, i ^ k) for i in range(4)])  38.5 us
    ppermute x21, starting transfers between devices, xor_shift(): return lax.ppermute(array, axis, [(i, i ^ k) for i in range(4)])  23.6 us
    pallas_call x14, Pallas kernels, call(): pl.pallas_call(kernel, out_shape=tuple(out), in_specs=[any_spec() if a el...  18.8 us
    ppermute x10, starting transfers between devices, on_cores(): return lax.ppermute(array, ('zl', 'core', 'zh'), pairs)  17.8 us
    ppermute x10, waiting for transfers between devices, on_cores(): return lax.ppermute(array, ('zl', 'core', 'zh'), pairs)  11.8 us
    ppermute x6, starting transfers between devices, other_core(): return lax.ppermute(array, 'core', [(0, 1), (1, 0)])  6.39 us
  transfers between devices with their start and end apart: 37, of which 22 were waited for; matrix products, arithmetic and copies ran while one was open for 0% of the time, Pallas kernels for 13%

profile of v3, /device:TPU:1, one launch (start us, length us, event | category | flops | bytes accessed | tf_op | source)
XLA Modules:
  0.0 118.9 jit_solution(730433019344523953)
XLA Ops:
  0.6 3.3 %collective-permute-start.2 = (bf16[576,2304]{1,0:T(8,128)(2,1)}, bf16[576,2304]{1,0:T(8,128)(2,1)S(1)}, u32[]{:S(2)}, u32[]{:S(2)}) collective-permute-start(bf16[576,2304]{1,0:T(8,128)(2,1)} %up_own.1), channel_id=1, source_target_pairs={{0,32},{32,0},{1,33},{33,1},{2,34},{34,2},{3,35},{35,3},{4,36},{36... | collective-permute-start | bytes 7962632 | tf_op jit(solution)/shard_map/ppermute | solution.py:40
  5.1 5.7 %collective-permute-start = (bf16[16,2304]{1,0:T(8,128)(2,1)S(1)}, bf16[16,2304]{1,0:T(8,128)(2,1)S(1)}, u32[]{:S(2)}, u32[]{:S(2)}) collective-permute-start(bf16[16,2304]{1,0:T(8,128)(2,1)S(1)} %dequant.1), channel_id=1, source_target_pairs={{0,0},{32,225},{64,64},{96,32},{128,128},{160,96},{192,192},{224,1... | collective-permute-start | bytes 221192 | tf_op jit(solution)/shard_map/ppermute | solution.py:24
  12.2 2.4 %collective-permute-done.1.oth = bf16[16,2304]{1,0:T(8,128)(2,1)S(1)} collective-permute-done((bf16[16,2304]{1,0:T(8,128)(2,1)S(1)}, bf16[16,2304]{1,0:T(8,128)(2,1)S(1)}, u32[]{:S(2)}, u32[]{:S(2)}) %collective-permute-start.1) | collective-permute-done | bytes 73760 | tf_op jit(solution)/shard_map/ppermute | solution.py:24
  15.9 1.8 %collective-permute-start.4 = (bf16[16,2304]{1,0:T(8,128)(2,1)S(1)}, bf16[16,2304]{1,0:T(8,128)(2,1)S(1)}, u32[]{:S(2)}, u32[]{:S(2)}) collective-permute-start(bf16[16,2304]{1,0:T(8,128)(2,1)S(1)} %get-tuple-element.37.x0), channel_id=1, source_target_pairs={{0,6},{2,4},{4,2},{6,0},{1,7},{3,5},{5,3},{7,1},{8,14},{10,12},{12... | collective-permute-start | bytes 221192 | tf_op jit(solution)/shard_map/ppermute | solution.py:32
  18.4 1.9 %collective-permute-start.6 = (bf16[16,2304]{1,0:T(8,128)(2,1)S(1)}, bf16[16,2304]{1,0:T(8,128)(2,1)S(1)}, u32[]{:S(2)}, u32[]{:S(2)}) collective-permute-start(bf16[16,2304]{1,0:T(8,128)(2,1)S(1)} %get-tuple-element.38.g0), channel_id=1, source_target_pairs={{0,64},{32,225},{64,128},{96,32},{128,192},{160,96},{192,1},{224,1... | collective-permute-start | bytes 221192 | tf_op jit(solution)/shard_map/ppermute | solution.py:24
  21.4 1.9 %collective-permute-done.5.x3 = bf16[16,2304]{1,0:T(8,128)(2,1)S(1)} collective-permute-done((bf16[16,2304]{1,0:T(8,128)(2,1)S(1)}, bf16[16,2304]{1,0:T(8,128)(2,1)S(1)}, u32[]{:S(2)}, u32[]{:S(2)}) %collective-permute-start.5) | collective-permute-done | bytes 73760 | tf_op jit(solution)/shard_map/ppermute | solution.py:32
  25.7 1.8 %collective-permute-start.11 = (bf16[2,16,2304]{2,1,0:T(8,128)(2,1)S(1)}, bf16[2,16,2304]{2,1,0:T(8,128)(2,1)S(1)}, u32[]{:S(2)}, u32[]{:S(2)}) collective-permute-start(bf16[2,16,2304]{2,1,0:T(8,128)(2,1)S(1)} %get-tuple-element.40.refs_0_), channel_id=1, source_target_pairs={{0,6},{2,4},{4,2},{6,0},{1,7},{3,5},{5,3},{7,1},{8,14},{10,12},{12... | collective-permute-start | bytes 442376 | tf_op jit(solution)/shard_map/ppermute | solution.py:32
  27.5 3.0 %collective-permute-done.10._.refs_1_ = bf16[2,16,2304]{2,1,0:T(8,128)(2,1)S(1)} collective-permute-done((bf16[2,16,2304]{2,1,0:T(8,128)(2,1)S(1)}, bf16[2,16,2304]{2,1,0:T(8,128)(2,1)S(1)}, u32[]{:S(2)}, u32[]{:S(2)}) %collective-permute-start.10) | collective-permute-done | bytes 147488 | tf_op jit(solution)/shard_map/ppermute | solution.py:32
  30.5 2.0 %collective-permute-done.11.__.refs_2_ = bf16[2,16,2304]{2,1,0:T(8,128)(2,1)S(1)} collective-permute-done((bf16[2,16,2304]{2,1,0:T(8,128)(2,1)S(1)}, bf16[2,16,2304]{2,1,0:T(8,128)(2,1)S(1)}, u32[]{:S(2)}, u32[]{:S(2)}) %collective-permute-start.11) | collective-permute-done | bytes 147488 | tf_op jit(solution)/shard_map/ppermute | solution.py:32
  33.4 2.4 %collective-permute-start.12 = (bf16[2,4,16,2304]{3,2,1,0:T(8,128)(2,1)S(1)}, bf16[2,4,16,2304]{3,2,1,0:T(8,128)(2,1)S(1)}, u32[]{:S(2)}, u32[]{:S(2)}) collective-permute-start(bf16[2,4,16,2304]{3,2,1,0:T(8,128)(2,1)S(1)} %get-tuple-element.41.refs_0_), channel_id=1, source_target_pairs={{0,128},{32,161},{64,192},{96,225},{128,1},{160,32},{192,65},{224,... | collective-permute-start | bytes 1769480 | tf_op jit(solution)/shard_map/ppermute | solution.py:24
  35.8 2.3 %collective-permute-start.13 = (bf16[2,16,2304]{2,1,0:T(8,128)(2,1)S(1)}, bf16[2,16,2304]{2,1,0:T(8,128)(2,1)S(1)}, u32[]{:S(2)}, u32[]{:S(2)}) collective-permute-start(bf16[2,16,2304]{2,1,0:T(8,128)(2,1)S(1)} %get-tuple-element.40.refs_0_), channel_id=1, source_target_pairs={{0,4},{2,6},{4,0},{6,2},{1,5},{3,7},{5,1},{7,3},{8,12},{10,14},{12... | collective-permute-start | bytes 442376 | tf_op jit(solution)/shard_map/ppermute | solution.py:32
  39.1 2.3 %collective-permute-start.16 = (bf16[2,16,2304]{2,1,0:T(8,128)(2,1)S(1)}, bf16[2,16,2304]{2,1,0:T(8,128)(2,1)S(1)}, u32[]{:S(2)}, u32[]{:S(2)}) collective-permute-start(bf16[2,16,2304]{2,1,0:T(8,128)(2,1)S(1)} %get-tuple-element.43.refs_4_), channel_id=1, source_target_pairs={{0,4},{2,6},{4,0},{6,2},{1,5},{3,7},{5,1},{7,3},{8,12},{10,14},{12... | collective-permute-start | bytes 442376 | tf_op jit(solution)/shard_map/ppermute | solution.py:32
  41.4 4.1 %join.1 = (bf16[1152,2304]{1,0:T(8,128)(2,1)S(1)}, bf16[1152,2304]{1,0:T(8,128)(2,1)S(1)}) custom-call(bf16[576,2304]{1,0:T(8,128)(2,1)} %up_own.1, bf16[576,2304]{1,0:T(8,128)(2,1)} %copy-done, bf16[576,2304]{1,0:T(8,128)(2,1)} %down_own.1, bf16[576,2304]{1,0:T(8,128)(2,1)} %copy-done.1, bf16[4,16,2304]{2,1,0:T(8,128)(2,1)S(1)} %get-tuple-element.39.row._), custom_call_target="tpu_custom_call" | custom-call | flops 1 | bytes 1 | tf_op jit(solution)/shard_map/join/pallas_call | solution.py:62
  48.2 3.9 %pre.2 = (f32[2,64,1152]{2,1,0:T(8,128)S(1)}, bf16[2,64,1152]{2,1,0:T(8,128)(2,1)S(1)}, bf16[2,64,1152]{2,1,0:T(8,128)(2,1)S(1)}, bf16[2,64,1152]{2,1,0:T(8,128)(2,1)S(1)}, bf16[4,4,16,2304]{3,2,1,0:T(8,128)(2,1)S(1)}) custom-call(bf16[2,16,2304]{2,1,0:T(8,128)(2,1)S(1)} %get-tuple-element.40.refs_0_, ...), custom_call_target="tpu_custom_call" | custom-call | flops 1 | bytes 1 | tf_op jit(solution)/shard_map/pre/pallas_call | solution.py:62
  52.1 2.2 %collective-permute-start.21 = (bf16[4,4,16,2304]{3,2,1,0:T(8,128)(2,1)S(1)}, bf16[4,4,16,2304]{3,2,1,0:T(8,128)(2,1)S(1)}, u32[]{:S(2)}, u32[]{:S(2)}) collective-permute-start(bf16[4,4,16,2304]{3,2,1,0:T(8,128)(2,1)S(1)} %get-tuple-element.54.g_own), channel_id=1, source_target_pairs={{0,32},{32,0},{1,33},{33,1},{2,34},{34,2},{3,35},{35,3},{4,36},{36... | collective-permute-start | bytes 3538952 | tf_op jit(solution)/shard_map/ppermute | solution.py:40
  54.4 2.6 %pre.3 = (f32[2,64,1152]{2,1,0:T(8,128)S(1)}, bf16[2,64,1152]{2,1,0:T(8,128)(2,1)S(1)}, bf16[2,64,1152]{2,1,0:T(8,128)(2,1)S(1)}, bf16[2,64,1152]{2,1,0:T(8,128)(2,1)S(1)}, bf16[4,4,16,2304]{3,2,1,0:T(8,128)(2,1)S(1)}) custom-call(bf16[2,4,16,2304]{3,2,1,0:T(8,128)(2,1)S(1)} %get-tuple-element.41.refs_0_, ...), custom_call_target="tpu_custom_call" | custom-call | flops 1 | bytes 1 | tf_op jit(solution)/shard_map/pre/pallas_call | solution.py:62
  58.7 1.9 %collective-permute-start.18 = (bf16[2,64,1152]{2,1,0:T(8,128)(2,1)S(1)}, bf16[2,64,1152]{2,1,0:T(8,128)(2,1)S(1)}, u32[]{:S(2)}, u32[]{:S(2)}) collective-permute-start(bf16[2,64,1152]{2,1,0:T(8,128)(2,1)S(1)} %get-tuple-element.51), channel_id=1, source_target_pairs={{0,24},{8,16},{16,8},{24,0},{1,25},{9,17},{17,9},{25,1},{2,26},{10... | collective-permute-start | bytes 884744 | tf_op jit(solution)/shard_map/ppermute | solution.py:32
  61.4 4.5 %collective-permute-done.17.r1 = bf16[2,64,1152]{2,1,0:T(8,128)(2,1)S(1)} collective-permute-done((bf16[2,64,1152]{2,1,0:T(8,128)(2,1)S(1)}, bf16[2,64,1152]{2,1,0:T(8,128)(2,1)S(1)}, u32[]{:S(2)}, u32[]{:S(2)}) %collective-permute-start.17) | collective-permute-done | bytes 294944 | tf_op jit(solution)/shard_map/ppermute | solution.py:32
  65.9 6.8 %collective-permute-done.18.r2 = bf16[2,64,1152]{2,1,0:T(8,128)(2,1)S(1)} collective-permute-done((bf16[2,64,1152]{2,1,0:T(8,128)(2,1)S(1)}, bf16[2,64,1152]{2,1,0:T(8,128)(2,1)S(1)}, u32[]{:S(2)}, u32[]{:S(2)}) %collective-permute-start.18) | collective-permute-done | bytes 294944 | tf_op jit(solution)/shard_map/ppermute | solution.py:32
  72.7 1.9 %collective-permute-done.19.r3 = bf16[2,64,1152]{2,1,0:T(8,128)(2,1)S(1)} collective-permute-done((bf16[2,64,1152]{2,1,0:T(8,128)(2,1)S(1)}, bf16[2,64,1152]{2,1,0:T(8,128)(2,1)S(1)}, u32[]{:S(2)}, u32[]{:S(2)}) %collective-permute-start.19) | collective-permute-done | bytes 294944 | tf_op jit(solution)/shard_map/ppermute | solution.py:32
  74.9 1.7 %collective-permute-start.23 = (bf16[64,1152]{1,0:T(8,128)(2,1)S(1)}, bf16[64,1152]{1,0:T(8,128)(2,1)S(1)}, u32[]{:S(2)}, u32[]{:S(2)}) collective-permute-start(bf16[64,1152]{1,0:T(8,128)(2,1)S(1)} %get-tuple-element.55.p0.refs_4_), channel_id=1, source_target_pairs={{0,24},{8,16},{16,8},{24,0},{1,25},{9,17},{17,9},{25,1},{2,26},{10... | collective-permute-start | bytes 442376 | tf_op jit(solution)/shard_map/ppermute | solution.py:32
  80.6 3.5 %collective-permute-done.24.p3.refs_7_ = bf16[64,1152]{1,0:T(8,128)(2,1)S(1)} collective-permute-done((bf16[64,1152]{1,0:T(8,128)(2,1)S(1)}, bf16[64,1152]{1,0:T(8,128)(2,1)S(1)}, u32[]{:S(2)}, u32[]{:S(2)}) %collective-permute-start.24) | collective-permute-done | bytes 147488 | tf_op jit(solution)/shard_map/ppermute | solution.py:32
  84.0 1.7 %back.1 = (bf16[64,2304]{1,0:T(8,128)(2,1)S(1)}, bf16[64,2304]{1,0:T(8,128)(2,1)S(1)}, bf16[64,2304]{1,0:T(8,128)(2,1)S(1)}, bf16[64,2304]{1,0:T(8,128)(2,1)S(1)}) custom-call(bf16[64,1152]{1,0:T(8,128)(2,1)S(1)} %get-tuple-element.55.p0.refs_4_, bf16[64,1152]{1,0:T(8,128)(2,1)S(1)} %collective-permute-done.22.p1.refs_5_, ...), custom_call_target="tpu_custom_call" | custom-call | flops 1 | bytes 1 | tf_op jit(solution)/shard_map/back/pallas_call | solution.py:62
  87.4 1.7 %collective-permute-start.27 = (bf16[64,2304]{1,0:T(8,128)(2,1)S(1)}, bf16[64,2304]{1,0:T(8,128)(2,1)S(1)}, u32[]{:S(2)}, u32[]{:S(2)}) collective-permute-start(bf16[64,2304]{1,0:T(8,128)(2,1)S(1)} %get-tuple-element.59), channel_id=1, source_target_pairs={{0,4},{2,6},{4,0},{6,2},{1,5},{3,7},{5,1},{7,3},{8,12},{10,14},{12... | collective-permute-start | bytes 884744 | tf_op jit(solution)/shard_map/ppermute | solution.py:32
  90.1 2.4 %collective-permute-done.25.refs_1_ = bf16[64,2304]{1,0:T(8,128)(2,1)S(1)} collective-permute-done((bf16[64,2304]{1,0:T(8,128)(2,1)S(1)}, bf16[64,2304]{1,0:T(8,128)(2,1)S(1)}, u32[]{:S(2)}, u32[]{:S(2)}) %collective-permute-start.25) | collective-permute-done | bytes 294944 | tf_op jit(solution)/shard_map/ppermute | solution.py:32
  92.5 1.8 %collective-permute-done.26.refs_2_ = bf16[64,2304]{1,0:T(8,128)(2,1)S(1)} collective-permute-done((bf16[64,2304]{1,0:T(8,128)(2,1)S(1)}, bf16[64,2304]{1,0:T(8,128)(2,1)S(1)}, u32[]{:S(2)}, u32[]{:S(2)}) %collective-permute-start.26) | collective-permute-done | bytes 294944 | tf_op jit(solution)/shard_map/ppermute | solution.py:32
  94.4 4.5 %collective-permute-done.27.refs_3_ = bf16[64,2304]{1,0:T(8,128)(2,1)S(1)} collective-permute-done((bf16[64,2304]{1,0:T(8,128)(2,1)S(1)}, bf16[64,2304]{1,0:T(8,128)(2,1)S(1)}, u32[]{:S(2)}, u32[]{:S(2)}) %collective-permute-start.27) | collective-permute-done | bytes 294944 | tf_op jit(solution)/shard_map/ppermute | solution.py:32
  99.0 1.9 %collective-permute-start.28 = (bf16[16,2304]{1,0:T(8,128)(2,1)S(1)}, bf16[16,2304]{1,0:T(8,128)(2,1)S(1)}, u32[]{:S(2)}, u32[]{:S(2)}) collective-permute-start(bf16[16,2304]{1,0:T(8,128)(2,1)S(1)} %get-tuple-element.60), channel_id=1, source_target_pairs={{0,0},{32,96},{64,64},{96,160},{128,128},{160,224},{192,192},{224,... | collective-permute-start | bytes 221192 | tf_op jit(solution)/shard_map/ppermute | solution.py:24
  101.0 4.3 %collective-permute-done.28.refs_8_.refs_0_ = bf16[16,2304]{1,0:T(8,128)(2,1)S(1)} collective-permute-done((bf16[16,2304]{1,0:T(8,128)(2,1)S(1)}, bf16[16,2304]{1,0:T(8,128)(2,1)S(1)}, u32[]{:S(2)}, u32[]{:S(2)}) %collective-permute-start.28) | collective-permute-done | bytes 73760 | tf_op jit(solution)/shard_map/ppermute | solution.py:24
  107.5 2.6 %collective-permute-start.31 = (bf16[16,2304]{1,0:T(8,128)(2,1)S(1)}, bf16[16,2304]{1,0:T(8,128)(2,1)S(1)}, u32[]{:S(2)}, u32[]{:S(2)}) collective-permute-start(bf16[16,2304]{1,0:T(8,128)(2,1)S(1)} %get-tuple-element.63), channel_id=1, source_target_pairs={{0,65},{32,33},{64,129},{96,97},{128,193},{160,161},{192,0},{224,2... | collective-permute-start | bytes 221192 | tf_op jit(solution)/shard_map/ppermute | solution.py:24
  110.1 3.9 %weight_grads.1 = (bf16[576,2304]{1,0:T(8,128)(2,1)}, bf16[576,2304]{1,0:T(8,128)(2,1)}) custom-call(bf16[2,576,256]{2,1,0:T(8,128)(2,1)S(1)} %get-tuple-element.65.keep, bf16[2,576,256]{2,1,0:T(8,128)(2,1)S(1)} %collective-permute-done.35.came, bf16[4,4,16,2304]{3,2,1,0:T(8,128)(2,1)S(1)} %get-tuple-element.53.i_own, ...), custom_call_target="tpu_custom_call" | custom-call | flops 1 | bytes 1 | tf_op jit(solution)/shard_map/weight_grads/pallas_call | solution.py:62
  114.0 2.8 %collective-permute-done.31.refs_3_ = bf16[16,2304]{1,0:T(8,128)(2,1)S(1)} collective-permute-done((bf16[16,2304]{1,0:T(8,128)(2,1)S(1)}, bf16[16,2304]{1,0:T(8,128)(2,1)S(1)}, u32[]{:S(2)}, u32[]{:S(2)}) %collective-permute-start.31) | collective-permute-done | bytes 73760 | tf_op jit(solution)/shard_map/ppermute | solution.py:24
  (60 shorter events, 26.0 us)
Async XLA Ops:
  0.6 14.0 %collective-permute-start.2 = (bf16[576,2304]{1,0:T(8,128)(2,1)}, bf16[576,2304]{1,0:T(8,128)(2,1)S(1)}, u32[]{:S(2)}, u32[]{:S(2)}) collective-permute-start(bf16[576,2304]{1,0:T(8,128)(2,1)} %up_own.1), channel_id=1, source_target_pairs={{0,32},{32,0},{1,33},{33,1},{2,34},{34,2},{3,35},{35,3},{4,36},{36... | collective-permute-start | bytes 7962632 | tf_op jit(solution)/shard_map/ppermute | solution.py:40
  4.0 16.4 %collective-permute-start.7 = (bf16[576,2304]{1,0:T(8,128)(2,1)}, bf16[576,2304]{1,0:T(8,128)(2,1)S(1)}, u32[]{:S(2)}, u32[]{:S(2)}) collective-permute-start(bf16[576,2304]{1,0:T(8,128)(2,1)} %down_own.1), channel_id=1, source_target_pairs={{0,32},{32,0},{1,33},{33,1},{2,34},{34,2},{3,35},{35,3},{4,36},{36... | collective-permute-start | bytes 7962632 | tf_op jit(solution)/shard_map/ppermute | solution.py:40
  5.1 7.1 %collective-permute-start = (bf16[16,2304]{1,0:T(8,128)(2,1)S(1)}, bf16[16,2304]{1,0:T(8,128)(2,1)S(1)}, u32[]{:S(2)}, u32[]{:S(2)}) collective-permute-start(bf16[16,2304]{1,0:T(8,128)(2,1)S(1)} %dequant.1), channel_id=1, source_target_pairs={{0,0},{32,225},{64,64},{96,32},{128,128},{160,96},{192,192},{224,1... | collective-permute-start | bytes 221192 | tf_op jit(solution)/shard_map/ppermute | solution.py:24
  14.6 5.7 %collective-permute-start.3 = (bf16[16,2304]{1,0:T(8,128)(2,1)S(1)}, bf16[16,2304]{1,0:T(8,128)(2,1)S(1)}, u32[]{:S(2)}, u32[]{:S(2)}) collective-permute-start(bf16[16,2304]{1,0:T(8,128)(2,1)S(1)} %get-tuple-element.37.x0), channel_id=1, source_target_pairs={{0,2},{2,0},{4,6},{6,4},{1,3},{3,1},{5,7},{7,5},{8,10},{10,8},{12,... | collective-permute-start | bytes 221192 | tf_op jit(solution)/shard_map/ppermute | solution.py:32
  15.9 5.4 %collective-permute-start.4 = (bf16[16,2304]{1,0:T(8,128)(2,1)S(1)}, bf16[16,2304]{1,0:T(8,128)(2,1)S(1)}, u32[]{:S(2)}, u32[]{:S(2)}) collective-permute-start(bf16[16,2304]{1,0:T(8,128)(2,1)S(1)} %get-tuple-element.37.x0), channel_id=1, source_target_pairs={{0,6},{2,4},{4,2},{6,0},{1,7},{3,5},{5,3},{7,1},{8,14},{10,12},{12... | collective-permute-start | bytes 221192 | tf_op jit(solution)/shard_map/ppermute | solution.py:32
  17.7 5.5 %collective-permute-start.5 = (bf16[16,2304]{1,0:T(8,128)(2,1)S(1)}, bf16[16,2304]{1,0:T(8,128)(2,1)S(1)}, u32[]{:S(2)}, u32[]{:S(2)}) collective-permute-start(bf16[16,2304]{1,0:T(8,128)(2,1)S(1)} %get-tuple-element.37.x0), channel_id=1, source_target_pairs={{0,4},{2,6},{4,0},{6,2},{1,5},{3,7},{5,1},{7,3},{8,12},{10,14},{12... | collective-permute-start | bytes 221192 | tf_op jit(solution)/shard_map/ppermute | solution.py:32
  23.3 10.1 %collective-permute-start.8 = (bf16[4,16,2304]{2,1,0:T(8,128)(2,1)S(1)}, bf16[4,16,2304]{2,1,0:T(8,128)(2,1)S(1)}, u32[]{:S(2)}, u32[]{:S(2)}) collective-permute-start(bf16[4,16,2304]{2,1,0:T(8,128)(2,1)S(1)} %get-tuple-element.39.row._), channel_id=1, source_target_pairs={{0,64},{32,225},{64,128},{96,32},{128,192},{160,96},{192,1},{224,1... | collective-permute-start | bytes 884744 | tf_op jit(solution)/shard_map/ppermute | solution.py:24
  24.8 5.6 %collective-permute-start.10 = (bf16[2,16,2304]{2,1,0:T(8,128)(2,1)S(1)}, bf16[2,16,2304]{2,1,0:T(8,128)(2,1)S(1)}, u32[]{:S(2)}, u32[]{:S(2)}) collective-permute-start(bf16[2,16,2304]{2,1,0:T(8,128)(2,1)S(1)} %get-tuple-element.40.refs_0_), channel_id=1, source_target_pairs={{0,2},{2,0},{4,6},{6,4},{1,3},{3,1},{5,7},{7,5},{8,10},{10,8},{12,... | collective-permute-start | bytes 442376 | tf_op jit(solution)/shard_map/ppermute | solution.py:32
  25.7 6.9 %collective-permute-start.11 = (bf16[2,16,2304]{2,1,0:T(8,128)(2,1)S(1)}, bf16[2,16,2304]{2,1,0:T(8,128)(2,1)S(1)}, u32[]{:S(2)}, u32[]{:S(2)}) collective-permute-start(bf16[2,16,2304]{2,1,0:T(8,128)(2,1)S(1)} %get-tuple-element.40.refs_0_), channel_id=1, source_target_pairs={{0,6},{2,4},{4,2},{6,0},{1,7},{3,5},{5,3},{7,1},{8,14},{10,12},{12... | collective-permute-start | bytes 442376 | tf_op jit(solution)/shard_map/ppermute | solution.py:32
  27.5 5.9 %collective-permute-start.9 = (bf16[2,16,2304]{2,1,0:T(8,128)(2,1)S(1)}, bf16[2,16,2304]{2,1,0:T(8,128)(2,1)S(1)}, u32[]{:S(2)}, u32[]{:S(2)}) collective-permute-start(bf16[2,16,2304]{2,1,0:T(8,128)(2,1)S(1)} %get-tuple-element.40.refs_0_), channel_id=1, source_target_pairs={{0,128},{32,161},{64,192},{96,225},{128,1},{160,32},{192,65},{224,... | collective-permute-start | bytes 442376 | tf_op jit(solution)/shard_map/ppermute | solution.py:24
  33.4 20.9 %collective-permute-start.12 = (bf16[2,4,16,2304]{3,2,1,0:T(8,128)(2,1)S(1)}, bf16[2,4,16,2304]{3,2,1,0:T(8,128)(2,1)S(1)}, u32[]{:S(2)}, u32[]{:S(2)}) collective-permute-start(bf16[2,4,16,2304]{3,2,1,0:T(8,128)(2,1)S(1)} %get-tuple-element.41.refs_0_), channel_id=1, source_target_pairs={{0,128},{32,161},{64,192},{96,225},{128,1},{160,32},{192,65},{224,... | collective-permute-start | bytes 1769480 | tf_op jit(solution)/shard_map/ppermute | solution.py:24
  35.8 9.7 %collective-permute-start.13 = (bf16[2,16,2304]{2,1,0:T(8,128)(2,1)S(1)}, bf16[2,16,2304]{2,1,0:T(8,128)(2,1)S(1)}, u32[]{:S(2)}, u32[]{:S(2)}) collective-permute-start(bf16[2,16,2304]{2,1,0:T(8,128)(2,1)S(1)} %get-tuple-element.40.refs_0_), channel_id=1, source_target_pairs={{0,4},{2,6},{4,0},{6,2},{1,5},{3,7},{5,1},{7,3},{8,12},{10,14},{12... | collective-permute-start | bytes 442376 | tf_op jit(solution)/shard_map/ppermute | solution.py:32
  38.2 7.8 %collective-permute-start.14 = (bf16[2,16,2304]{2,1,0:T(8,128)(2,1)S(1)}, bf16[2,16,2304]{2,1,0:T(8,128)(2,1)S(1)}, u32[]{:S(2)}, u32[]{:S(2)}) collective-permute-start(bf16[2,16,2304]{2,1,0:T(8,128)(2,1)S(1)} %get-tuple-element.43.refs_4_), channel_id=1, source_target_pairs={{0,2},{2,0},{4,6},{6,4},{1,3},{3,1},{5,7},{7,5},{8,10},{10,8},{12,... | collective-permute-start | bytes 442376 | tf_op jit(solution)/shard_map/ppermute | solution.py:32
  38.5 9.0 %collective-permute-start.15 = (bf16[2,16,2304]{2,1,0:T(8,128)(2,1)S(1)}, bf16[2,16,2304]{2,1,0:T(8,128)(2,1)S(1)}, u32[]{:S(2)}, u32[]{:S(2)}) collective-permute-start(bf16[2,16,2304]{2,1,0:T(8,128)(2,1)S(1)} %get-tuple-element.43.refs_4_), channel_id=1, source_target_pairs={{0,6},{2,4},{4,2},{6,0},{1,7},{3,5},{5,3},{7,1},{8,14},{10,12},{12... | collective-permute-start | bytes 442376 | tf_op jit(solution)/shard_map/ppermute | solution.py:32
  39.1 9.1 %collective-permute-start.16 = (bf16[2,16,2304]{2,1,0:T(8,128)(2,1)S(1)}, bf16[2,16,2304]{2,1,0:T(8,128)(2,1)S(1)}, u32[]{:S(2)}, u32[]{:S(2)}) collective-permute-start(bf16[2,16,2304]{2,1,0:T(8,128)(2,1)S(1)} %get-tuple-element.43.refs_4_), channel_id=1, source_target_pairs={{0,4},{2,6},{4,0},{6,2},{1,5},{3,7},{5,1},{7,3},{8,12},{10,14},{12... | collective-permute-start | bytes 442376 | tf_op jit(solution)/shard_map/ppermute | solution.py:32
  52.1 22.5 %collective-permute-start.21 = (bf16[4,4,16,2304]{3,2,1,0:T(8,128)(2,1)S(1)}, bf16[4,4,16,2304]{3,2,1,0:T(8,128)(2,1)S(1)}, u32[]{:S(2)}, u32[]{:S(2)}) collective-permute-start(bf16[4,4,16,2304]{3,2,1,0:T(8,128)(2,1)S(1)} %get-tuple-element.54.g_own), channel_id=1, source_target_pairs={{0,32},{32,0},{1,33},{33,1},{2,34},{34,2},{3,35},{35,3},{4,36},{36... | collective-permute-start | bytes 3538952 | tf_op jit(solution)/shard_map/ppermute | solution.py:40
  57.0 17.7 %collective-permute-start.20 = (bf16[4,4,16,2304]{3,2,1,0:T(8,128)(2,1)S(1)}, bf16[4,4,16,2304]{3,2,1,0:T(8,128)(2,1)S(1)}, u32[]{:S(2)}, u32[]{:S(2)}) collective-permute-start(bf16[4,4,16,2304]{3,2,1,0:T(8,128)(2,1)S(1)} %get-tuple-element.53.i_own), channel_id=1, source_target_pairs={{0,32},{32,0},{1,33},{33,1},{2,34},{34,2},{3,35},{35,3},{4,36},{36... | collective-permute-start | bytes 3538952 | tf_op jit(solution)/shard_map/ppermute | solution.py:40
  57.4 8.5 %collective-permute-start.17 = (bf16[2,64,1152]{2,1,0:T(8,128)(2,1)S(1)}, bf16[2,64,1152]{2,1,0:T(8,128)(2,1)S(1)}, u32[]{:S(2)}, u32[]{:S(2)}) collective-permute-start(bf16[2,64,1152]{2,1,0:T(8,128)(2,1)S(1)} %get-tuple-element.50), channel_id=1, source_target_pairs={{0,8},{8,0},{16,24},{24,16},{1,9},{9,1},{17,25},{25,17},{2,10},{10... | collective-permute-start | bytes 884744 | tf_op jit(solution)/shard_map/ppermute | solution.py:32
  58.7 14.0 %collective-permute-start.18 = (bf16[2,64,1152]{2,1,0:T(8,128)(2,1)S(1)}, bf16[2,64,1152]{2,1,0:T(8,128)(2,1)S(1)}, u32[]{:S(2)}, u32[]{:S(2)}) collective-permute-start(bf16[2,64,1152]{2,1,0:T(8,128)(2,1)S(1)} %get-tuple-element.51), channel_id=1, source_target_pairs={{0,24},{8,16},{16,8},{24,0},{1,25},{9,17},{17,9},{25,1},{2,26},{10... | collective-permute-start | bytes 884744 | tf_op jit(solution)/shard_map/ppermute | solution.py:32
  60.6 14.0 %collective-permute-start.19 = (bf16[2,64,1152]{2,1,0:T(8,128)(2,1)S(1)}, bf16[2,64,1152]{2,1,0:T(8,128)(2,1)S(1)}, u32[]{:S(2)}, u32[]{:S(2)}) collective-permute-start(bf16[2,64,1152]{2,1,0:T(8,128)(2,1)S(1)} %get-tuple-element.52), channel_id=1, source_target_pairs={{0,16},{8,24},{16,0},{24,8},{1,17},{9,25},{17,1},{25,9},{2,18},{10... | collective-permute-start | bytes 884744 | tf_op jit(solution)/shard_map/ppermute | solution.py:32
  74.9 5.6 %collective-permute-start.23 = (bf16[64,1152]{1,0:T(8,128)(2,1)S(1)}, bf16[64,1152]{1,0:T(8,128)(2,1)S(1)}, u32[]{:S(2)}, u32[]{:S(2)}) collective-permute-start(bf16[64,1152]{1,0:T(8,128)(2,1)S(1)} %get-tuple-element.55.p0.refs_4_), channel_id=1, source_target_pairs={{0,24},{8,16},{16,8},{24,0},{1,25},{9,17},{17,9},{25,1},{2,26},{10... | collective-permute-start | bytes 442376 | tf_op jit(solution)/shard_map/ppermute | solution.py:32
  76.7 7.4 %collective-permute-start.24 = (bf16[64,1152]{1,0:T(8,128)(2,1)S(1)}, bf16[64,1152]{1,0:T(8,128)(2,1)S(1)}, u32[]{:S(2)}, u32[]{:S(2)}) collective-permute-start(bf16[64,1152]{1,0:T(8,128)(2,1)S(1)} %get-tuple-element.55.p0.refs_4_), channel_id=1, source_target_pairs={{0,16},{8,24},{16,0},{24,8},{1,17},{9,25},{17,1},{25,9},{2,18},{10... | collective-permute-start | bytes 442376 | tf_op jit(solution)/shard_map/ppermute | solution.py:32
  85.8 6.8 %collective-permute-start.25 = (bf16[64,2304]{1,0:T(8,128)(2,1)S(1)}, bf16[64,2304]{1,0:T(8,128)(2,1)S(1)}, u32[]{:S(2)}, u32[]{:S(2)}) collective-permute-start(bf16[64,2304]{1,0:T(8,128)(2,1)S(1)} %get-tuple-element.57), channel_id=1, source_target_pairs={{0,2},{2,0},{4,6},{6,4},{1,3},{3,1},{5,7},{7,5},{8,10},{10,8},{12,... | collective-permute-start | bytes 884744 | tf_op jit(solution)/shard_map/ppermute | solution.py:32
  85.9 8.5 %collective-permute-start.26 = (bf16[64,2304]{1,0:T(8,128)(2,1)S(1)}, bf16[64,2304]{1,0:T(8,128)(2,1)S(1)}, u32[]{:S(2)}, u32[]{:S(2)}) collective-permute-start(bf16[64,2304]{1,0:T(8,128)(2,1)S(1)} %get-tuple-element.58), channel_id=1, source_target_pairs={{0,6},{2,4},{4,2},{6,0},{1,7},{3,5},{5,3},{7,1},{8,14},{10,12},{12... | collective-permute-start | bytes 884744 | tf_op jit(solution)/shard_map/ppermute | solution.py:32
  87.4 11.5 %collective-permute-start.27 = (bf16[64,2304]{1,0:T(8,128)(2,1)S(1)}, bf16[64,2304]{1,0:T(8,128)(2,1)S(1)}, u32[]{:S(2)}, u32[]{:S(2)}) collective-permute-start(bf16[64,2304]{1,0:T(8,128)(2,1)S(1)} %get-tuple-element.59), channel_id=1, source_target_pairs={{0,4},{2,6},{4,0},{6,2},{1,5},{3,7},{5,1},{7,3},{8,12},{10,14},{12... | collective-permute-start | bytes 884744 | tf_op jit(solution)/shard_map/ppermute | solution.py:32
  89.1 11.8 %collective-permute-start.32 = (bf16[64,1152]{1,0:T(8,128)(2,1)S(1)}, bf16[64,1152]{1,0:T(8,128)(2,1)S(1)}, u32[]{:S(2)}, u32[]{:S(2)}) collective-permute-start(bf16[64,1152]{1,0:T(8,128)(2,1)S(1)} %get-tuple-element.64.refs_0_), channel_id=1, source_target_pairs={{0,8},{8,0},{16,24},{24,16},{1,9},{9,1},{17,25},{25,17},{2,10},{10... | collective-permute-start | bytes 442376 | tf_op jit(solution)/shard_map/ppermute | solution.py:32
  89.1 11.8 %collective-permute-start.33 = (bf16[64,1152]{1,0:T(8,128)(2,1)S(1)}, bf16[64,1152]{1,0:T(8,128)(2,1)S(1)}, u32[]{:S(2)}, u32[]{:S(2)}) collective-permute-start(bf16[64,1152]{1,0:T(8,128)(2,1)S(1)} %get-tuple-element.64.refs_0_), channel_id=1, source_target_pairs={{0,24},{8,16},{16,8},{24,0},{1,25},{9,17},{17,9},{25,1},{2,26},{10... | collective-permute-start | bytes 442376 | tf_op jit(solution)/shard_map/ppermute | solution.py:32
  92.5 8.4 %collective-permute-start.34 = (bf16[64,1152]{1,0:T(8,128)(2,1)S(1)}, bf16[64,1152]{1,0:T(8,128)(2,1)S(1)}, u32[]{:S(2)}, u32[]{:S(2)}) collective-permute-start(bf16[64,1152]{1,0:T(8,128)(2,1)S(1)} %get-tuple-element.64.refs_0_), channel_id=1, source_target_pairs={{0,16},{8,24},{16,0},{24,8},{1,17},{9,25},{17,1},{25,9},{2,18},{10... | collective-permute-start | bytes 442376 | tf_op jit(solution)/shard_map/ppermute | solution.py:32
  99.0 6.3 %collective-permute-start.28 = (bf16[16,2304]{1,0:T(8,128)(2,1)S(1)}, bf16[16,2304]{1,0:T(8,128)(2,1)S(1)}, u32[]{:S(2)}, u32[]{:S(2)}) collective-permute-start(bf16[16,2304]{1,0:T(8,128)(2,1)S(1)} %get-tuple-element.60), channel_id=1, source_target_pairs={{0,0},{32,96},{64,64},{96,160},{128,128},{160,224},{192,192},{224,... | collective-permute-start | bytes 221192 | tf_op jit(solution)/shard_map/ppermute | solution.py:24
  105.9 8.2 %collective-permute-start.29 = (bf16[16,2304]{1,0:T(8,128)(2,1)S(1)}, bf16[16,2304]{1,0:T(8,128)(2,1)S(1)}, u32[]{:S(2)}, u32[]{:S(2)}) collective-permute-start(bf16[16,2304]{1,0:T(8,128)(2,1)S(1)} %get-tuple-element.61), channel_id=1, source_target_pairs={{0,193},{32,160},{64,0},{96,224},{128,64},{160,33},{192,128},{224,... | collective-permute-start | bytes 221192 | tf_op jit(solution)/shard_map/ppermute | solution.py:24
  106.0 8.1 %collective-permute-start.30 = (bf16[16,2304]{1,0:T(8,128)(2,1)S(1)}, bf16[16,2304]{1,0:T(8,128)(2,1)S(1)}, u32[]{:S(2)}, u32[]{:S(2)}) collective-permute-start(bf16[16,2304]{1,0:T(8,128)(2,1)S(1)} %get-tuple-element.62), channel_id=1, source_target_pairs={{0,129},{32,224},{64,193},{96,33},{128,0},{160,97},{192,64},{224,1... | collective-permute-start | bytes 221192 | tf_op jit(solution)/shard_map/ppermute | solution.py:24
  107.5 9.4 %collective-permute-start.31 = (bf16[16,2304]{1,0:T(8,128)(2,1)S(1)}, bf16[16,2304]{1,0:T(8,128)(2,1)S(1)}, u32[]{:S(2)}, u32[]{:S(2)}) collective-permute-start(bf16[16,2304]{1,0:T(8,128)(2,1)S(1)} %get-tuple-element.63), channel_id=1, source_target_pairs={{0,65},{32,33},{64,129},{96,97},{128,193},{160,161},{192,0},{224,2... | collective-permute-start | bytes 221192 | tf_op jit(solution)/shard_map/ppermute | solution.py:24
  (7 other events, 48.6 us)

commit v4 on v3

--- a/solution.py
+++ b/solution.py
@@ -133,25 +133,7 @@
         copy.wait()
 
 
-def pre_kernel(*refs, parts, at, before):
-    parts, weights, before, refs = refs[:parts], refs[parts], refs[parts + 1 : parts + 1 + before], refs[parts + 1 + before :]
-    outs, rows_out, (rows, slots, sems, out_sem) = refs[:4], refs[4], refs[5:]
-    y = lax.axis_index("y")
-    copies = []
-    if at:
-        for n, ref in enumerate(parts):
-            copies.append(pltpu.make_async_copy(ref, rows.at[n % 4, pl.ds(2 * (n // 4), 2)], sems.at[n]))
-    else:
-        for n in range(4):
-            copies.append(pltpu.make_async_copy(parts[n // 2].at[n % 2], rows.at[:, n], sems.at[n]))
-    for copy in copies:
-        copy.start()
-    for done, out in zip(before, outs):
-        out[1 - at] = done[1 - at]
-    for copy in copies:
-        copy.wait()
-    back = pltpu.make_async_copy(rows, rows_out, out_sem)
-    back.start()
+def times(rows, weights, y, slots, outs, at):
     hidden, wide = weights.shape
     step = slots.shape[2]
     for n in range(0, hidden, step):
@@ -160,24 +142,60 @@
         )
         slots[...] = part.reshape(4, 64, step)
         for k, out in zip(NEAR_FIRST, outs):
-            out[at, :, n : n + step] = slots[jnp.bitwise_xor(y, k)].astype(out.dtype)
-    back.wait()
-
-
-def pre(parts, weights, at, before):
-    hidden, wide = weights.shape
-    sent = struct(2, 64, hidden)
-    *partial, rows = call(
-        functools.partial(pre_kernel, parts=len(parts), at=at, before=len(before)), "pre",
-        [struct(2, 64, hidden, dtype=F32), sent, sent, sent, struct(4, 4, 16, wide)], (*parts, in_vmem(weights), *before),
-        ins=[True] * len(parts) + [False] * (1 + len(before)), outs=[False] * 4 + [pl.ANY],
-        scratch=[pltpu.VMEM((4, 4, 16, wide), BF), pltpu.VMEM((4, 64, 384), F32), pltpu.SemaphoreType.DMA((8,)), pltpu.SemaphoreType.DMA],
-        limit=12,
-    )
-    return partial, rows
-
-
-def act_kernel(own, r1, r2, r3, _, __, squared, grad_pre):
+            value = slots[jnp.bitwise_xor(y, k)].astype(out.dtype)
+            if at is None:
+                out[:, n : n + step] = value
+            else:
+                out[at, :, n : n + step] = value
+
+
+def grads_kernel(*refs):
+    parts, weights, outs, rows, slots = refs[:8], refs[8], refs[9:13], refs[13], refs[14]
+    for n, ref in enumerate(parts):
+        rows[n % 4, 2 * (n // 4) : 2 * (n // 4) + 2] = ref[...]
+    times(rows, weights, lax.axis_index("y"), slots, outs, None)
+
+
+def inputs_kernel(near, far, weights, g0, g1, g2, g3, g_rows, o0, o1, o2, o3, rows_out, rows, slots):
+    for n in range(4):
+        rows[:, n] = (near, far)[n // 2][n % 2]
+    for done, out in zip((g0, g1, g2, g3), (o0, o1, o2, o3)):
+        out[1] = done[...]
+    rows_out[0] = rows[...]
+    rows_out[1] = g_rows[...]
+    times(rows, weights, lax.axis_index("y"), slots, (o0, o1, o2, o3), 0)
+
+
+def pre(i_parts, g_parts, up, down):
+    hidden, wide = up.shape
+    rows = struct(4, 4, 16, wide)
+    slots = pltpu.VMEM((4, 64, 384), F32)
+    *partial, g_rows = call(
+        grads_kernel, "grads", [struct(64, hidden, dtype=F32)] + [struct(64, hidden)] * 3 + [rows], (*g_parts, in_vmem(down)),
+        scratch=[slots], limit=12,
+    )
+    *partial, both = call(
+        inputs_kernel, "inputs", [struct(2, 64, hidden, dtype=F32)] + [struct(2, 64, hidden)] * 3 + [struct(2, 4, 4, 16, wide)],
+        (*i_parts, in_vmem(up), *partial, g_rows), scratch=[pltpu.VMEM((4, 4, 16, wide), BF), slots], limit=12,
+    )
+    return partial, both
+
+
+def copy_kernel(src, _, out, sem):
+    copy = pltpu.make_async_copy(src, out, sem)
+    copy.start()
+    copy.wait()
+
+
+def copied(array, after):
+    (out,) = call(
+        copy_kernel, "copied", [struct(*array.shape)], (array, after), ins=[True] * 2, outs=[pl.ANY],
+        scratch=[pltpu.SemaphoreType.DMA], limit=1,
+    )
+    return out
+
+
+def act_kernel(own, r1, r2, r3, squared, grad_pre):
     total = [own[at] + r1[at].astype(F32) + r2[at].astype(F32) + r3[at].astype(F32) for at in range(2)]
     positive = jnp.maximum(total[0], 0.0)
     squared[...] = (positive * positive).astype(BF)
@@ -208,15 +226,15 @@
         send[at] = turned[hid:]
 
 
-def weights_kernel(keep, came, i_own, i_oth, g_own, g_oth, up, down, up_block, down_block, sems):
+def weights_kernel(keep, came, own, oth, up, down, up_block, down_block, sems):
     hid, wide = up_block.shape
     step = 768
     copies = []
-    for at, (own, oth, block, out) in enumerate(((g_own, g_oth, down_block, down), (i_own, i_oth, up_block, up))):
+    for at, (mat, block, out) in enumerate(((1, down_block, down), (0, up_block, up))):
         for i, n in enumerate(range(0, wide, step)):
             cols = pl.ds(n, step)
-            total = jnp.dot(keep[at], own[:, :, :, cols].reshape(256, step), preferred_element_type=F32)
-            total += jnp.dot(came[at], oth[:, :, :, cols].reshape(256, step), preferred_element_type=F32)
+            total = jnp.dot(keep[at], own[mat, :, :, :, cols].reshape(256, step), preferred_element_type=F32)
+            total += jnp.dot(came[at], oth[mat, :, :, :, cols].reshape(256, step), preferred_element_type=F32)
             block[:, cols] = total.astype(BF)
             copies.append(pltpu.make_async_copy(block.at[:, cols], out.at[:, cols], sems.at[at, i]))
             copies[-1].start()
@@ -265,21 +283,17 @@
     far = z_shift(pair, 2, -2)
     g_distant = exchange([distant] * 4, "x")
     up_both, down_both = call(
-        join_kernel, "join", [struct(2 * hid, wide)] * 2, (*in_hbm(up_weight, up_other, down_weight, down_other), row),
+        join_kernel, "join", [struct(2 * hid, wide)] * 2, (*in_hbm(up_weight), in_vmem(up_other), *in_hbm(down_weight), in_vmem(down_other), row),
         ins=[True] * 5, outs=[pl.ANY] * 2, scratch=[pltpu.SemaphoreType.DMA((4,))], limit=1,
     )
-    partial, g_rows = pre((*g_near, *g_distant), down_both, 1, ())
-    partial, i_rows = pre((pair, far), up_both, 0, partial)
-    i_other = other_core(i_rows)
-    g_other = other_core(g_rows)
+    partial, both = pre((pair, far), (*g_near, *g_distant), up_both, down_both)
     squared, grad_pre = call(
-        act_kernel, "act", [struct(64, 2 * hid)] * 2, (*exchange(partial, "y"), i_other, g_other),
-        ins=[False] * 4 + [True] * 2,
+        act_kernel, "act", [struct(64, 2 * hid)] * 2, exchange(partial, "y"),
     )
     grad_pre = exchange([grad_pre] * 4, "y")
     squared = exchange([squared] * 4, "y")
     pieces = call(
-        back_kernel, "back", [struct(64, wide)] * 4, (*grad_pre, in_vmem(up_both)), scratch=[pltpu.VMEM((4, 64, 2 * hid), BF)], limit=12
+        back_kernel, "back", [struct(64, wide)] * 4, (*grad_pre, in_vmem(up_both)), scratch=[pltpu.VMEM((4, 64, 2 * hid), BF)], limit=12,
     )
     pieces = exchange(pieces, "x")
     blocks = add(pieces, 4, pieces[0])
@@ -288,12 +302,13 @@
         turn_kernel, "turn", [struct(2, hid, 256)] * 2, (*squared, *grad_pre, home[0]), ins=[False] * 8 + [True],
         scratch=[pltpu.VMEM((2, 4, 64, 2 * hid), BF)],
     )
+    both_other = other_core(copied(both, keep))
     grad_up, grad_down = call(
-        weights_kernel, "weight_grads", [struct(hid, wide)] * 2, (keep, other_core(send), i_rows, i_other, g_rows, g_other),
+        weights_kernel, "weight_grads", [struct(hid, wide)] * 2, (keep, other_core(send), both, both_other),
         outs=[pltpu.HBM] * 2, scratch=[pltpu.VMEM((hid, wide), BF), pltpu.VMEM((hid, wide), BF), pltpu.SemaphoreType.DMA((2, 3))],
         limit=24,
     )
-    half, other_half = add(home, 2, *in_hbm(grad_up))
+    half, other_half = add(home[:1] + home[:0:-1], 2, *in_hbm(grad_up))
     (grad_input,) = add([half, other_core(other_half)], 1, half)
     return (grad_input, grad_up, grad_down)
 

time: 119 us -> 114 us (0.958)
  waiting for transfers between devices: 51.4 us -> 43.1 us
  starting transfers between devices: 47.8 us -> 54.1 us
  Pallas kernels: 18.8 us -> 15.2 us
    ppermute x21, waiting for transfers between devices: 38.5 us -> 29.8 us  [xor_shift(): return lax.ppermute(array, axis, [(i, i ^ k) for i in range(4)])]
    ppermute x21, starting transfers between devices: 23.6 us -> 29 us  [xor_shift(): return lax.ppermute(array, axis, [(i, i ^ k) for i in range(4)])]
    pallas_call x14 -> x15, Pallas kernels: 18.8 us -> 15.2 us  [call(): pl.pallas_call(kernel, out_shape=tuple(out), in_specs=[any_spec() if a el...]
    ppermute x10, starting transfers between devices: 17.8 us -> 19 us  [on_cores(): return lax.ppermute(array, ('zl', 'core', 'zh'), pairs)]
    ppermute x6 -> x5, starting transfers between devices: 6.39 us -> 6.06 us  [other_core(): return lax.ppermute(array, 'core', [(0, 1), (1, 0)])]
  transfers between devices with their start and end apart: 37 -> 36, of which waited for: 22 -> 20; matrix products, arithmetic and copies ran while one was open for 0% -> 0% of each run, Pallas kernels for 13% -> 9%
where the time goes in v4:
time: 114 us; the launch traced here: 113 us
  starting transfers between devices  54.1 us (47%)
  waiting for transfers between devices  43.1 us (38%)
  Pallas kernels  15.2 us (13%)
    ppermute x21, waiting for transfers between devices, xor_shift(): return lax.ppermute(array, axis, [(i, i ^ k) for i in range(4)])  29.8 us
    ppermute x21, starting transfers between devices, xor_shift(): return lax.ppermute(array, axis, [(i, i ^ k) for i in range(4)])  29 us
    ppermute x10, starting transfers between devices, on_cores(): return lax.ppermute(array, ('zl', 'core', 'zh'), pairs)  19 us
    pallas_call x15, Pallas kernels, call(): pl.pallas_call(kernel, out_shape=tuple(out), in_specs=[any_spec() if a el...  15.2 us
    ppermute x10, waiting for transfers between devices, on_cores(): return lax.ppermute(array, ('zl', 'core', 'zh'), pairs)  12.1 us
    ppermute x5, starting transfers between devices, other_core(): return lax.ppermute(array, 'core', [(0, 1), (1, 0)])  6.06 us
  transfers between devices with their start and end apart: 36, of which 20 were waited for; matrix products, arithmetic and copies ran while one was open for 0% of the time, Pallas kernels for 9%

profile of v4, /device:TPU:1, one launch (start us, length us, event | category | flops | bytes accessed | tf_op | source)
XLA Modules:
  0.0 113.2 jit_solution(340233820255278480)
XLA Ops:
  0.6 3.3 %collective-permute-start.2 = (bf16[576,2304]{1,0:T(8,128)(2,1)}, bf16[576,2304]{1,0:T(8,128)(2,1)S(1)}, u32[]{:S(2)}, u32[]{:S(2)}) collective-permute-start(bf16[576,2304]{1,0:T(8,128)(2,1)} %up_own.1), channel_id=1, source_target_pairs={{0,32},{32,0},{1,33},{33,1},{2,34},{34,2},{3,35},{35,3},{4,36},{36... | collective-permute-start | bytes 7962632 | tf_op jit(solution)/shard_map/ppermute | solution.py:40
  5.1 5.7 %collective-permute-start = (bf16[16,2304]{1,0:T(8,128)(2,1)S(1)}, bf16[16,2304]{1,0:T(8,128)(2,1)S(1)}, u32[]{:S(2)}, u32[]{:S(2)}) collective-permute-start(bf16[16,2304]{1,0:T(8,128)(2,1)S(1)} %dequant.1), channel_id=1, source_target_pairs={{0,0},{32,225},{64,64},{96,32},{128,128},{160,96},{192,192},{224,1... | collective-permute-start | bytes 221192 | tf_op jit(solution)/shard_map/ppermute | solution.py:24
  12.2 2.4 %collective-permute-done.1.oth = bf16[16,2304]{1,0:T(8,128)(2,1)S(1)} collective-permute-done((bf16[16,2304]{1,0:T(8,128)(2,1)S(1)}, bf16[16,2304]{1,0:T(8,128)(2,1)S(1)}, u32[]{:S(2)}, u32[]{:S(2)}) %collective-permute-start.1) | collective-permute-done | bytes 73760 | tf_op jit(solution)/shard_map/ppermute | solution.py:24
  15.9 1.8 %collective-permute-start.4 = (bf16[16,2304]{1,0:T(8,128)(2,1)S(1)}, bf16[16,2304]{1,0:T(8,128)(2,1)S(1)}, u32[]{:S(2)}, u32[]{:S(2)}) collective-permute-start(bf16[16,2304]{1,0:T(8,128)(2,1)S(1)} %get-tuple-element.37.x0), channel_id=1, source_target_pairs={{0,6},{2,4},{4,2},{6,0},{1,7},{3,5},{5,3},{7,1},{8,14},{10,12},{12... | collective-permute-start | bytes 221192 | tf_op jit(solution)/shard_map/ppermute | solution.py:32
  18.4 1.9 %collective-permute-start.6 = (bf16[16,2304]{1,0:T(8,128)(2,1)S(1)}, bf16[16,2304]{1,0:T(8,128)(2,1)S(1)}, u32[]{:S(2)}, u32[]{:S(2)}) collective-permute-start(bf16[16,2304]{1,0:T(8,128)(2,1)S(1)} %get-tuple-element.38.g0), channel_id=1, source_target_pairs={{0,64},{32,225},{64,128},{96,32},{128,192},{160,96},{192,1},{224,1... | collective-permute-start | bytes 221192 | tf_op jit(solution)/shard_map/ppermute | solution.py:24
  21.3 1.9 %collective-permute-done.5.x3 = bf16[16,2304]{1,0:T(8,128)(2,1)S(1)} collective-permute-done((bf16[16,2304]{1,0:T(8,128)(2,1)S(1)}, bf16[16,2304]{1,0:T(8,128)(2,1)S(1)}, u32[]{:S(2)}, u32[]{:S(2)}) %collective-permute-start.5) | collective-permute-done | bytes 73760 | tf_op jit(solution)/shard_map/ppermute | solution.py:32
  25.6 1.8 %collective-permute-start.11 = (bf16[2,16,2304]{2,1,0:T(8,128)(2,1)S(1)}, bf16[2,16,2304]{2,1,0:T(8,128)(2,1)S(1)}, u32[]{:S(2)}, u32[]{:S(2)}) collective-permute-start(bf16[2,16,2304]{2,1,0:T(8,128)(2,1)S(1)} %get-tuple-element.40.refs_0_), channel_id=1, source_target_pairs={{0,6},{2,4},{4,2},{6,0},{1,7},{3,5},{5,3},{7,1},{8,14},{10,12},{12... | collective-permute-start | bytes 442376 | tf_op jit(solution)/shard_map/ppermute | solution.py:32
  27.5 3.0 %collective-permute-done.10._.refs_1_ = bf16[2,16,2304]{2,1,0:T(8,128)(2,1)S(1)} collective-permute-done((bf16[2,16,2304]{2,1,0:T(8,128)(2,1)S(1)}, bf16[2,16,2304]{2,1,0:T(8,128)(2,1)S(1)}, u32[]{:S(2)}, u32[]{:S(2)}) %collective-permute-start.10) | collective-permute-done | bytes 147488 | tf_op jit(solution)/shard_map/ppermute | solution.py:32
  30.5 2.0 %collective-permute-done.11.__.refs_2_ = bf16[2,16,2304]{2,1,0:T(8,128)(2,1)S(1)} collective-permute-done((bf16[2,16,2304]{2,1,0:T(8,128)(2,1)S(1)}, bf16[2,16,2304]{2,1,0:T(8,128)(2,1)S(1)}, u32[]{:S(2)}, u32[]{:S(2)}) %collective-permute-start.11) | collective-permute-done | bytes 147488 | tf_op jit(solution)/shard_map/ppermute | solution.py:32
  33.4 2.4 %collective-permute-start.12 = (bf16[2,4,16,2304]{3,2,1,0:T(8,128)(2,1)S(1)}, bf16[2,4,16,2304]{3,2,1,0:T(8,128)(2,1)S(1)}, u32[]{:S(2)}, u32[]{:S(2)}) collective-permute-start(bf16[2,4,16,2304]{3,2,1,0:T(8,128)(2,1)S(1)} %get-tuple-element.41.near), channel_id=1, source_target_pairs={{0,128},{32,161},{64,192},{96,225},{128,1},{160,32},{192,65},{224,... | collective-permute-start | bytes 1769480 | tf_op jit(solution)/shard_map/ppermute | solution.py:24
  35.8 2.3 %collective-permute-start.13 = (bf16[2,16,2304]{2,1,0:T(8,128)(2,1)S(1)}, bf16[2,16,2304]{2,1,0:T(8,128)(2,1)S(1)}, u32[]{:S(2)}, u32[]{:S(2)}) collective-permute-start(bf16[2,16,2304]{2,1,0:T(8,128)(2,1)S(1)} %get-tuple-element.40.refs_0_), channel_id=1, source_target_pairs={{0,4},{2,6},{4,0},{6,2},{1,5},{3,7},{5,1},{7,3},{8,12},{10,14},{12... | collective-permute-start | bytes 442376 | tf_op jit(solution)/shard_map/ppermute | solution.py:32
  39.1 2.3 %collective-permute-start.16 = (bf16[2,16,2304]{2,1,0:T(8,128)(2,1)S(1)}, bf16[2,16,2304]{2,1,0:T(8,128)(2,1)S(1)}, u32[]{:S(2)}, u32[]{:S(2)}) collective-permute-start(bf16[2,16,2304]{2,1,0:T(8,128)(2,1)S(1)} %get-tuple-element.43.refs_4_), channel_id=1, source_target_pairs={{0,4},{2,6},{4,0},{6,2},{1,5},{3,7},{5,1},{7,3},{8,12},{10,14},{12... | collective-permute-start | bytes 442376 | tf_op jit(solution)/shard_map/ppermute | solution.py:32
  41.4 2.6 %join.1 = (bf16[1152,2304]{1,0:T(8,128)(2,1)S(1)}, bf16[1152,2304]{1,0:T(8,128)(2,1)S(1)}) custom-call(bf16[576,2304]{1,0:T(8,128)(2,1)} %up_own.1, bf16[576,2304]{1,0:T(8,128)(2,1)S(1)} %collective-permute-done.2._.up_oth, bf16[576,2304]{1,0:T(8,128)(2,1)} %down_own.1, bf16[576,2304]{1,0:T(8,128)(2,1)S(1)} %collective-permute-done.7._.down_oth, ...), custom_call_target="tpu_custom_call" | custom-call | flops 1 | bytes 1 | tf_op jit(solution)/shard_map/join/pallas_call | solution.py:62
  44.1 1.9 %collective-permute-done.14.refs_5_ = bf16[2,16,2304]{2,1,0:T(8,128)(2,1)S(1)} collective-permute-done((bf16[2,16,2304]{2,1,0:T(8,128)(2,1)S(1)}, bf16[2,16,2304]{2,1,0:T(8,128)(2,1)S(1)}, u32[]{:S(2)}, u32[]{:S(2)}) %collective-permute-start.14) | collective-permute-done | bytes 147488 | tf_op jit(solution)/shard_map/ppermute | solution.py:32
  48.2 2.1 %grads.1 = (f32[64,1152]{1,0:T(8,128)S(1)}, bf16[64,1152]{1,0:T(8,128)(2,1)S(1)}, bf16[64,1152]{1,0:T(8,128)(2,1)S(1)}, bf16[64,1152]{1,0:T(8,128)(2,1)S(1)}, bf16[4,4,16,2304]{3,2,1,0:T(8,128)(2,1)S(1)}) custom-call(bf16[2,16,2304]{2,1,0:T(8,128)(2,1)S(1)} %get-tuple-element.40.refs_0_, bf16[2,16,2304]{2,1,0:T(8,128)(2,1)S(1)} %collective-permute-done.10._.refs_1_, ...), custom_call_target="tpu_custom_call" | custom-call | flops 1 | bytes 1 | tf_op jit(solution)/shard_map/grads/pallas_call | solution.py:62
  50.3 2.2 %inputs.1 = (f32[2,64,1152]{2,1,0:T(8,128)S(1)}, bf16[2,64,1152]{2,1,0:T(8,128)(2,1)S(1)}, bf16[2,64,1152]{2,1,0:T(8,128)(2,1)S(1)}, bf16[2,64,1152]{2,1,0:T(8,128)(2,1)S(1)}, bf16[2,4,4,16,2304]{4,3,2,1,0:T(8,128)(2,1)S(1)}) custom-call(bf16[2,4,16,2304]{3,2,1,0:T(8,128)(2,1)S(1)} %get-tuple-element.41.near, ...), custom_call_target="tpu_custom_call" | custom-call | flops 1 | bytes 1 | tf_op jit(solution)/shard_map/inputs/pallas_call | solution.py:62
  53.9 1.9 %collective-permute-start.18 = (bf16[2,64,1152]{2,1,0:T(8,128)(2,1)S(1)}, bf16[2,64,1152]{2,1,0:T(8,128)(2,1)S(1)}, u32[]{:S(2)}, u32[]{:S(2)}) collective-permute-start(bf16[2,64,1152]{2,1,0:T(8,128)(2,1)S(1)} %get-tuple-element.52), channel_id=1, source_target_pairs={{0,24},{8,16},{16,8},{24,0},{1,25},{9,17},{17,9},{25,1},{2,26},{10... | collective-permute-start | bytes 884744 | tf_op jit(solution)/shard_map/ppermute | solution.py:32
  58.2 5.1 %collective-permute-done.18.r2 = bf16[2,64,1152]{2,1,0:T(8,128)(2,1)S(1)} collective-permute-done((bf16[2,64,1152]{2,1,0:T(8,128)(2,1)S(1)}, bf16[2,64,1152]{2,1,0:T(8,128)(2,1)S(1)}, u32[]{:S(2)}, u32[]{:S(2)}) %collective-permute-start.18) | collective-permute-done | bytes 294944 | tf_op jit(solution)/shard_map/ppermute | solution.py:32
  63.3 2.0 %collective-permute-done.19.r3 = bf16[2,64,1152]{2,1,0:T(8,128)(2,1)S(1)} collective-permute-done((bf16[2,64,1152]{2,1,0:T(8,128)(2,1)S(1)}, bf16[2,64,1152]{2,1,0:T(8,128)(2,1)S(1)}, u32[]{:S(2)}, u32[]{:S(2)}) %collective-permute-start.19) | collective-permute-done | bytes 294944 | tf_op jit(solution)/shard_map/ppermute | solution.py:32
  67.2 1.6 %collective-permute-start.22 = (bf16[64,1152]{1,0:T(8,128)(2,1)S(1)}, bf16[64,1152]{1,0:T(8,128)(2,1)S(1)}, u32[]{:S(2)}, u32[]{:S(2)}) collective-permute-start(bf16[64,1152]{1,0:T(8,128)(2,1)S(1)} %get-tuple-element.54.p0.refs_4_), channel_id=1, source_target_pairs={{0,16},{8,24},{16,0},{24,8},{1,17},{9,25},{17,1},{25,9},{2,18},{10... | collective-permute-start | bytes 442376 | tf_op jit(solution)/shard_map/ppermute | solution.py:32
  69.9 3.6 %collective-permute-done.21.p2.refs_6_ = bf16[64,1152]{1,0:T(8,128)(2,1)S(1)} collective-permute-done((bf16[64,1152]{1,0:T(8,128)(2,1)S(1)}, bf16[64,1152]{1,0:T(8,128)(2,1)S(1)}, u32[]{:S(2)}, u32[]{:S(2)}) %collective-permute-start.21) | collective-permute-done | bytes 147488 | tf_op jit(solution)/shard_map/ppermute | solution.py:32
  73.5 1.7 %back.1 = (bf16[64,2304]{1,0:T(8,128)(2,1)S(1)}, bf16[64,2304]{1,0:T(8,128)(2,1)S(1)}, bf16[64,2304]{1,0:T(8,128)(2,1)S(1)}, bf16[64,2304]{1,0:T(8,128)(2,1)S(1)}) custom-call(bf16[64,1152]{1,0:T(8,128)(2,1)S(1)} %get-tuple-element.54.p0.refs_4_, bf16[64,1152]{1,0:T(8,128)(2,1)S(1)} %collective-permute-done.20.p1.refs_5_, ...), custom_call_target="tpu_custom_call" | custom-call | flops 1 | bytes 1 | tf_op jit(solution)/shard_map/back/pallas_call | solution.py:62
  75.2 1.9 %collective-permute-start.23 = (bf16[64,2304]{1,0:T(8,128)(2,1)S(1)}, bf16[64,2304]{1,0:T(8,128)(2,1)S(1)}, u32[]{:S(2)}, u32[]{:S(2)}) collective-permute-start(bf16[64,2304]{1,0:T(8,128)(2,1)S(1)} %get-tuple-element.56), channel_id=1, source_target_pairs={{0,2},{2,0},{4,6},{6,4},{1,3},{3,1},{5,7},{7,5},{8,10},{10,8},{12,... | collective-permute-start | bytes 884744 | tf_op jit(solution)/shard_map/ppermute | solution.py:32
  77.1 3.8 %collective-permute-start.24 = (bf16[64,2304]{1,0:T(8,128)(2,1)S(1)}, bf16[64,2304]{1,0:T(8,128)(2,1)S(1)}, u32[]{:S(2)}, u32[]{:S(2)}) collective-permute-start(bf16[64,2304]{1,0:T(8,128)(2,1)S(1)} %get-tuple-element.57), channel_id=1, source_target_pairs={{0,6},{2,4},{4,2},{6,0},{1,7},{3,5},{5,3},{7,1},{8,14},{10,12},{12... | collective-permute-start | bytes 884744 | tf_op jit(solution)/shard_map/ppermute | solution.py:32
  81.5 3.3 %collective-permute-start.31 = (bf16[64,1152]{1,0:T(8,128)(2,1)S(1)}, bf16[64,1152]{1,0:T(8,128)(2,1)S(1)}, u32[]{:S(2)}, u32[]{:S(2)}) collective-permute-start(bf16[64,1152]{1,0:T(8,128)(2,1)S(1)} %get-tuple-element.63.refs_0_), channel_id=1, source_target_pairs={{0,24},{8,16},{16,8},{24,0},{1,25},{9,17},{17,9},{25,1},{2,26},{10... | collective-permute-start | bytes 442376 | tf_op jit(solution)/shard_map/ppermute | solution.py:32
  84.8 3.6 %collective-permute-done.24.refs_2_ = bf16[64,2304]{1,0:T(8,128)(2,1)S(1)} collective-permute-done((bf16[64,2304]{1,0:T(8,128)(2,1)S(1)}, bf16[64,2304]{1,0:T(8,128)(2,1)S(1)}, u32[]{:S(2)}, u32[]{:S(2)}) %collective-permute-start.24) | collective-permute-done | bytes 294944 | tf_op jit(solution)/shard_map/ppermute | solution.py:32
  89.3 1.9 %collective-permute-start.26 = (bf16[16,2304]{1,0:T(8,128)(2,1)S(1)}, bf16[16,2304]{1,0:T(8,128)(2,1)S(1)}, u32[]{:S(2)}, u32[]{:S(2)}) collective-permute-start(bf16[16,2304]{1,0:T(8,128)(2,1)S(1)} %get-tuple-element.59), channel_id=1, source_target_pairs={{0,0},{32,96},{64,64},{96,160},{128,128},{160,224},{192,192},{224,... | collective-permute-start | bytes 221192 | tf_op jit(solution)/shard_map/ppermute | solution.py:24
  91.2 4.6 %collective-permute-done.26.refs_8_.refs_0_ = bf16[16,2304]{1,0:T(8,128)(2,1)S(1)} collective-permute-done((bf16[16,2304]{1,0:T(8,128)(2,1)S(1)}, bf16[16,2304]{1,0:T(8,128)(2,1)S(1)}, u32[]{:S(2)}, u32[]{:S(2)}) %collective-permute-start.26) | collective-permute-done | bytes 73760 | tf_op jit(solution)/shard_map/ppermute | solution.py:24
  96.5 2.4 %collective-permute-start.34 = (bf16[2,4,4,16,2304]{4,3,2,1,0:T(8,128)(2,1)S(1)}, bf16[2,4,4,16,2304]{4,3,2,1,0:T(8,128)(2,1)S(1)}, u32[]{:S(2)}, u32[]{:S(2)}) collective-permute-start(bf16[2,4,4,16,2304]{4,3,2,1,0:T(8,128)(2,1)S(1)} %copied.1), channel_id=1, source_target_pairs={{0,32},{32,0},{1,33},{33,1},{2,34},{34,2},{3,35},{35,3},{4,36},{36... | collective-permute-start | bytes 7077896 | tf_op jit(solution)/shard_map/ppermute | solution.py:40
  99.1 5.5 %collective-permute-start.27 = (bf16[16,2304]{1,0:T(8,128)(2,1)S(1)}, bf16[16,2304]{1,0:T(8,128)(2,1)S(1)}, u32[]{:S(2)}, u32[]{:S(2)}) collective-permute-start(bf16[16,2304]{1,0:T(8,128)(2,1)S(1)} %get-tuple-element.60), channel_id=1, source_target_pairs={{0,65},{32,33},{64,129},{96,97},{128,193},{160,161},{192,0},{224,2... | collective-permute-start | bytes 221192 | tf_op jit(solution)/shard_map/ppermute | solution.py:24
  104.6 3.9 %weight_grads.1 = (bf16[576,2304]{1,0:T(8,128)(2,1)}, bf16[576,2304]{1,0:T(8,128)(2,1)}) custom-call(bf16[2,576,256]{2,1,0:T(8,128)(2,1)S(1)} %get-tuple-element.64._.keep, bf16[2,576,256]{2,1,0:T(8,128)(2,1)S(1)} %collective-permute-done.33.came, bf16[2,4,4,16,2304]{4,3,2,1,0:T(8,128)(2,1)S(1)} %get-tuple-element.66.src.own, ...), custom_call_target="tpu_custom_call" | custom-call | flops 1 | bytes 1 | tf_op jit(solution)/shard_map/weight_grads/pallas_call | solution.py:62
  108.5 2.8 %collective-permute-done.28.refs_2_ = bf16[16,2304]{1,0:T(8,128)(2,1)S(1)} collective-permute-done((bf16[16,2304]{1,0:T(8,128)(2,1)S(1)}, bf16[16,2304]{1,0:T(8,128)(2,1)S(1)}, u32[]{:S(2)}, u32[]{:S(2)}) %collective-permute-start.28) | collective-permute-done | bytes 73760 | tf_op jit(solution)/shard_map/ppermute | solution.py:24
  (55 shorter events, 22.7 us)
Async XLA Ops:
  0.6 14.0 %collective-permute-start.2 = (bf16[576,2304]{1,0:T(8,128)(2,1)}, bf16[576,2304]{1,0:T(8,128)(2,1)S(1)}, u32[]{:S(2)}, u32[]{:S(2)}) collective-permute-start(bf16[576,2304]{1,0:T(8,128)(2,1)} %up_own.1), channel_id=1, source_target_pairs={{0,32},{32,0},{1,33},{33,1},{2,34},{34,2},{3,35},{35,3},{4,36},{36... | collective-permute-start | bytes 7962632 | tf_op jit(solution)/shard_map/ppermute | solution.py:40
  4.0 16.4 %collective-permute-start.7 = (bf16[576,2304]{1,0:T(8,128)(2,1)}, bf16[576,2304]{1,0:T(8,128)(2,1)S(1)}, u32[]{:S(2)}, u32[]{:S(2)}) collective-permute-start(bf16[576,2304]{1,0:T(8,128)(2,1)} %down_own.1), channel_id=1, source_target_pairs={{0,32},{32,0},{1,33},{33,1},{2,34},{34,2},{3,35},{35,3},{4,36},{36... | collective-permute-start | bytes 7962632 | tf_op jit(solution)/shard_map/ppermute | solution.py:40
  5.1 7.1 %collective-permute-start = (bf16[16,2304]{1,0:T(8,128)(2,1)S(1)}, bf16[16,2304]{1,0:T(8,128)(2,1)S(1)}, u32[]{:S(2)}, u32[]{:S(2)}) collective-permute-start(bf16[16,2304]{1,0:T(8,128)(2,1)S(1)} %dequant.1), channel_id=1, source_target_pairs={{0,0},{32,225},{64,64},{96,32},{128,128},{160,96},{192,192},{224,1... | collective-permute-start | bytes 221192 | tf_op jit(solution)/shard_map/ppermute | solution.py:24
  14.6 5.7 %collective-permute-start.3 = (bf16[16,2304]{1,0:T(8,128)(2,1)S(1)}, bf16[16,2304]{1,0:T(8,128)(2,1)S(1)}, u32[]{:S(2)}, u32[]{:S(2)}) collective-permute-start(bf16[16,2304]{1,0:T(8,128)(2,1)S(1)} %get-tuple-element.37.x0), channel_id=1, source_target_pairs={{0,2},{2,0},{4,6},{6,4},{1,3},{3,1},{5,7},{7,5},{8,10},{10,8},{12,... | collective-permute-start | bytes 221192 | tf_op jit(solution)/shard_map/ppermute | solution.py:32
  15.9 5.4 %collective-permute-start.4 = (bf16[16,2304]{1,0:T(8,128)(2,1)S(1)}, bf16[16,2304]{1,0:T(8,128)(2,1)S(1)}, u32[]{:S(2)}, u32[]{:S(2)}) collective-permute-start(bf16[16,2304]{1,0:T(8,128)(2,1)S(1)} %get-tuple-element.37.x0), channel_id=1, source_target_pairs={{0,6},{2,4},{4,2},{6,0},{1,7},{3,5},{5,3},{7,1},{8,14},{10,12},{12... | collective-permute-start | bytes 221192 | tf_op jit(solution)/shard_map/ppermute | solution.py:32
  17.7 5.5 %collective-permute-start.5 = (bf16[16,2304]{1,0:T(8,128)(2,1)S(1)}, bf16[16,2304]{1,0:T(8,128)(2,1)S(1)}, u32[]{:S(2)}, u32[]{:S(2)}) collective-permute-start(bf16[16,2304]{1,0:T(8,128)(2,1)S(1)} %get-tuple-element.37.x0), channel_id=1, source_target_pairs={{0,4},{2,6},{4,0},{6,2},{1,5},{3,7},{5,1},{7,3},{8,12},{10,14},{12... | collective-permute-start | bytes 221192 | tf_op jit(solution)/shard_map/ppermute | solution.py:32
  23.3 10.1 %collective-permute-start.8 = (bf16[4,16,2304]{2,1,0:T(8,128)(2,1)S(1)}, bf16[4,16,2304]{2,1,0:T(8,128)(2,1)S(1)}, u32[]{:S(2)}, u32[]{:S(2)}) collective-permute-start(bf16[4,16,2304]{2,1,0:T(8,128)(2,1)S(1)} %get-tuple-element.39.row._), channel_id=1, source_target_pairs={{0,64},{32,225},{64,128},{96,32},{128,192},{160,96},{192,1},{224,1... | collective-permute-start | bytes 884744 | tf_op jit(solution)/shard_map/ppermute | solution.py:24
  24.8 5.6 %collective-permute-start.10 = (bf16[2,16,2304]{2,1,0:T(8,128)(2,1)S(1)}, bf16[2,16,2304]{2,1,0:T(8,128)(2,1)S(1)}, u32[]{:S(2)}, u32[]{:S(2)}) collective-permute-start(bf16[2,16,2304]{2,1,0:T(8,128)(2,1)S(1)} %get-tuple-element.40.refs_0_), channel_id=1, source_target_pairs={{0,2},{2,0},{4,6},{6,4},{1,3},{3,1},{5,7},{7,5},{8,10},{10,8},{12,... | collective-permute-start | bytes 442376 | tf_op jit(solution)/shard_map/ppermute | solution.py:32
  25.6 6.9 %collective-permute-start.11 = (bf16[2,16,2304]{2,1,0:T(8,128)(2,1)S(1)}, bf16[2,16,2304]{2,1,0:T(8,128)(2,1)S(1)}, u32[]{:S(2)}, u32[]{:S(2)}) collective-permute-start(bf16[2,16,2304]{2,1,0:T(8,128)(2,1)S(1)} %get-tuple-element.40.refs_0_), channel_id=1, source_target_pairs={{0,6},{2,4},{4,2},{6,0},{1,7},{3,5},{5,3},{7,1},{8,14},{10,12},{12... | collective-permute-start | bytes 442376 | tf_op jit(solution)/shard_map/ppermute | solution.py:32
  27.5 5.9 %collective-permute-start.9 = (bf16[2,16,2304]{2,1,0:T(8,128)(2,1)S(1)}, bf16[2,16,2304]{2,1,0:T(8,128)(2,1)S(1)}, u32[]{:S(2)}, u32[]{:S(2)}) collective-permute-start(bf16[2,16,2304]{2,1,0:T(8,128)(2,1)S(1)} %get-tuple-element.40.refs_0_), channel_id=1, source_target_pairs={{0,128},{32,161},{64,192},{96,225},{128,1},{160,32},{192,65},{224,... | collective-permute-start | bytes 442376 | tf_op jit(solution)/shard_map/ppermute | solution.py:24
  33.4 16.9 %collective-permute-start.12 = (bf16[2,4,16,2304]{3,2,1,0:T(8,128)(2,1)S(1)}, bf16[2,4,16,2304]{3,2,1,0:T(8,128)(2,1)S(1)}, u32[]{:S(2)}, u32[]{:S(2)}) collective-permute-start(bf16[2,4,16,2304]{3,2,1,0:T(8,128)(2,1)S(1)} %get-tuple-element.41.near), channel_id=1, source_target_pairs={{0,128},{32,161},{64,192},{96,225},{128,1},{160,32},{192,65},{224,... | collective-permute-start | bytes 1769480 | tf_op jit(solution)/shard_map/ppermute | solution.py:24
  35.8 8.2 %collective-permute-start.13 = (bf16[2,16,2304]{2,1,0:T(8,128)(2,1)S(1)}, bf16[2,16,2304]{2,1,0:T(8,128)(2,1)S(1)}, u32[]{:S(2)}, u32[]{:S(2)}) collective-permute-start(bf16[2,16,2304]{2,1,0:T(8,128)(2,1)S(1)} %get-tuple-element.40.refs_0_), channel_id=1, source_target_pairs={{0,4},{2,6},{4,0},{6,2},{1,5},{3,7},{5,1},{7,3},{8,12},{10,14},{12... | collective-permute-start | bytes 442376 | tf_op jit(solution)/shard_map/ppermute | solution.py:32
  38.2 7.8 %collective-permute-start.14 = (bf16[2,16,2304]{2,1,0:T(8,128)(2,1)S(1)}, bf16[2,16,2304]{2,1,0:T(8,128)(2,1)S(1)}, u32[]{:S(2)}, u32[]{:S(2)}) collective-permute-start(bf16[2,16,2304]{2,1,0:T(8,128)(2,1)S(1)} %get-tuple-element.43.refs_4_), channel_id=1, source_target_pairs={{0,2},{2,0},{4,6},{6,4},{1,3},{3,1},{5,7},{7,5},{8,10},{10,8},{12,... | collective-permute-start | bytes 442376 | tf_op jit(solution)/shard_map/ppermute | solution.py:32
  38.5 9.0 %collective-permute-start.15 = (bf16[2,16,2304]{2,1,0:T(8,128)(2,1)S(1)}, bf16[2,16,2304]{2,1,0:T(8,128)(2,1)S(1)}, u32[]{:S(2)}, u32[]{:S(2)}) collective-permute-start(bf16[2,16,2304]{2,1,0:T(8,128)(2,1)S(1)} %get-tuple-element.43.refs_4_), channel_id=1, source_target_pairs={{0,6},{2,4},{4,2},{6,0},{1,7},{3,5},{5,3},{7,1},{8,14},{10,12},{12... | collective-permute-start | bytes 442376 | tf_op jit(solution)/shard_map/ppermute | solution.py:32
  39.1 9.1 %collective-permute-start.16 = (bf16[2,16,2304]{2,1,0:T(8,128)(2,1)S(1)}, bf16[2,16,2304]{2,1,0:T(8,128)(2,1)S(1)}, u32[]{:S(2)}, u32[]{:S(2)}) collective-permute-start(bf16[2,16,2304]{2,1,0:T(8,128)(2,1)S(1)} %get-tuple-element.43.refs_4_), channel_id=1, source_target_pairs={{0,4},{2,6},{4,0},{6,2},{1,5},{3,7},{5,1},{7,3},{8,12},{10,14},{12... | collective-permute-start | bytes 442376 | tf_op jit(solution)/shard_map/ppermute | solution.py:32
  52.5 5.7 %collective-permute-start.17 = (bf16[2,64,1152]{2,1,0:T(8,128)(2,1)S(1)}, bf16[2,64,1152]{2,1,0:T(8,128)(2,1)S(1)}, u32[]{:S(2)}, u32[]{:S(2)}) collective-permute-start(bf16[2,64,1152]{2,1,0:T(8,128)(2,1)S(1)} %get-tuple-element.51), channel_id=1, source_target_pairs={{0,8},{8,0},{16,24},{24,16},{1,9},{9,1},{17,25},{25,17},{2,10},{10... | collective-permute-start | bytes 884744 | tf_op jit(solution)/shard_map/ppermute | solution.py:32
  53.9 9.4 %collective-permute-start.18 = (bf16[2,64,1152]{2,1,0:T(8,128)(2,1)S(1)}, bf16[2,64,1152]{2,1,0:T(8,128)(2,1)S(1)}, u32[]{:S(2)}, u32[]{:S(2)}) collective-permute-start(bf16[2,64,1152]{2,1,0:T(8,128)(2,1)S(1)} %get-tuple-element.52), channel_id=1, source_target_pairs={{0,24},{8,16},{16,8},{24,0},{1,25},{9,17},{17,9},{25,1},{2,26},{10... | collective-permute-start | bytes 884744 | tf_op jit(solution)/shard_map/ppermute | solution.py:32
  55.8 9.5 %collective-permute-start.19 = (bf16[2,64,1152]{2,1,0:T(8,128)(2,1)S(1)}, bf16[2,64,1152]{2,1,0:T(8,128)(2,1)S(1)}, u32[]{:S(2)}, u32[]{:S(2)}) collective-permute-start(bf16[2,64,1152]{2,1,0:T(8,128)(2,1)S(1)} %get-tuple-element.53), channel_id=1, source_target_pairs={{0,16},{8,24},{16,0},{24,8},{1,17},{9,25},{17,1},{25,9},{2,18},{10... | collective-permute-start | bytes 884744 | tf_op jit(solution)/shard_map/ppermute | solution.py:32
  65.6 7.9 %collective-permute-start.21 = (bf16[64,1152]{1,0:T(8,128)(2,1)S(1)}, bf16[64,1152]{1,0:T(8,128)(2,1)S(1)}, u32[]{:S(2)}, u32[]{:S(2)}) collective-permute-start(bf16[64,1152]{1,0:T(8,128)(2,1)S(1)} %get-tuple-element.54.p0.refs_4_), channel_id=1, source_target_pairs={{0,24},{8,16},{16,8},{24,0},{1,25},{9,17},{17,9},{25,1},{2,26},{10... | collective-permute-start | bytes 442376 | tf_op jit(solution)/shard_map/ppermute | solution.py:32
  67.2 6.3 %collective-permute-start.22 = (bf16[64,1152]{1,0:T(8,128)(2,1)S(1)}, bf16[64,1152]{1,0:T(8,128)(2,1)S(1)}, u32[]{:S(2)}, u32[]{:S(2)}) collective-permute-start(bf16[64,1152]{1,0:T(8,128)(2,1)S(1)} %get-tuple-element.54.p0.refs_4_), channel_id=1, source_target_pairs={{0,16},{8,24},{16,0},{24,8},{1,17},{9,25},{17,1},{25,9},{2,18},{10... | collective-permute-start | bytes 442376 | tf_op jit(solution)/shard_map/ppermute | solution.py:32
  75.2 9.6 %collective-permute-start.23 = (bf16[64,2304]{1,0:T(8,128)(2,1)S(1)}, bf16[64,2304]{1,0:T(8,128)(2,1)S(1)}, u32[]{:S(2)}, u32[]{:S(2)}) collective-permute-start(bf16[64,2304]{1,0:T(8,128)(2,1)S(1)} %get-tuple-element.56), channel_id=1, source_target_pairs={{0,2},{2,0},{4,6},{6,4},{1,3},{3,1},{5,7},{7,5},{8,10},{10,8},{12,... | collective-permute-start | bytes 884744 | tf_op jit(solution)/shard_map/ppermute | solution.py:32
  77.1 11.3 %collective-permute-start.24 = (bf16[64,2304]{1,0:T(8,128)(2,1)S(1)}, bf16[64,2304]{1,0:T(8,128)(2,1)S(1)}, u32[]{:S(2)}, u32[]{:S(2)}) collective-permute-start(bf16[64,2304]{1,0:T(8,128)(2,1)S(1)} %get-tuple-element.57), channel_id=1, source_target_pairs={{0,6},{2,4},{4,2},{6,0},{1,7},{3,5},{5,3},{7,1},{8,14},{10,12},{12... | collective-permute-start | bytes 884744 | tf_op jit(solution)/shard_map/ppermute | solution.py:32
  81.0 8.2 %collective-permute-start.25 = (bf16[64,2304]{1,0:T(8,128)(2,1)S(1)}, bf16[64,2304]{1,0:T(8,128)(2,1)S(1)}, u32[]{:S(2)}, u32[]{:S(2)}) collective-permute-start(bf16[64,2304]{1,0:T(8,128)(2,1)S(1)} %get-tuple-element.58), channel_id=1, source_target_pairs={{0,4},{2,6},{4,0},{6,2},{1,5},{3,7},{5,1},{7,3},{8,12},{10,14},{12... | collective-permute-start | bytes 884744 | tf_op jit(solution)/shard_map/ppermute | solution.py:32
  81.2 10.0 %collective-permute-start.30 = (bf16[64,1152]{1,0:T(8,128)(2,1)S(1)}, bf16[64,1152]{1,0:T(8,128)(2,1)S(1)}, u32[]{:S(2)}, u32[]{:S(2)}) collective-permute-start(bf16[64,1152]{1,0:T(8,128)(2,1)S(1)} %get-tuple-element.63.refs_0_), channel_id=1, source_target_pairs={{0,8},{8,0},{16,24},{24,16},{1,9},{9,1},{17,25},{25,17},{2,10},{10... | collective-permute-start | bytes 442376 | tf_op jit(solution)/shard_map/ppermute | solution.py:32
  81.5 9.7 %collective-permute-start.31 = (bf16[64,1152]{1,0:T(8,128)(2,1)S(1)}, bf16[64,1152]{1,0:T(8,128)(2,1)S(1)}, u32[]{:S(2)}, u32[]{:S(2)}) collective-permute-start(bf16[64,1152]{1,0:T(8,128)(2,1)S(1)} %get-tuple-element.63.refs_0_), channel_id=1, source_target_pairs={{0,24},{8,16},{16,8},{24,0},{1,25},{9,17},{17,9},{25,1},{2,26},{10... | collective-permute-start | bytes 442376 | tf_op jit(solution)/shard_map/ppermute | solution.py:32
  84.8 6.4 %collective-permute-start.32 = (bf16[64,1152]{1,0:T(8,128)(2,1)S(1)}, bf16[64,1152]{1,0:T(8,128)(2,1)S(1)}, u32[]{:S(2)}, u32[]{:S(2)}) collective-permute-start(bf16[64,1152]{1,0:T(8,128)(2,1)S(1)} %get-tuple-element.63.refs_0_), channel_id=1, source_target_pairs={{0,16},{8,24},{16,0},{24,8},{1,17},{9,25},{17,1},{25,9},{2,18},{10... | collective-permute-start | bytes 442376 | tf_op jit(solution)/shard_map/ppermute | solution.py:32
  89.3 6.6 %collective-permute-start.26 = (bf16[16,2304]{1,0:T(8,128)(2,1)S(1)}, bf16[16,2304]{1,0:T(8,128)(2,1)S(1)}, u32[]{:S(2)}, u32[]{:S(2)}) collective-permute-start(bf16[16,2304]{1,0:T(8,128)(2,1)S(1)} %get-tuple-element.59), channel_id=1, source_target_pairs={{0,0},{32,96},{64,64},{96,160},{128,128},{160,224},{192,192},{224,... | collective-permute-start | bytes 221192 | tf_op jit(solution)/shard_map/ppermute | solution.py:24
  96.5 8.1 %collective-permute-start.34 = (bf16[2,4,4,16,2304]{4,3,2,1,0:T(8,128)(2,1)S(1)}, bf16[2,4,4,16,2304]{4,3,2,1,0:T(8,128)(2,1)S(1)}, u32[]{:S(2)}, u32[]{:S(2)}) collective-permute-start(bf16[2,4,4,16,2304]{4,3,2,1,0:T(8,128)(2,1)S(1)} %copied.1), channel_id=1, source_target_pairs={{0,32},{32,0},{1,33},{33,1},{2,34},{34,2},{3,35},{35,3},{4,36},{36... | collective-permute-start | bytes 7077896 | tf_op jit(solution)/shard_map/ppermute | solution.py:40
  99.0 5.6 %collective-permute-start.33 = (bf16[2,576,256]{2,1,0:T(8,128)(2,1)S(1)}, bf16[2,576,256]{2,1,0:T(8,128)(2,1)S(1)}, u32[]{:S(2)}, u32[]{:S(2)}) collective-permute-start(bf16[2,576,256]{2,1,0:T(8,128)(2,1)S(1)} %get-tuple-element.65), channel_id=1, source_target_pairs={{0,32},{32,0},{1,33},{33,1},{2,34},{34,2},{3,35},{35,3},{4,36},{36... | collective-permute-start | bytes 1769480 | tf_op jit(solution)/shard_map/ppermute | solution.py:40
  99.1 9.4 %collective-permute-start.27 = (bf16[16,2304]{1,0:T(8,128)(2,1)S(1)}, bf16[16,2304]{1,0:T(8,128)(2,1)S(1)}, u32[]{:S(2)}, u32[]{:S(2)}) collective-permute-start(bf16[16,2304]{1,0:T(8,128)(2,1)S(1)} %get-tuple-element.60), channel_id=1, source_target_pairs={{0,65},{32,33},{64,129},{96,97},{128,193},{160,161},{192,0},{224,2... | collective-permute-start | bytes 221192 | tf_op jit(solution)/shard_map/ppermute | solution.py:24
  104.6 6.7 %collective-permute-start.28 = (bf16[16,2304]{1,0:T(8,128)(2,1)S(1)}, bf16[16,2304]{1,0:T(8,128)(2,1)S(1)}, u32[]{:S(2)}, u32[]{:S(2)}) collective-permute-start(bf16[16,2304]{1,0:T(8,128)(2,1)S(1)} %get-tuple-element.61), channel_id=1, source_target_pairs={{0,129},{32,224},{64,193},{96,33},{128,0},{160,97},{192,64},{224,1... | collective-permute-start | bytes 221192 | tf_op jit(solution)/shard_map/ppermute | solution.py:24
  104.6 6.7 %collective-permute-start.29 = (bf16[16,2304]{1,0:T(8,128)(2,1)S(1)}, bf16[16,2304]{1,0:T(8,128)(2,1)S(1)}, u32[]{:S(2)}, u32[]{:S(2)}) collective-permute-start(bf16[16,2304]{1,0:T(8,128)(2,1)S(1)} %get-tuple-element.62), channel_id=1, source_target_pairs={{0,193},{32,160},{64,0},{96,224},{128,64},{160,33},{192,128},{224,... | collective-permute-start | bytes 221192 | tf_op jit(solution)/shard_map/ppermute | solution.py:24
  (4 other events, 14.4 us)

commit v5 on v4

--- a/solution.py
+++ b/solution.py
@@ -299,7 +299,7 @@
     blocks = add(pieces, 4, pieces[0])
     home = [z_shift(block, -t, 1 + t) for t, block in enumerate(blocks)]
     keep, send = call(
-        turn_kernel, "turn", [struct(2, hid, 256)] * 2, (*squared, *grad_pre, home[0]), ins=[False] * 8 + [True],
+        turn_kernel, "turn", [struct(2, hid, 256)] * 2, (*squared, *grad_pre, blocks[0]), ins=[False] * 8 + [True],
         scratch=[pltpu.VMEM((2, 4, 64, 2 * hid), BF)],
     )
     both_other = other_core(copied(both, keep))

time: 114 us -> 114 us (level)
  starting transfers between devices: 54.1 us -> 59.8 us
  waiting for transfers between devices: 43.1 us -> 38.3 us
    ppermute x10, waiting for transfers between devices: 12.1 us -> 6.23 us  [on_cores(): return lax.ppermute(array, ('zl', 'core', 'zh'), pairs)]
    ppermute x5, starting transfers between devices: 6.06 us -> 11.6 us  [other_core(): return lax.ppermute(array, 'core', [(0, 1), (1, 0)])]
where the time goes in v5:
time: 114 us
  starting transfers between devices  59.8 us (52%)
  waiting for transfers between devices  38.3 us (34%)
  Pallas kernels  15.2 us (13%)
    ppermute x21, waiting for transfers between devices, xor_shift(): return lax.ppermute(array, axis, [(i, i ^ k) for i in range(4)])  30.8 us
    ppermute x21, starting transfers between devices, xor_shift(): return lax.ppermute(array, axis, [(i, i ^ k) for i in range(4)])  29 us
    ppermute x10, starting transfers between devices, on_cores(): return lax.ppermute(array, ('zl', 'core', 'zh'), pairs)  19.2 us
    pallas_call x15, Pallas kernels, call(): pl.pallas_call(kernel, out_shape=tuple(out), in_specs=[any_spec() if a el...  15.2 us
    ppermute x5, starting transfers between devices, other_core(): return lax.ppermute(array, 'core', [(0, 1), (1, 0)])  11.6 us
    ppermute x10, waiting for transfers between devices, on_cores(): return lax.ppermute(array, ('zl', 'core', 'zh'), pairs)  6.23 us
  transfers between devices with their start and end apart: 36, of which 20 were waited for; matrix products, arithmetic and copies ran while one was open for 0% of the time, Pallas kernels for 9%

profile of v5, /device:TPU:1, one launch (start us, length us, event | category | flops | bytes accessed | tf_op | source)
XLA Modules:
  0.0 114.2 jit_solution(6139544684590679117)
XLA Ops:
  0.6 3.3 %collective-permute-start.2 = (bf16[576,2304]{1,0:T(8,128)(2,1)}, bf16[576,2304]{1,0:T(8,128)(2,1)S(1)}, u32[]{:S(2)}, u32[]{:S(2)}) collective-permute-start(bf16[576,2304]{1,0:T(8,128)(2,1)} %up_own.1), channel_id=1, source_target_pairs={{0,32},{32,0},{1,33},{33,1},{2,34},{34,2},{3,35},{35,3},{4,36},{36... | collective-permute-start | bytes 7962632 | tf_op jit(solution)/shard_map/ppermute | solution.py:40
  5.1 5.7 %collective-permute-start = (bf16[16,2304]{1,0:T(8,128)(2,1)S(1)}, bf16[16,2304]{1,0:T(8,128)(2,1)S(1)}, u32[]{:S(2)}, u32[]{:S(2)}) collective-permute-start(bf16[16,2304]{1,0:T(8,128)(2,1)S(1)} %dequant.1), channel_id=1, source_target_pairs={{0,0},{32,225},{64,64},{96,32},{128,128},{160,96},{192,192},{224,1... | collective-permute-start | bytes 221192 | tf_op jit(solution)/shard_map/ppermute | solution.py:24
  12.2 2.4 %collective-permute-done.1.oth = bf16[16,2304]{1,0:T(8,128)(2,1)S(1)} collective-permute-done((bf16[16,2304]{1,0:T(8,128)(2,1)S(1)}, bf16[16,2304]{1,0:T(8,128)(2,1)S(1)}, u32[]{:S(2)}, u32[]{:S(2)}) %collective-permute-start.1) | collective-permute-done | bytes 73760 | tf_op jit(solution)/shard_map/ppermute | solution.py:24
  15.9 1.8 %collective-permute-start.4 = (bf16[16,2304]{1,0:T(8,128)(2,1)S(1)}, bf16[16,2304]{1,0:T(8,128)(2,1)S(1)}, u32[]{:S(2)}, u32[]{:S(2)}) collective-permute-start(bf16[16,2304]{1,0:T(8,128)(2,1)S(1)} %get-tuple-element.37.x0), channel_id=1, source_target_pairs={{0,6},{2,4},{4,2},{6,0},{1,7},{3,5},{5,3},{7,1},{8,14},{10,12},{12... | collective-permute-start | bytes 221192 | tf_op jit(solution)/shard_map/ppermute | solution.py:32
  18.4 1.9 %collective-permute-start.6 = (bf16[16,2304]{1,0:T(8,128)(2,1)S(1)}, bf16[16,2304]{1,0:T(8,128)(2,1)S(1)}, u32[]{:S(2)}, u32[]{:S(2)}) collective-permute-start(bf16[16,2304]{1,0:T(8,128)(2,1)S(1)} %get-tuple-element.38.g0), channel_id=1, source_target_pairs={{0,64},{32,225},{64,128},{96,32},{128,192},{160,96},{192,1},{224,1... | collective-permute-start | bytes 221192 | tf_op jit(solution)/shard_map/ppermute | solution.py:24
  21.3 1.9 %collective-permute-done.5.x3 = bf16[16,2304]{1,0:T(8,128)(2,1)S(1)} collective-permute-done((bf16[16,2304]{1,0:T(8,128)(2,1)S(1)}, bf16[16,2304]{1,0:T(8,128)(2,1)S(1)}, u32[]{:S(2)}, u32[]{:S(2)}) %collective-permute-start.5) | collective-permute-done | bytes 73760 | tf_op jit(solution)/shard_map/ppermute | solution.py:32
  25.6 1.8 %collective-permute-start.11 = (bf16[2,16,2304]{2,1,0:T(8,128)(2,1)S(1)}, bf16[2,16,2304]{2,1,0:T(8,128)(2,1)S(1)}, u32[]{:S(2)}, u32[]{:S(2)}) collective-permute-start(bf16[2,16,2304]{2,1,0:T(8,128)(2,1)S(1)} %get-tuple-element.40.refs_0_), channel_id=1, source_target_pairs={{0,6},{2,4},{4,2},{6,0},{1,7},{3,5},{5,3},{7,1},{8,14},{10,12},{12... | collective-permute-start | bytes 442376 | tf_op jit(solution)/shard_map/ppermute | solution.py:32
  27.5 3.0 %collective-permute-done.10._.refs_1_ = bf16[2,16,2304]{2,1,0:T(8,128)(2,1)S(1)} collective-permute-done((bf16[2,16,2304]{2,1,0:T(8,128)(2,1)S(1)}, bf16[2,16,2304]{2,1,0:T(8,128)(2,1)S(1)}, u32[]{:S(2)}, u32[]{:S(2)}) %collective-permute-start.10) | collective-permute-done | bytes 147488 | tf_op jit(solution)/shard_map/ppermute | solution.py:32
  30.5 2.0 %collective-permute-done.11.__.refs_2_ = bf16[2,16,2304]{2,1,0:T(8,128)(2,1)S(1)} collective-permute-done((bf16[2,16,2304]{2,1,0:T(8,128)(2,1)S(1)}, bf16[2,16,2304]{2,1,0:T(8,128)(2,1)S(1)}, u32[]{:S(2)}, u32[]{:S(2)}) %collective-permute-start.11) | collective-permute-done | bytes 147488 | tf_op jit(solution)/shard_map/ppermute | solution.py:32
  33.4 2.4 %collective-permute-start.12 = (bf16[2,4,16,2304]{3,2,1,0:T(8,128)(2,1)S(1)}, bf16[2,4,16,2304]{3,2,1,0:T(8,128)(2,1)S(1)}, u32[]{:S(2)}, u32[]{:S(2)}) collective-permute-start(bf16[2,4,16,2304]{3,2,1,0:T(8,128)(2,1)S(1)} %get-tuple-element.41.near), channel_id=1, source_target_pairs={{0,128},{32,161},{64,192},{96,225},{128,1},{160,32},{192,65},{224,... | collective-permute-start | bytes 1769480 | tf_op jit(solution)/shard_map/ppermute | solution.py:24
  35.8 2.3 %collective-permute-start.13 = (bf16[2,16,2304]{2,1,0:T(8,128)(2,1)S(1)}, bf16[2,16,2304]{2,1,0:T(8,128)(2,1)S(1)}, u32[]{:S(2)}, u32[]{:S(2)}) collective-permute-start(bf16[2,16,2304]{2,1,0:T(8,128)(2,1)S(1)} %get-tuple-element.40.refs_0_), channel_id=1, source_target_pairs={{0,4},{2,6},{4,0},{6,2},{1,5},{3,7},{5,1},{7,3},{8,12},{10,14},{12... | collective-permute-start | bytes 442376 | tf_op jit(solution)/shard_map/ppermute | solution.py:32
  39.1 2.3 %collective-permute-start.16 = (bf16[2,16,2304]{2,1,0:T(8,128)(2,1)S(1)}, bf16[2,16,2304]{2,1,0:T(8,128)(2,1)S(1)}, u32[]{:S(2)}, u32[]{:S(2)}) collective-permute-start(bf16[2,16,2304]{2,1,0:T(8,128)(2,1)S(1)} %get-tuple-element.43.refs_4_), channel_id=1, source_target_pairs={{0,4},{2,6},{4,0},{6,2},{1,5},{3,7},{5,1},{7,3},{8,12},{10,14},{12... | collective-permute-start | bytes 442376 | tf_op jit(solution)/shard_map/ppermute | solution.py:32
  41.4 2.6 %join.1 = (bf16[1152,2304]{1,0:T(8,128)(2,1)S(1)}, bf16[1152,2304]{1,0:T(8,128)(2,1)S(1)}) custom-call(bf16[576,2304]{1,0:T(8,128)(2,1)} %up_own.1, bf16[576,2304]{1,0:T(8,128)(2,1)S(1)} %collective-permute-done.2._.up_oth, bf16[576,2304]{1,0:T(8,128)(2,1)} %down_own.1, bf16[576,2304]{1,0:T(8,128)(2,1)S(1)} %collective-permute-done.7._.down_oth, ...), custom_call_target="tpu_custom_call" | custom-call | flops 1 | bytes 1 | tf_op jit(solution)/shard_map/join/pallas_call | solution.py:62
  44.1 1.9 %collective-permute-done.14.refs_5_ = bf16[2,16,2304]{2,1,0:T(8,128)(2,1)S(1)} collective-permute-done((bf16[2,16,2304]{2,1,0:T(8,128)(2,1)S(1)}, bf16[2,16,2304]{2,1,0:T(8,128)(2,1)S(1)}, u32[]{:S(2)}, u32[]{:S(2)}) %collective-permute-start.14) | collective-permute-done | bytes 147488 | tf_op jit(solution)/shard_map/ppermute | solution.py:32
  48.2 2.1 %grads.1 = (f32[64,1152]{1,0:T(8,128)S(1)}, bf16[64,1152]{1,0:T(8,128)(2,1)S(1)}, bf16[64,1152]{1,0:T(8,128)(2,1)S(1)}, bf16[64,1152]{1,0:T(8,128)(2,1)S(1)}, bf16[4,4,16,2304]{3,2,1,0:T(8,128)(2,1)S(1)}) custom-call(bf16[2,16,2304]{2,1,0:T(8,128)(2,1)S(1)} %get-tuple-element.40.refs_0_, bf16[2,16,2304]{2,1,0:T(8,128)(2,1)S(1)} %collective-permute-done.10._.refs_1_, ...), custom_call_target="tpu_custom_call" | custom-call | flops 1 | bytes 1 | tf_op jit(solution)/shard_map/grads/pallas_call | solution.py:62
  50.3 2.2 %inputs.1 = (f32[2,64,1152]{2,1,0:T(8,128)S(1)}, bf16[2,64,1152]{2,1,0:T(8,128)(2,1)S(1)}, bf16[2,64,1152]{2,1,0:T(8,128)(2,1)S(1)}, bf16[2,64,1152]{2,1,0:T(8,128)(2,1)S(1)}, bf16[2,4,4,16,2304]{4,3,2,1,0:T(8,128)(2,1)S(1)}) custom-call(bf16[2,4,16,2304]{3,2,1,0:T(8,128)(2,1)S(1)} %get-tuple-element.41.near, ...), custom_call_target="tpu_custom_call" | custom-call | flops 1 | bytes 1 | tf_op jit(solution)/shard_map/inputs/pallas_call | solution.py:62
  53.9 1.9 %collective-permute-start.18 = (bf16[2,64,1152]{2,1,0:T(8,128)(2,1)S(1)}, bf16[2,64,1152]{2,1,0:T(8,128)(2,1)S(1)}, u32[]{:S(2)}, u32[]{:S(2)}) collective-permute-start(bf16[2,64,1152]{2,1,0:T(8,128)(2,1)S(1)} %get-tuple-element.52), channel_id=1, source_target_pairs={{0,24},{8,16},{16,8},{24,0},{1,25},{9,17},{17,9},{25,1},{2,26},{10... | collective-permute-start | bytes 884744 | tf_op jit(solution)/shard_map/ppermute | solution.py:32
  58.2 5.1 %collective-permute-done.18.r2 = bf16[2,64,1152]{2,1,0:T(8,128)(2,1)S(1)} collective-permute-done((bf16[2,64,1152]{2,1,0:T(8,128)(2,1)S(1)}, bf16[2,64,1152]{2,1,0:T(8,128)(2,1)S(1)}, u32[]{:S(2)}, u32[]{:S(2)}) %collective-permute-start.18) | collective-permute-done | bytes 294944 | tf_op jit(solution)/shard_map/ppermute | solution.py:32
  63.3 2.0 %collective-permute-done.19.r3 = bf16[2,64,1152]{2,1,0:T(8,128)(2,1)S(1)} collective-permute-done((bf16[2,64,1152]{2,1,0:T(8,128)(2,1)S(1)}, bf16[2,64,1152]{2,1,0:T(8,128)(2,1)S(1)}, u32[]{:S(2)}, u32[]{:S(2)}) %collective-permute-start.19) | collective-permute-done | bytes 294944 | tf_op jit(solution)/shard_map/ppermute | solution.py:32
  65.6 1.6 %collective-permute-start.21 = (bf16[64,1152]{1,0:T(8,128)(2,1)S(1)}, bf16[64,1152]{1,0:T(8,128)(2,1)S(1)}, u32[]{:S(2)}, u32[]{:S(2)}) collective-permute-start(bf16[64,1152]{1,0:T(8,128)(2,1)S(1)} %get-tuple-element.54.p0.refs_4_), channel_id=1, source_target_pairs={{0,24},{8,16},{16,8},{24,0},{1,25},{9,17},{17,9},{25,1},{2,26},{10... | collective-permute-start | bytes 442376 | tf_op jit(solution)/shard_map/ppermute | solution.py:32
  67.2 1.6 %collective-permute-start.22 = (bf16[64,1152]{1,0:T(8,128)(2,1)S(1)}, bf16[64,1152]{1,0:T(8,128)(2,1)S(1)}, u32[]{:S(2)}, u32[]{:S(2)}) collective-permute-start(bf16[64,1152]{1,0:T(8,128)(2,1)S(1)} %get-tuple-element.54.p0.refs_4_), channel_id=1, source_target_pairs={{0,16},{8,24},{16,0},{24,8},{1,17},{9,25},{17,1},{25,9},{2,18},{10... | collective-permute-start | bytes 442376 | tf_op jit(solution)/shard_map/ppermute | solution.py:32
  69.9 3.6 %collective-permute-done.21.p2.refs_6_ = bf16[64,1152]{1,0:T(8,128)(2,1)S(1)} collective-permute-done((bf16[64,1152]{1,0:T(8,128)(2,1)S(1)}, bf16[64,1152]{1,0:T(8,128)(2,1)S(1)}, u32[]{:S(2)}, u32[]{:S(2)}) %collective-permute-start.21) | collective-permute-done | bytes 147488 | tf_op jit(solution)/shard_map/ppermute | solution.py:32
  73.5 1.7 %back.1 = (bf16[64,2304]{1,0:T(8,128)(2,1)S(1)}, bf16[64,2304]{1,0:T(8,128)(2,1)S(1)}, bf16[64,2304]{1,0:T(8,128)(2,1)S(1)}, bf16[64,2304]{1,0:T(8,128)(2,1)S(1)}) custom-call(bf16[64,1152]{1,0:T(8,128)(2,1)S(1)} %get-tuple-element.54.p0.refs_4_, bf16[64,1152]{1,0:T(8,128)(2,1)S(1)} %collective-permute-done.20.p1.refs_5_, ...), custom_call_target="tpu_custom_call" | custom-call | flops 1 | bytes 1 | tf_op jit(solution)/shard_map/back/pallas_call | solution.py:62
  75.2 1.9 %collective-permute-start.23 = (bf16[64,2304]{1,0:T(8,128)(2,1)S(1)}, bf16[64,2304]{1,0:T(8,128)(2,1)S(1)}, u32[]{:S(2)}, u32[]{:S(2)}) collective-permute-start(bf16[64,2304]{1,0:T(8,128)(2,1)S(1)} %get-tuple-element.56), channel_id=1, source_target_pairs={{0,2},{2,0},{4,6},{6,4},{1,3},{3,1},{5,7},{7,5},{8,10},{10,8},{12,... | collective-permute-start | bytes 884744 | tf_op jit(solution)/shard_map/ppermute | solution.py:32
  77.1 3.8 %collective-permute-start.24 = (bf16[64,2304]{1,0:T(8,128)(2,1)S(1)}, bf16[64,2304]{1,0:T(8,128)(2,1)S(1)}, u32[]{:S(2)}, u32[]{:S(2)}) collective-permute-start(bf16[64,2304]{1,0:T(8,128)(2,1)S(1)} %get-tuple-element.57), channel_id=1, source_target_pairs={{0,6},{2,4},{4,2},{6,0},{1,7},{3,5},{5,3},{7,1},{8,14},{10,12},{12... | collective-permute-start | bytes 884744 | tf_op jit(solution)/shard_map/ppermute | solution.py:32
  81.5 3.3 %collective-permute-start.31 = (bf16[64,1152]{1,0:T(8,128)(2,1)S(1)}, bf16[64,1152]{1,0:T(8,128)(2,1)S(1)}, u32[]{:S(2)}, u32[]{:S(2)}) collective-permute-start(bf16[64,1152]{1,0:T(8,128)(2,1)S(1)} %get-tuple-element.63.refs_0_), channel_id=1, source_target_pairs={{0,24},{8,16},{16,8},{24,0},{1,25},{9,17},{17,9},{25,1},{2,26},{10... | collective-permute-start | bytes 442376 | tf_op jit(solution)/shard_map/ppermute | solution.py:32
  84.8 3.6 %collective-permute-done.24.refs_2_ = bf16[64,2304]{1,0:T(8,128)(2,1)S(1)} collective-permute-done((bf16[64,2304]{1,0:T(8,128)(2,1)S(1)}, bf16[64,2304]{1,0:T(8,128)(2,1)S(1)}, u32[]{:S(2)}, u32[]{:S(2)}) %collective-permute-start.24) | collective-permute-done | bytes 294944 | tf_op jit(solution)/shard_map/ppermute | solution.py:32
  91.0 8.0 %collective-permute-start.34 = (bf16[2,4,4,16,2304]{4,3,2,1,0:T(8,128)(2,1)S(1)}, bf16[2,4,4,16,2304]{4,3,2,1,0:T(8,128)(2,1)S(1)}, u32[]{:S(2)}, u32[]{:S(2)}) collective-permute-start(bf16[2,4,4,16,2304]{4,3,2,1,0:T(8,128)(2,1)S(1)} %copied.1), channel_id=1, source_target_pairs={{0,32},{32,0},{1,33},{33,1},{2,34},{34,2},{3,35},{35,3},{4,36},{36... | collective-permute-start | bytes 7077896 | tf_op jit(solution)/shard_map/ppermute | solution.py:40
  99.1 1.9 %collective-permute-start.26 = (bf16[16,2304]{1,0:T(8,128)(2,1)S(1)}, bf16[16,2304]{1,0:T(8,128)(2,1)S(1)}, u32[]{:S(2)}, u32[]{:S(2)}) collective-permute-start(bf16[16,2304]{1,0:T(8,128)(2,1)S(1)} %get-tuple-element.59.refs_8_), channel_id=1, source_target_pairs={{0,0},{32,96},{64,64},{96,160},{128,128},{160,224},{192,192},{224,... | collective-permute-start | bytes 221192 | tf_op jit(solution)/shard_map/ppermute | solution.py:24
  101.0 2.2 %collective-permute-start.27 = (bf16[16,2304]{1,0:T(8,128)(2,1)S(1)}, bf16[16,2304]{1,0:T(8,128)(2,1)S(1)}, u32[]{:S(2)}, u32[]{:S(2)}) collective-permute-start(bf16[16,2304]{1,0:T(8,128)(2,1)S(1)} %get-tuple-element.60), channel_id=1, source_target_pairs={{0,65},{32,33},{64,129},{96,97},{128,193},{160,161},{192,0},{224,2... | collective-permute-start | bytes 221192 | tf_op jit(solution)/shard_map/ppermute | solution.py:24
  103.2 3.5 %collective-permute-start.28 = (bf16[16,2304]{1,0:T(8,128)(2,1)S(1)}, bf16[16,2304]{1,0:T(8,128)(2,1)S(1)}, u32[]{:S(2)}, u32[]{:S(2)}) collective-permute-start(bf16[16,2304]{1,0:T(8,128)(2,1)S(1)} %get-tuple-element.61), channel_id=1, source_target_pairs={{0,129},{32,224},{64,193},{96,33},{128,0},{160,97},{192,64},{224,1... | collective-permute-start | bytes 221192 | tf_op jit(solution)/shard_map/ppermute | solution.py:24
  106.7 3.9 %weight_grads.1 = (bf16[576,2304]{1,0:T(8,128)(2,1)}, bf16[576,2304]{1,0:T(8,128)(2,1)}) custom-call(bf16[2,576,256]{2,1,0:T(8,128)(2,1)S(1)} %get-tuple-element.64._.keep, bf16[2,576,256]{2,1,0:T(8,128)(2,1)S(1)} %collective-permute-done.33.came, bf16[2,4,4,16,2304]{4,3,2,1,0:T(8,128)(2,1)S(1)} %get-tuple-element.66.src.own, ...), custom_call_target="tpu_custom_call" | custom-call | flops 1 | bytes 1 | tf_op jit(solution)/shard_map/weight_grads/pallas_call | solution.py:62
  (55 shorter events, 23.7 us)
Async XLA Ops:
  0.6 14.0 %collective-permute-start.2 = (bf16[576,2304]{1,0:T(8,128)(2,1)}, bf16[576,2304]{1,0:T(8,128)(2,1)S(1)}, u32[]{:S(2)}, u32[]{:S(2)}) collective-permute-start(bf16[576,2304]{1,0:T(8,128)(2,1)} %up_own.1), channel_id=1, source_target_pairs={{0,32},{32,0},{1,33},{33,1},{2,34},{34,2},{3,35},{35,3},{4,36},{36... | collective-permute-start | bytes 7962632 | tf_op jit(solution)/shard_map/ppermute | solution.py:40
  4.0 16.4 %collective-permute-start.7 = (bf16[576,2304]{1,0:T(8,128)(2,1)}, bf16[576,2304]{1,0:T(8,128)(2,1)S(1)}, u32[]{:S(2)}, u32[]{:S(2)}) collective-permute-start(bf16[576,2304]{1,0:T(8,128)(2,1)} %down_own.1), channel_id=1, source_target_pairs={{0,32},{32,0},{1,33},{33,1},{2,34},{34,2},{3,35},{35,3},{4,36},{36... | collective-permute-start | bytes 7962632 | tf_op jit(solution)/shard_map/ppermute | solution.py:40
  5.1 7.1 %collective-permute-start = (bf16[16,2304]{1,0:T(8,128)(2,1)S(1)}, bf16[16,2304]{1,0:T(8,128)(2,1)S(1)}, u32[]{:S(2)}, u32[]{:S(2)}) collective-permute-start(bf16[16,2304]{1,0:T(8,128)(2,1)S(1)} %dequant.1), channel_id=1, source_target_pairs={{0,0},{32,225},{64,64},{96,32},{128,128},{160,96},{192,192},{224,1... | collective-permute-start | bytes 221192 | tf_op jit(solution)/shard_map/ppermute | solution.py:24
  14.6 5.7 %collective-permute-start.3 = (bf16[16,2304]{1,0:T(8,128)(2,1)S(1)}, bf16[16,2304]{1,0:T(8,128)(2,1)S(1)}, u32[]{:S(2)}, u32[]{:S(2)}) collective-permute-start(bf16[16,2304]{1,0:T(8,128)(2,1)S(1)} %get-tuple-element.37.x0), channel_id=1, source_target_pairs={{0,2},{2,0},{4,6},{6,4},{1,3},{3,1},{5,7},{7,5},{8,10},{10,8},{12,... | collective-permute-start | bytes 221192 | tf_op jit(solution)/shard_map/ppermute | solution.py:32
  15.9 5.4 %collective-permute-start.4 = (bf16[16,2304]{1,0:T(8,128)(2,1)S(1)}, bf16[16,2304]{1,0:T(8,128)(2,1)S(1)}, u32[]{:S(2)}, u32[]{:S(2)}) collective-permute-start(bf16[16,2304]{1,0:T(8,128)(2,1)S(1)} %get-tuple-element.37.x0), channel_id=1, source_target_pairs={{0,6},{2,4},{4,2},{6,0},{1,7},{3,5},{5,3},{7,1},{8,14},{10,12},{12... | collective-permute-start | bytes 221192 | tf_op jit(solution)/shard_map/ppermute | solution.py:32
  17.7 5.5 %collective-permute-start.5 = (bf16[16,2304]{1,0:T(8,128)(2,1)S(1)}, bf16[16,2304]{1,0:T(8,128)(2,1)S(1)}, u32[]{:S(2)}, u32[]{:S(2)}) collective-permute-start(bf16[16,2304]{1,0:T(8,128)(2,1)S(1)} %get-tuple-element.37.x0), channel_id=1, source_target_pairs={{0,4},{2,6},{4,0},{6,2},{1,5},{3,7},{5,1},{7,3},{8,12},{10,14},{12... | collective-permute-start | bytes 221192 | tf_op jit(solution)/shard_map/ppermute | solution.py:32
  23.3 10.1 %collective-permute-start.8 = (bf16[4,16,2304]{2,1,0:T(8,128)(2,1)S(1)}, bf16[4,16,2304]{2,1,0:T(8,128)(2,1)S(1)}, u32[]{:S(2)}, u32[]{:S(2)}) collective-permute-start(bf16[4,16,2304]{2,1,0:T(8,128)(2,1)S(1)} %get-tuple-element.39.row._), channel_id=1, source_target_pairs={{0,64},{32,225},{64,128},{96,32},{128,192},{160,96},{192,1},{224,1... | collective-permute-start | bytes 884744 | tf_op jit(solution)/shard_map/ppermute | solution.py:24
  24.8 5.6 %collective-permute-start.10 = (bf16[2,16,2304]{2,1,0:T(8,128)(2,1)S(1)}, bf16[2,16,2304]{2,1,0:T(8,128)(2,1)S(1)}, u32[]{:S(2)}, u32[]{:S(2)}) collective-permute-start(bf16[2,16,2304]{2,1,0:T(8,128)(2,1)S(1)} %get-tuple-element.40.refs_0_), channel_id=1, source_target_pairs={{0,2},{2,0},{4,6},{6,4},{1,3},{3,1},{5,7},{7,5},{8,10},{10,8},{12,... | collective-permute-start | bytes 442376 | tf_op jit(solution)/shard_map/ppermute | solution.py:32
  25.6 6.9 %collective-permute-start.11 = (bf16[2,16,2304]{2,1,0:T(8,128)(2,1)S(1)}, bf16[2,16,2304]{2,1,0:T(8,128)(2,1)S(1)}, u32[]{:S(2)}, u32[]{:S(2)}) collective-permute-start(bf16[2,16,2304]{2,1,0:T(8,128)(2,1)S(1)} %get-tuple-element.40.refs_0_), channel_id=1, source_target_pairs={{0,6},{2,4},{4,2},{6,0},{1,7},{3,5},{5,3},{7,1},{8,14},{10,12},{12... | collective-permute-start | bytes 442376 | tf_op jit(solution)/shard_map/ppermute | solution.py:32
  27.5 5.9 %collective-permute-start.9 = (bf16[2,16,2304]{2,1,0:T(8,128)(2,1)S(1)}, bf16[2,16,2304]{2,1,0:T(8,128)(2,1)S(1)}, u32[]{:S(2)}, u32[]{:S(2)}) collective-permute-start(bf16[2,16,2304]{2,1,0:T(8,128)(2,1)S(1)} %get-tuple-element.40.refs_0_), channel_id=1, source_target_pairs={{0,128},{32,161},{64,192},{96,225},{128,1},{160,32},{192,65},{224,... | collective-permute-start | bytes 442376 | tf_op jit(solution)/shard_map/ppermute | solution.py:24
  33.4 16.9 %collective-permute-start.12 = (bf16[2,4,16,2304]{3,2,1,0:T(8,128)(2,1)S(1)}, bf16[2,4,16,2304]{3,2,1,0:T(8,128)(2,1)S(1)}, u32[]{:S(2)}, u32[]{:S(2)}) collective-permute-start(bf16[2,4,16,2304]{3,2,1,0:T(8,128)(2,1)S(1)} %get-tuple-element.41.near), channel_id=1, source_target_pairs={{0,128},{32,161},{64,192},{96,225},{128,1},{160,32},{192,65},{224,... | collective-permute-start | bytes 1769480 | tf_op jit(solution)/shard_map/ppermute | solution.py:24
  35.8 8.2 %collective-permute-start.13 = (bf16[2,16,2304]{2,1,0:T(8,128)(2,1)S(1)}, bf16[2,16,2304]{2,1,0:T(8,128)(2,1)S(1)}, u32[]{:S(2)}, u32[]{:S(2)}) collective-permute-start(bf16[2,16,2304]{2,1,0:T(8,128)(2,1)S(1)} %get-tuple-element.40.refs_0_), channel_id=1, source_target_pairs={{0,4},{2,6},{4,0},{6,2},{1,5},{3,7},{5,1},{7,3},{8,12},{10,14},{12... | collective-permute-start | bytes 442376 | tf_op jit(solution)/shard_map/ppermute | solution.py:32
  38.2 7.8 %collective-permute-start.14 = (bf16[2,16,2304]{2,1,0:T(8,128)(2,1)S(1)}, bf16[2,16,2304]{2,1,0:T(8,128)(2,1)S(1)}, u32[]{:S(2)}, u32[]{:S(2)}) collective-permute-start(bf16[2,16,2304]{2,1,0:T(8,128)(2,1)S(1)} %get-tuple-element.43.refs_4_), channel_id=1, source_target_pairs={{0,2},{2,0},{4,6},{6,4},{1,3},{3,1},{5,7},{7,5},{8,10},{10,8},{12,... | collective-permute-start | bytes 442376 | tf_op jit(solution)/shard_map/ppermute | solution.py:32
  38.5 9.0 %collective-permute-start.15 = (bf16[2,16,2304]{2,1,0:T(8,128)(2,1)S(1)}, bf16[2,16,2304]{2,1,0:T(8,128)(2,1)S(1)}, u32[]{:S(2)}, u32[]{:S(2)}) collective-permute-start(bf16[2,16,2304]{2,1,0:T(8,128)(2,1)S(1)} %get-tuple-element.43.refs_4_), channel_id=1, source_target_pairs={{0,6},{2,4},{4,2},{6,0},{1,7},{3,5},{5,3},{7,1},{8,14},{10,12},{12... | collective-permute-start | bytes 442376 | tf_op jit(solution)/shard_map/ppermute | solution.py:32
  39.1 9.1 %collective-permute-start.16 = (bf16[2,16,2304]{2,1,0:T(8,128)(2,1)S(1)}, bf16[2,16,2304]{2,1,0:T(8,128)(2,1)S(1)}, u32[]{:S(2)}, u32[]{:S(2)}) collective-permute-start(bf16[2,16,2304]{2,1,0:T(8,128)(2,1)S(1)} %get-tuple-element.43.refs_4_), channel_id=1, source_target_pairs={{0,4},{2,6},{4,0},{6,2},{1,5},{3,7},{5,1},{7,3},{8,12},{10,14},{12... | collective-permute-start | bytes 442376 | tf_op jit(solution)/shard_map/ppermute | solution.py:32
  52.5 5.7 %collective-permute-start.17 = (bf16[2,64,1152]{2,1,0:T(8,128)(2,1)S(1)}, bf16[2,64,1152]{2,1,0:T(8,128)(2,1)S(1)}, u32[]{:S(2)}, u32[]{:S(2)}) collective-permute-start(bf16[2,64,1152]{2,1,0:T(8,128)(2,1)S(1)} %get-tuple-element.51), channel_id=1, source_target_pairs={{0,8},{8,0},{16,24},{24,16},{1,9},{9,1},{17,25},{25,17},{2,10},{10... | collective-permute-start | bytes 884744 | tf_op jit(solution)/shard_map/ppermute | solution.py:32
  53.9 9.4 %collective-permute-start.18 = (bf16[2,64,1152]{2,1,0:T(8,128)(2,1)S(1)}, bf16[2,64,1152]{2,1,0:T(8,128)(2,1)S(1)}, u32[]{:S(2)}, u32[]{:S(2)}) collective-permute-start(bf16[2,64,1152]{2,1,0:T(8,128)(2,1)S(1)} %get-tuple-element.52), channel_id=1, source_target_pairs={{0,24},{8,16},{16,8},{24,0},{1,25},{9,17},{17,9},{25,1},{2,26},{10... | collective-permute-start | bytes 884744 | tf_op jit(solution)/shard_map/ppermute | solution.py:32
  55.8 9.5 %collective-permute-start.19 = (bf16[2,64,1152]{2,1,0:T(8,128)(2,1)S(1)}, bf16[2,64,1152]{2,1,0:T(8,128)(2,1)S(1)}, u32[]{:S(2)}, u32[]{:S(2)}) collective-permute-start(bf16[2,64,1152]{2,1,0:T(8,128)(2,1)S(1)} %get-tuple-element.53), channel_id=1, source_target_pairs={{0,16},{8,24},{16,0},{24,8},{1,17},{9,25},{17,1},{25,9},{2,18},{10... | collective-permute-start | bytes 884744 | tf_op jit(solution)/shard_map/ppermute | solution.py:32
  65.6 7.9 %collective-permute-start.21 = (bf16[64,1152]{1,0:T(8,128)(2,1)S(1)}, bf16[64,1152]{1,0:T(8,128)(2,1)S(1)}, u32[]{:S(2)}, u32[]{:S(2)}) collective-permute-start(bf16[64,1152]{1,0:T(8,128)(2,1)S(1)} %get-tuple-element.54.p0.refs_4_), channel_id=1, source_target_pairs={{0,24},{8,16},{16,8},{24,0},{1,25},{9,17},{17,9},{25,1},{2,26},{10... | collective-permute-start | bytes 442376 | tf_op jit(solution)/shard_map/ppermute | solution.py:32
  67.2 6.3 %collective-permute-start.22 = (bf16[64,1152]{1,0:T(8,128)(2,1)S(1)}, bf16[64,1152]{1,0:T(8,128)(2,1)S(1)}, u32[]{:S(2)}, u32[]{:S(2)}) collective-permute-start(bf16[64,1152]{1,0:T(8,128)(2,1)S(1)} %get-tuple-element.54.p0.refs_4_), channel_id=1, source_target_pairs={{0,16},{8,24},{16,0},{24,8},{1,17},{9,25},{17,1},{25,9},{2,18},{10... | collective-permute-start | bytes 442376 | tf_op jit(solution)/shard_map/ppermute | solution.py:32
  75.2 9.6 %collective-permute-start.23 = (bf16[64,2304]{1,0:T(8,128)(2,1)S(1)}, bf16[64,2304]{1,0:T(8,128)(2,1)S(1)}, u32[]{:S(2)}, u32[]{:S(2)}) collective-permute-start(bf16[64,2304]{1,0:T(8,128)(2,1)S(1)} %get-tuple-element.56), channel_id=1, source_target_pairs={{0,2},{2,0},{4,6},{6,4},{1,3},{3,1},{5,7},{7,5},{8,10},{10,8},{12,... | collective-permute-start | bytes 884744 | tf_op jit(solution)/shard_map/ppermute | solution.py:32
  77.1 11.3 %collective-permute-start.24 = (bf16[64,2304]{1,0:T(8,128)(2,1)S(1)}, bf16[64,2304]{1,0:T(8,128)(2,1)S(1)}, u32[]{:S(2)}, u32[]{:S(2)}) collective-permute-start(bf16[64,2304]{1,0:T(8,128)(2,1)S(1)} %get-tuple-element.57), channel_id=1, source_target_pairs={{0,6},{2,4},{4,2},{6,0},{1,7},{3,5},{5,3},{7,1},{8,14},{10,12},{12... | collective-permute-start | bytes 884744 | tf_op jit(solution)/shard_map/ppermute | solution.py:32
  81.0 8.2 %collective-permute-start.25 = (bf16[64,2304]{1,0:T(8,128)(2,1)S(1)}, bf16[64,2304]{1,0:T(8,128)(2,1)S(1)}, u32[]{:S(2)}, u32[]{:S(2)}) collective-permute-start(bf16[64,2304]{1,0:T(8,128)(2,1)S(1)} %get-tuple-element.58), channel_id=1, source_target_pairs={{0,4},{2,6},{4,0},{6,2},{1,5},{3,7},{5,1},{7,3},{8,12},{10,14},{12... | collective-permute-start | bytes 884744 | tf_op jit(solution)/shard_map/ppermute | solution.py:32
  81.2 8.1 %collective-permute-start.30 = (bf16[64,1152]{1,0:T(8,128)(2,1)S(1)}, bf16[64,1152]{1,0:T(8,128)(2,1)S(1)}, u32[]{:S(2)}, u32[]{:S(2)}) collective-permute-start(bf16[64,1152]{1,0:T(8,128)(2,1)S(1)} %get-tuple-element.63.refs_0_), channel_id=1, source_target_pairs={{0,8},{8,0},{16,24},{24,16},{1,9},{9,1},{17,25},{25,17},{2,10},{10... | collective-permute-start | bytes 442376 | tf_op jit(solution)/shard_map/ppermute | solution.py:32
  81.5 7.8 %collective-permute-start.31 = (bf16[64,1152]{1,0:T(8,128)(2,1)S(1)}, bf16[64,1152]{1,0:T(8,128)(2,1)S(1)}, u32[]{:S(2)}, u32[]{:S(2)}) collective-permute-start(bf16[64,1152]{1,0:T(8,128)(2,1)S(1)} %get-tuple-element.63.refs_0_), channel_id=1, source_target_pairs={{0,24},{8,16},{16,8},{24,0},{1,25},{9,17},{17,9},{25,1},{2,26},{10... | collective-permute-start | bytes 442376 | tf_op jit(solution)/shard_map/ppermute | solution.py:32
  84.8 5.5 %collective-permute-start.32 = (bf16[64,1152]{1,0:T(8,128)(2,1)S(1)}, bf16[64,1152]{1,0:T(8,128)(2,1)S(1)}, u32[]{:S(2)}, u32[]{:S(2)}) collective-permute-start(bf16[64,1152]{1,0:T(8,128)(2,1)S(1)} %get-tuple-element.63.refs_0_), channel_id=1, source_target_pairs={{0,16},{8,24},{16,0},{24,8},{1,17},{9,25},{17,1},{25,9},{2,18},{10... | collective-permute-start | bytes 442376 | tf_op jit(solution)/shard_map/ppermute | solution.py:32
  91.0 15.7 %collective-permute-start.34 = (bf16[2,4,4,16,2304]{4,3,2,1,0:T(8,128)(2,1)S(1)}, bf16[2,4,4,16,2304]{4,3,2,1,0:T(8,128)(2,1)S(1)}, u32[]{:S(2)}, u32[]{:S(2)}) collective-permute-start(bf16[2,4,4,16,2304]{4,3,2,1,0:T(8,128)(2,1)S(1)} %copied.1), channel_id=1, source_target_pairs={{0,32},{32,0},{1,33},{33,1},{2,34},{34,2},{3,35},{35,3},{4,36},{36... | collective-permute-start | bytes 7077896 | tf_op jit(solution)/shard_map/ppermute | solution.py:40
  99.0 7.7 %collective-permute-start.33 = (bf16[2,576,256]{2,1,0:T(8,128)(2,1)S(1)}, bf16[2,576,256]{2,1,0:T(8,128)(2,1)S(1)}, u32[]{:S(2)}, u32[]{:S(2)}) collective-permute-start(bf16[2,576,256]{2,1,0:T(8,128)(2,1)S(1)} %get-tuple-element.65), channel_id=1, source_target_pairs={{0,32},{32,0},{1,33},{33,1},{2,34},{34,2},{3,35},{35,3},{4,36},{36... | collective-permute-start | bytes 1769480 | tf_op jit(solution)/shard_map/ppermute | solution.py:40
  99.1 11.6 %collective-permute-start.26 = (bf16[16,2304]{1,0:T(8,128)(2,1)S(1)}, bf16[16,2304]{1,0:T(8,128)(2,1)S(1)}, u32[]{:S(2)}, u32[]{:S(2)}) collective-permute-start(bf16[16,2304]{1,0:T(8,128)(2,1)S(1)} %get-tuple-element.59.refs_8_), channel_id=1, source_target_pairs={{0,0},{32,96},{64,64},{96,160},{128,128},{160,224},{192,192},{224,... | collective-permute-start | bytes 221192 | tf_op jit(solution)/shard_map/ppermute | solution.py:24
  101.0 9.7 %collective-permute-start.27 = (bf16[16,2304]{1,0:T(8,128)(2,1)S(1)}, bf16[16,2304]{1,0:T(8,128)(2,1)S(1)}, u32[]{:S(2)}, u32[]{:S(2)}) collective-permute-start(bf16[16,2304]{1,0:T(8,128)(2,1)S(1)} %get-tuple-element.60), channel_id=1, source_target_pairs={{0,65},{32,33},{64,129},{96,97},{128,193},{160,161},{192,0},{224,2... | collective-permute-start | bytes 221192 | tf_op jit(solution)/shard_map/ppermute | solution.py:24
  103.2 7.4 %collective-permute-start.28 = (bf16[16,2304]{1,0:T(8,128)(2,1)S(1)}, bf16[16,2304]{1,0:T(8,128)(2,1)S(1)}, u32[]{:S(2)}, u32[]{:S(2)}) collective-permute-start(bf16[16,2304]{1,0:T(8,128)(2,1)S(1)} %get-tuple-element.61), channel_id=1, source_target_pairs={{0,129},{32,224},{64,193},{96,33},{128,0},{160,97},{192,64},{224,1... | collective-permute-start | bytes 221192 | tf_op jit(solution)/shard_map/ppermute | solution.py:24
  106.7 5.5 %collective-permute-start.29 = (bf16[16,2304]{1,0:T(8,128)(2,1)S(1)}, bf16[16,2304]{1,0:T(8,128)(2,1)S(1)}, u32[]{:S(2)}, u32[]{:S(2)}) collective-permute-start(bf16[16,2304]{1,0:T(8,128)(2,1)S(1)} %get-tuple-element.62), channel_id=1, source_target_pairs={{0,193},{32,160},{64,0},{96,224},{128,64},{160,33},{192,128},{224,... | collective-permute-start | bytes 221192 | tf_op jit(solution)/shard_map/ppermute | solution.py:24
  (4 other events, 14.4 us)
